TPU v7x, 128 devices: a whole 4x4x4 slice. The times are simulated.
128 devices in a mesh: section: 4 (over x), seq: 32 (over z, y, core).
Axes of the slice: x: 4, y: 4, z: 4, core: 2. Of those that a mesh axis runs over, the one named last changes fastest.
Arguments:
- stream: float32 [4, 4096, 1024], P('section', 'seq'), may hold values from -40 to 40
- norm_gain: float32 [4, 1024], P('section'), may hold values from 0.1 to 1.9
- w_query: bfloat16 [4, 1024, 1024], P('section'), may hold values from -0.1875 to 0.1875
- w_key: bfloat16 [4, 1024, 1024], P('section'), may hold values from -0.1875 to 0.1875
- w_value: bfloat16 [4, 1024, 2048], P('section'), may hold values from -0.1875 to 0.1875
- w_beta: bfloat16 [4, 1024, 16], P('section'), may hold values from -0.1875 to 0.1875
- w_decay: bfloat16 [4, 1024, 16], P('section'), may hold values from -0.1875 to 0.1875
- a_log: float32 [4, 16], P('section'), may hold values from -13 to -3
- dt_bias: float32 [4, 16], P('section'), may hold values from -1.5 to 1.5
- beta_bias: float32 [4, 16], P('section'), may hold values from -7 to -1
- head_gain: float32 [4, 128], P('section'), may hold values from 0.1 to 1.9
- w_output: bfloat16 [4, 2048, 1024], P('section'), may hold values from -0.125 to 0.125
- carry_state: float32 [4, 16, 128, 128], P('section'), may hold values from -6 to 6
Outputs:
- next_stream: float32 [4, 4096, 1024], P('section', 'seq')
- boundary_states: float32 [4, 32, 16, 128, 128], P('section', 'seq')
All inputs are finite; a program needn't handle non-finite values.
Results may differ from a plain program's by a relative error of at most 0.0022.
Values sent between devices are 32-bit elements; how exact they have to be, the bound alone decides.
No kernel may reach another device: no remote copies, remote signals or barrier semaphores. Data moves between devices by JAX's collectives and lax.ppermute only.
A program may use at most 192 MiB of HBM per device.

v0:
```python
import jax
import jax.numpy as jnp
from jax import lax
from jax.sharding import PartitionSpec as P

KH = 8
VH = 16
DK = 128
DV = 128
BLOCK = 128


highest = lax.Precision.HIGHEST


def from_behind(value, axis, steps):
    count = lax.axis_size(axis)
    leading, last = (max(0, -steps), min(count, count - steps))
    return lax.ppermute(value, axis, [(source, source + steps) for source in range(leading, last)])


def passed_along(block, axis, distance):
    devices = range(lax.axis_size(axis))
    route = [((i - distance) % len(devices), i) for i in devices]
    return lax.ppermute(block, axis, route)


def normalize_rows(values, scale_row, epsilon):
    mean_square = jnp.mean(values * values, axis=-1, keepdims=True)
    return values * lax.rsqrt(mean_square + epsilon) * scale_row


def unit_heads(values, head_count):
    shaped = values.reshape(values.shape[0], head_count, -1)
    return shaped * lax.rsqrt(jnp.sum(shaped * shaped, axis=-1, keepdims=True) + 1e-06)


def project(
    stream_rows,
    norm_row,
    query_weight,
    key_weight,
    value_weight,
    beta_weight,
    decay_weight,
    log_rate,
    decay_bias,
    update_bias,
):
    normed = normalize_rows(stream_rows, norm_row, 1e-06).astype(jnp.bfloat16)
    query_heads = unit_heads(
        jax.nn.silu(jnp.dot(normed, query_weight, preferred_element_type=jnp.float32)), KH
    ) * DK ** (-0.5)
    key_heads = unit_heads(
        jax.nn.silu(jnp.dot(normed, key_weight, preferred_element_type=jnp.float32)), KH
    )
    query_heads = jnp.repeat(query_heads, VH // KH, axis=1)
    key_heads = jnp.repeat(key_heads, VH // KH, axis=1)
    value_heads = jax.nn.silu(
        jnp.dot(normed, value_weight, preferred_element_type=jnp.float32)
    ).reshape(-1, VH, DV)
    strength = jax.nn.sigmoid(
        jnp.dot(normed, beta_weight, preferred_element_type=jnp.float32) + update_bias
    )
    log_decay = -jnp.exp(log_rate) * jax.nn.softplus(
        jnp.dot(normed, decay_weight, preferred_element_type=jnp.float32) + decay_bias
    )
    return (query_heads, key_heads, value_heads, strength, log_decay)


def to_blocks(values):
    blocks = values.shape[0] // BLOCK
    if values.ndim == 3:
        return values.reshape(blocks, BLOCK, values.shape[1], values.shape[2]).transpose(2, 0, 1, 3)
    return values.reshape(blocks, BLOCK, values.shape[1]).transpose(2, 0, 1)


def block_parts(query_heads, key_heads, value_heads, strength, log_decay):
    running = jnp.cumsum(log_decay, axis=-1)
    spread = running[..., :, None] - running[..., None, :]
    strict = jnp.tri(BLOCK, BLOCK, -1, dtype=bool)
    inclusive = jnp.tri(BLOCK, BLOCK, 0, dtype=bool)
    strict_ratio = jnp.where(strict, jnp.exp(jnp.where(strict, spread, 0.0)), 0.0)
    inclusive_ratio = jnp.where(inclusive, jnp.exp(jnp.where(inclusive, spread, 0.0)), 0.0)
    key_gram = jnp.einsum("hncd,hnsd->hncs", key_heads, key_heads, precision=highest)
    system = jnp.eye(BLOCK, dtype=key_gram.dtype) + strength[..., :, None] * strict_ratio * key_gram
    decay_now = jnp.exp(running)
    right_side = jnp.concatenate(
        [strength[..., None] * value_heads, (strength * decay_now)[..., None] * key_heads], axis=-1
    )
    solved = lax.linalg.triangular_solve(
        system, right_side, left_side=True, lower=True, unit_diagonal=True
    )
    base_values = solved[..., :DV]
    key_mix = solved[..., DV:]
    to_end = jnp.exp(running[..., -1:] - running)
    carried_keys = to_end[..., None] * key_heads
    drive_term = jnp.einsum("hncd,hnce->hnde", carried_keys, base_values, precision=highest)
    identity = jnp.eye(DK, dtype=key_gram.dtype)
    transition = jnp.exp(running[..., -1])[..., None, None] * identity - jnp.einsum(
        "hncd,hnce->hnde", carried_keys, key_mix, precision=highest
    )
    scores = inclusive_ratio * jnp.einsum(
        "hncd,hnsd->hncs", query_heads, key_heads, precision=highest
    )
    local_part = jnp.einsum("hncs,hnse->hnce", scores, base_values, precision=highest)
    row_reader = decay_now[..., None] * query_heads - jnp.einsum(
        "hncs,hnsd->hncd", scores, key_mix, precision=highest
    )
    return (local_part, row_reader, drive_term, transition)


def apply_move(move_piece, current):
    return jnp.einsum("hde,hef->hdf", move_piece, current, precision=highest)


def sweep(entering, local_part, row_reader, drive_term, transition):

    def advance(current, pieces):
        local_piece, reader_piece, drive_piece, move_piece = pieces
        emitted = local_piece + jnp.einsum("hcd,hde->hce", reader_piece, current, precision=highest)
        following = apply_move(move_piece, current) + drive_piece
        return (following, (emitted, following))

    block_major = tuple(
        (jnp.moveaxis(member, 1, 0) for member in (local_part, row_reader, drive_term, transition))
    )
    return lax.scan(advance, entering, block_major)


def on_device(
    stream,
    norm_gain,
    w_query,
    w_key,
    w_value,
    w_beta,
    w_decay,
    a_log,
    dt_bias,
    beta_bias,
    head_gain,
    w_output,
    carry_state,
):
    stream_rows = stream[0]
    projected = project(
        stream_rows,
        norm_gain[0],
        w_query[0],
        w_key[0],
        w_value[0],
        w_beta[0],
        w_decay[0],
        a_log[0],
        dt_bias[0],
        beta_bias[0],
    )
    local_part, row_reader, drive_term, transition = block_parts(
        *[to_blocks(member) for member in projected]
    )
    identity = jnp.broadcast_to(jnp.eye(DK, dtype=jnp.float32), (VH, DK, DK))
    nothing = jnp.zeros((VH, DK, DV), jnp.float32)

    def accumulate(carried, pieces):
        current, composed = carried
        drive_piece, move_piece = pieces
        return (
            (apply_move(move_piece, current) + drive_piece, apply_move(move_piece, composed)),
            None,
        )

    (local_end, total_move), _ = lax.scan(
        accumulate,
        (nothing, identity),
        (jnp.moveaxis(drive_term, 1, 0), jnp.moveaxis(transition, 1, 0)),
    )
    initial = carry_state[0]
    position = lax.axis_index("seq")

    def handoff_turn(turn_index, entering_state):
        leaving = apply_move(total_move, entering_state) + local_end
        arrived = from_behind(leaving, "seq", 1)
        return jnp.where(position == 0, initial, arrived)

    entering = lax.fori_loop(0, lax.axis_size("seq") - 1, handoff_turn, initial)
    _, (emitted, states) = sweep(entering, local_part, row_reader, drive_term, transition)
    core_out = emitted.transpose(0, 2, 1, 3).reshape(-1, VH, DV)
    normalized = (
        normalize_rows(core_out, head_gain[0], 1e-06)
        .astype(jnp.bfloat16)
        .reshape(core_out.shape[0], VH * DV)
    )
    layer_out = stream_rows + jnp.dot(normalized, w_output[0], preferred_element_type=jnp.float32)
    next_rows = passed_along(layer_out, "section", 1)
    return (next_rows[None], states[-1][None, None])


def solution(mesh):
    placed = (
        P("section", "seq", None),
        P("section", None),
        P("section", None, None),
        P("section", None, None),
        P("section", None, None),
        P("section", None, None),
        P("section", None, None),
        P("section", None),
        P("section", None),
        P("section", None),
        P("section", None),
        P("section", None, None),
        P("section", None, None, None),
    )
    return jax.shard_map(
        on_device,
        mesh=mesh,
        in_specs=placed,
        out_specs=(P("section", "seq", None), P("section", "seq", None, None, None)),
        check_vma=False,
    )
```

profile of v0, /device:TPU:64, one launch (start us, length us, event | category | flops | bytes accessed | tf_op | source)
XLA Modules:
  0.0 974.3 jit_solution(7226341731318368379)
XLA Ops:
  16.3 158.6 %custom-call.3 = f32[16,1,1,128,128]{3,4,2,1,0:T(8,128)} custom-call(f32[16,1,1,128,128]{4,3,2,1,0:T(8,128)} %fusion.17), custom_call_target="InvertDiagBlocksLowerTriangular" | custom-call | tf_op jit(solution)/shard_map/triangular_solve | solution.py:91
  199.5 758.9 %while.8 = (s32[]{:T(128)}, f32[16,128,128]{2,1,0:T(8,128)S(1)}, pred[]{:T(512)}, f32[16,128,128]{2,1,0:T(8,128)}, f32[16,128,128]{2,1,0:T(8,128)}, /*index=5*/f32[16,128,128]{2,1,0:T(8,128)}, s32[]{:T(128)}) while((s32[]{:T(128)}, f32[16,128,128]{2,1,0:T(8,128)S(1)}, pred[]{:T(512)}, f32[16,128,128]{2,1,0:T(8,128)}, ...), condition=%wide.region_5.6_spmd, body=%wide.region_4.5_spmd.sunk | while | flops 403177472 | bytes 15728786 | solution.py:186
  205.1 16.5 %collective-permute-done = f32[16,128,128]{2,1,0:T(8,128)S(1)} collective-permute-done((f32[16,128,128]{2,1,0:T(8,128)}, f32[16,128,128]{2,1,0:T(8,128)S(1)}, u32[]{:S(2)}, u32[]{:S(2)}) %collective-permute-start) | collective-permute-done | bytes 1048608 | tf_op jit(solution)/shard_map/while/body/eval_jaxpr/ppermute | solution.py:19
  229.6 16.5 %collective-permute-done = f32[16,128,128]{2,1,0:T(8,128)S(1)} collective-permute-done((f32[16,128,128]{2,1,0:T(8,128)}, f32[16,128,128]{2,1,0:T(8,128)S(1)}, u32[]{:S(2)}, u32[]{:S(2)}) %collective-permute-start) | collective-permute-done | bytes 1048608 | tf_op jit(solution)/shard_map/while/body/eval_jaxpr/ppermute | solution.py:19
  254.1 16.5 %collective-permute-done = f32[16,128,128]{2,1,0:T(8,128)S(1)} collective-permute-done((f32[16,128,128]{2,1,0:T(8,128)}, f32[16,128,128]{2,1,0:T(8,128)S(1)}, u32[]{:S(2)}, u32[]{:S(2)}) %collective-permute-start) | collective-permute-done | bytes 1048608 | tf_op jit(solution)/shard_map/while/body/eval_jaxpr/ppermute | solution.py:19
  278.6 16.5 %collective-permute-done = f32[16,128,128]{2,1,0:T(8,128)S(1)} collective-permute-done((f32[16,128,128]{2,1,0:T(8,128)}, f32[16,128,128]{2,1,0:T(8,128)S(1)}, u32[]{:S(2)}, u32[]{:S(2)}) %collective-permute-start) | collective-permute-done | bytes 1048608 | tf_op jit(solution)/shard_map/while/body/eval_jaxpr/ppermute | solution.py:19
  303.1 16.5 %collective-permute-done = f32[16,128,128]{2,1,0:T(8,128)S(1)} collective-permute-done((f32[16,128,128]{2,1,0:T(8,128)}, f32[16,128,128]{2,1,0:T(8,128)S(1)}, u32[]{:S(2)}, u32[]{:S(2)}) %collective-permute-start) | collective-permute-done | bytes 1048608 | tf_op jit(solution)/shard_map/while/body/eval_jaxpr/ppermute | solution.py:19
  327.6 16.5 %collective-permute-done = f32[16,128,128]{2,1,0:T(8,128)S(1)} collective-permute-done((f32[16,128,128]{2,1,0:T(8,128)}, f32[16,128,128]{2,1,0:T(8,128)S(1)}, u32[]{:S(2)}, u32[]{:S(2)}) %collective-permute-start) | collective-permute-done | bytes 1048608 | tf_op jit(solution)/shard_map/while/body/eval_jaxpr/ppermute | solution.py:19
  352.0 16.5 %collective-permute-done = f32[16,128,128]{2,1,0:T(8,128)S(1)} collective-permute-done((f32[16,128,128]{2,1,0:T(8,128)}, f32[16,128,128]{2,1,0:T(8,128)S(1)}, u32[]{:S(2)}, u32[]{:S(2)}) %collective-permute-start) | collective-permute-done | bytes 1048608 | tf_op jit(solution)/shard_map/while/body/eval_jaxpr/ppermute | solution.py:19
  376.5 16.5 %collective-permute-done = f32[16,128,128]{2,1,0:T(8,128)S(1)} collective-permute-done((f32[16,128,128]{2,1,0:T(8,128)}, f32[16,128,128]{2,1,0:T(8,128)S(1)}, u32[]{:S(2)}, u32[]{:S(2)}) %collective-permute-start) | collective-permute-done | bytes 1048608 | tf_op jit(solution)/shard_map/while/body/eval_jaxpr/ppermute | solution.py:19
  401.0 16.5 %collective-permute-done = f32[16,128,128]{2,1,0:T(8,128)S(1)} collective-permute-done((f32[16,128,128]{2,1,0:T(8,128)}, f32[16,128,128]{2,1,0:T(8,128)S(1)}, u32[]{:S(2)}, u32[]{:S(2)}) %collective-permute-start) | collective-permute-done | bytes 1048608 | tf_op jit(solution)/shard_map/while/body/eval_jaxpr/ppermute | solution.py:19
  425.5 16.5 %collective-permute-done = f32[16,128,128]{2,1,0:T(8,128)S(1)} collective-permute-done((f32[16,128,128]{2,1,0:T(8,128)}, f32[16,128,128]{2,1,0:T(8,128)S(1)}, u32[]{:S(2)}, u32[]{:S(2)}) %collective-permute-start) | collective-permute-done | bytes 1048608 | tf_op jit(solution)/shard_map/while/body/eval_jaxpr/ppermute | solution.py:19
  450.0 16.5 %collective-permute-done = f32[16,128,128]{2,1,0:T(8,128)S(1)} collective-permute-done((f32[16,128,128]{2,1,0:T(8,128)}, f32[16,128,128]{2,1,0:T(8,128)S(1)}, u32[]{:S(2)}, u32[]{:S(2)}) %collective-permute-start) | collective-permute-done | bytes 1048608 | tf_op jit(solution)/shard_map/while/body/eval_jaxpr/ppermute | solution.py:19
  474.4 16.5 %collective-permute-done = f32[16,128,128]{2,1,0:T(8,128)S(1)} collective-permute-done((f32[16,128,128]{2,1,0:T(8,128)}, f32[16,128,128]{2,1,0:T(8,128)S(1)}, u32[]{:S(2)}, u32[]{:S(2)}) %collective-permute-start) | collective-permute-done | bytes 1048608 | tf_op jit(solution)/shard_map/while/body/eval_jaxpr/ppermute | solution.py:19
  498.9 16.5 %collective-permute-done = f32[16,128,128]{2,1,0:T(8,128)S(1)} collective-permute-done((f32[16,128,128]{2,1,0:T(8,128)}, f32[16,128,128]{2,1,0:T(8,128)S(1)}, u32[]{:S(2)}, u32[]{:S(2)}) %collective-permute-start) | collective-permute-done | bytes 1048608 | tf_op jit(solution)/shard_map/while/body/eval_jaxpr/ppermute | solution.py:19
  523.4 16.5 %collective-permute-done = f32[16,128,128]{2,1,0:T(8,128)S(1)} collective-permute-done((f32[16,128,128]{2,1,0:T(8,128)}, f32[16,128,128]{2,1,0:T(8,128)S(1)}, u32[]{:S(2)}, u32[]{:S(2)}) %collective-permute-start) | collective-permute-done | bytes 1048608 | tf_op jit(solution)/shard_map/while/body/eval_jaxpr/ppermute | solution.py:19
  547.9 16.5 %collective-permute-done = f32[16,128,128]{2,1,0:T(8,128)S(1)} collective-permute-done((f32[16,128,128]{2,1,0:T(8,128)}, f32[16,128,128]{2,1,0:T(8,128)S(1)}, u32[]{:S(2)}, u32[]{:S(2)}) %collective-permute-start) | collective-permute-done | bytes 1048608 | tf_op jit(solution)/shard_map/while/body/eval_jaxpr/ppermute | solution.py:19
  572.4 16.5 %collective-permute-done = f32[16,128,128]{2,1,0:T(8,128)S(1)} collective-permute-done((f32[16,128,128]{2,1,0:T(8,128)}, f32[16,128,128]{2,1,0:T(8,128)S(1)}, u32[]{:S(2)}, u32[]{:S(2)}) %collective-permute-start) | collective-permute-done | bytes 1048608 | tf_op jit(solution)/shard_map/while/body/eval_jaxpr/ppermute | solution.py:19
  596.9 16.5 %collective-permute-done = f32[16,128,128]{2,1,0:T(8,128)S(1)} collective-permute-done((f32[16,128,128]{2,1,0:T(8,128)}, f32[16,128,128]{2,1,0:T(8,128)S(1)}, u32[]{:S(2)}, u32[]{:S(2)}) %collective-permute-start) | collective-permute-done | bytes 1048608 | tf_op jit(solution)/shard_map/while/body/eval_jaxpr/ppermute | solution.py:19
  621.3 16.5 %collective-permute-done = f32[16,128,128]{2,1,0:T(8,128)S(1)} collective-permute-done((f32[16,128,128]{2,1,0:T(8,128)}, f32[16,128,128]{2,1,0:T(8,128)S(1)}, u32[]{:S(2)}, u32[]{:S(2)}) %collective-permute-start) | collective-permute-done | bytes 1048608 | tf_op jit(solution)/shard_map/while/body/eval_jaxpr/ppermute | solution.py:19
  645.8 16.5 %collective-permute-done = f32[16,128,128]{2,1,0:T(8,128)S(1)} collective-permute-done((f32[16,128,128]{2,1,0:T(8,128)}, f32[16,128,128]{2,1,0:T(8,128)S(1)}, u32[]{:S(2)}, u32[]{:S(2)}) %collective-permute-start) | collective-permute-done | bytes 1048608 | tf_op jit(solution)/shard_map/while/body/eval_jaxpr/ppermute | solution.py:19
  670.3 16.5 %collective-permute-done = f32[16,128,128]{2,1,0:T(8,128)S(1)} collective-permute-done((f32[16,128,128]{2,1,0:T(8,128)}, f32[16,128,128]{2,1,0:T(8,128)S(1)}, u32[]{:S(2)}, u32[]{:S(2)}) %collective-permute-start) | collective-permute-done | bytes 1048608 | tf_op jit(solution)/shard_map/while/body/eval_jaxpr/ppermute | solution.py:19
  694.8 16.5 %collective-permute-done = f32[16,128,128]{2,1,0:T(8,128)S(1)} collective-permute-done((f32[16,128,128]{2,1,0:T(8,128)}, f32[16,128,128]{2,1,0:T(8,128)S(1)}, u32[]{:S(2)}, u32[]{:S(2)}) %collective-permute-start) | collective-permute-done | bytes 1048608 | tf_op jit(solution)/shard_map/while/body/eval_jaxpr/ppermute | solution.py:19
  719.3 16.5 %collective-permute-done = f32[16,128,128]{2,1,0:T(8,128)S(1)} collective-permute-done((f32[16,128,128]{2,1,0:T(8,128)}, f32[16,128,128]{2,1,0:T(8,128)S(1)}, u32[]{:S(2)}, u32[]{:S(2)}) %collective-permute-start) | collective-permute-done | bytes 1048608 | tf_op jit(solution)/shard_map/while/body/eval_jaxpr/ppermute | solution.py:19
  743.8 16.5 %collective-permute-done = f32[16,128,128]{2,1,0:T(8,128)S(1)} collective-permute-done((f32[16,128,128]{2,1,0:T(8,128)}, f32[16,128,128]{2,1,0:T(8,128)S(1)}, u32[]{:S(2)}, u32[]{:S(2)}) %collective-permute-start) | collective-permute-done | bytes 1048608 | tf_op jit(solution)/shard_map/while/body/eval_jaxpr/ppermute | solution.py:19
  768.2 16.5 %collective-permute-done = f32[16,128,128]{2,1,0:T(8,128)S(1)} collective-permute-done((f32[16,128,128]{2,1,0:T(8,128)}, f32[16,128,128]{2,1,0:T(8,128)S(1)}, u32[]{:S(2)}, u32[]{:S(2)}) %collective-permute-start) | collective-permute-done | bytes 1048608 | tf_op jit(solution)/shard_map/while/body/eval_jaxpr/ppermute | solution.py:19
  792.7 16.5 %collective-permute-done = f32[16,128,128]{2,1,0:T(8,128)S(1)} collective-permute-done((f32[16,128,128]{2,1,0:T(8,128)}, f32[16,128,128]{2,1,0:T(8,128)S(1)}, u32[]{:S(2)}, u32[]{:S(2)}) %collective-permute-start) | collective-permute-done | bytes 1048608 | tf_op jit(solution)/shard_map/while/body/eval_jaxpr/ppermute | solution.py:19
  817.2 16.5 %collective-permute-done = f32[16,128,128]{2,1,0:T(8,128)S(1)} collective-permute-done((f32[16,128,128]{2,1,0:T(8,128)}, f32[16,128,128]{2,1,0:T(8,128)S(1)}, u32[]{:S(2)}, u32[]{:S(2)}) %collective-permute-start) | collective-permute-done | bytes 1048608 | tf_op jit(solution)/shard_map/while/body/eval_jaxpr/ppermute | solution.py:19
  841.7 16.5 %collective-permute-done = f32[16,128,128]{2,1,0:T(8,128)S(1)} collective-permute-done((f32[16,128,128]{2,1,0:T(8,128)}, f32[16,128,128]{2,1,0:T(8,128)S(1)}, u32[]{:S(2)}, u32[]{:S(2)}) %collective-permute-start) | collective-permute-done | bytes 1048608 | tf_op jit(solution)/shard_map/while/body/eval_jaxpr/ppermute | solution.py:19
  890.6 16.5 %collective-permute-done = f32[16,128,128]{2,1,0:T(8,128)S(1)} collective-permute-done((f32[16,128,128]{2,1,0:T(8,128)}, f32[16,128,128]{2,1,0:T(8,128)S(1)}, u32[]{:S(2)}, u32[]{:S(2)}) %collective-permute-start) | collective-permute-done | bytes 1048608 | tf_op jit(solution)/shard_map/while/body/eval_jaxpr/ppermute | solution.py:19
  915.1 16.5 %collective-permute-done = f32[16,128,128]{2,1,0:T(8,128)S(1)} collective-permute-done((f32[16,128,128]{2,1,0:T(8,128)}, f32[16,128,128]{2,1,0:T(8,128)S(1)}, u32[]{:S(2)}, u32[]{:S(2)}) %collective-permute-start) | collective-permute-done | bytes 1048608 | tf_op jit(solution)/shard_map/while/body/eval_jaxpr/ppermute | solution.py:19
  939.6 16.5 %collective-permute-done = f32[16,128,128]{2,1,0:T(8,128)S(1)} collective-permute-done((f32[16,128,128]{2,1,0:T(8,128)}, f32[16,128,128]{2,1,0:T(8,128)S(1)}, u32[]{:S(2)}, u32[]{:S(2)}) %collective-permute-start) | collective-permute-done | bytes 1048608 | tf_op jit(solution)/shard_map/while/body/eval_jaxpr/ppermute | solution.py:19
  (246 shorter events, 318.5 us)
Async XLA Ops:
  203.2 18.4 %collective-permute-start = (f32[16,128,128]{2,1,0:T(8,128)}, f32[16,128,128]{2,1,0:T(8,128)S(1)}, u32[]{:S(2)}, u32[]{:S(2)}) collective-permute-start(f32[16,128,128]{2,1,0:T(8,128)} %convolution_add_fusion.7), channel_id=1, source_target_pairs={{0,1},{1,2},{2,3},{3,4},{4,5},{5,6},{6,7},{7,8},{8,9},{9,10},{10,1... | collective-permute-start | bytes 3145736 | tf_op jit(solution)/shard_map/while/body/eval_jaxpr/ppermute | solution.py:19
  227.7 18.4 %collective-permute-start = (f32[16,128,128]{2,1,0:T(8,128)}, f32[16,128,128]{2,1,0:T(8,128)S(1)}, u32[]{:S(2)}, u32[]{:S(2)}) collective-permute-start(f32[16,128,128]{2,1,0:T(8,128)} %convolution_add_fusion.7), channel_id=1, source_target_pairs={{0,1},{1,2},{2,3},{3,4},{4,5},{5,6},{6,7},{7,8},{8,9},{9,10},{10,1... | collective-permute-start | bytes 3145736 | tf_op jit(solution)/shard_map/while/body/eval_jaxpr/ppermute | solution.py:19
  252.2 18.4 %collective-permute-start = (f32[16,128,128]{2,1,0:T(8,128)}, f32[16,128,128]{2,1,0:T(8,128)S(1)}, u32[]{:S(2)}, u32[]{:S(2)}) collective-permute-start(f32[16,128,128]{2,1,0:T(8,128)} %convolution_add_fusion.7), channel_id=1, source_target_pairs={{0,1},{1,2},{2,3},{3,4},{4,5},{5,6},{6,7},{7,8},{8,9},{9,10},{10,1... | collective-permute-start | bytes 3145736 | tf_op jit(solution)/shard_map/while/body/eval_jaxpr/ppermute | solution.py:19
  276.7 18.4 %collective-permute-start = (f32[16,128,128]{2,1,0:T(8,128)}, f32[16,128,128]{2,1,0:T(8,128)S(1)}, u32[]{:S(2)}, u32[]{:S(2)}) collective-permute-start(f32[16,128,128]{2,1,0:T(8,128)} %convolution_add_fusion.7), channel_id=1, source_target_pairs={{0,1},{1,2},{2,3},{3,4},{4,5},{5,6},{6,7},{7,8},{8,9},{9,10},{10,1... | collective-permute-start | bytes 3145736 | tf_op jit(solution)/shard_map/while/body/eval_jaxpr/ppermute | solution.py:19
  301.2 18.4 %collective-permute-start = (f32[16,128,128]{2,1,0:T(8,128)}, f32[16,128,128]{2,1,0:T(8,128)S(1)}, u32[]{:S(2)}, u32[]{:S(2)}) collective-permute-start(f32[16,128,128]{2,1,0:T(8,128)} %convolution_add_fusion.7), channel_id=1, source_target_pairs={{0,1},{1,2},{2,3},{3,4},{4,5},{5,6},{6,7},{7,8},{8,9},{9,10},{10,1... | collective-permute-start | bytes 3145736 | tf_op jit(solution)/shard_map/while/body/eval_jaxpr/ppermute | solution.py:19
  325.6 18.4 %collective-permute-start = (f32[16,128,128]{2,1,0:T(8,128)}, f32[16,128,128]{2,1,0:T(8,128)S(1)}, u32[]{:S(2)}, u32[]{:S(2)}) collective-permute-start(f32[16,128,128]{2,1,0:T(8,128)} %convolution_add_fusion.7), channel_id=1, source_target_pairs={{0,1},{1,2},{2,3},{3,4},{4,5},{5,6},{6,7},{7,8},{8,9},{9,10},{10,1... | collective-permute-start | bytes 3145736 | tf_op jit(solution)/shard_map/while/body/eval_jaxpr/ppermute | solution.py:19
  350.1 18.4 %collective-permute-start = (f32[16,128,128]{2,1,0:T(8,128)}, f32[16,128,128]{2,1,0:T(8,128)S(1)}, u32[]{:S(2)}, u32[]{:S(2)}) collective-permute-start(f32[16,128,128]{2,1,0:T(8,128)} %convolution_add_fusion.7), channel_id=1, source_target_pairs={{0,1},{1,2},{2,3},{3,4},{4,5},{5,6},{6,7},{7,8},{8,9},{9,10},{10,1... | collective-permute-start | bytes 3145736 | tf_op jit(solution)/shard_map/while/body/eval_jaxpr/ppermute | solution.py:19
  374.6 18.4 %collective-permute-start = (f32[16,128,128]{2,1,0:T(8,128)}, f32[16,128,128]{2,1,0:T(8,128)S(1)}, u32[]{:S(2)}, u32[]{:S(2)}) collective-permute-start(f32[16,128,128]{2,1,0:T(8,128)} %convolution_add_fusion.7), channel_id=1, source_target_pairs={{0,1},{1,2},{2,3},{3,4},{4,5},{5,6},{6,7},{7,8},{8,9},{9,10},{10,1... | collective-permute-start | bytes 3145736 | tf_op jit(solution)/shard_map/while/body/eval_jaxpr/ppermute | solution.py:19
  399.1 18.4 %collective-permute-start = (f32[16,128,128]{2,1,0:T(8,128)}, f32[16,128,128]{2,1,0:T(8,128)S(1)}, u32[]{:S(2)}, u32[]{:S(2)}) collective-permute-start(f32[16,128,128]{2,1,0:T(8,128)} %convolution_add_fusion.7), channel_id=1, source_target_pairs={{0,1},{1,2},{2,3},{3,4},{4,5},{5,6},{6,7},{7,8},{8,9},{9,10},{10,1... | collective-permute-start | bytes 3145736 | tf_op jit(solution)/shard_map/while/body/eval_jaxpr/ppermute | solution.py:19
  423.6 18.4 %collective-permute-start = (f32[16,128,128]{2,1,0:T(8,128)}, f32[16,128,128]{2,1,0:T(8,128)S(1)}, u32[]{:S(2)}, u32[]{:S(2)}) collective-permute-start(f32[16,128,128]{2,1,0:T(8,128)} %convolution_add_fusion.7), channel_id=1, source_target_pairs={{0,1},{1,2},{2,3},{3,4},{4,5},{5,6},{6,7},{7,8},{8,9},{9,10},{10,1... | collective-permute-start | bytes 3145736 | tf_op jit(solution)/shard_map/while/body/eval_jaxpr/ppermute | solution.py:19
  448.0 18.4 %collective-permute-start = (f32[16,128,128]{2,1,0:T(8,128)}, f32[16,128,128]{2,1,0:T(8,128)S(1)}, u32[]{:S(2)}, u32[]{:S(2)}) collective-permute-start(f32[16,128,128]{2,1,0:T(8,128)} %convolution_add_fusion.7), channel_id=1, source_target_pairs={{0,1},{1,2},{2,3},{3,4},{4,5},{5,6},{6,7},{7,8},{8,9},{9,10},{10,1... | collective-permute-start | bytes 3145736 | tf_op jit(solution)/shard_map/while/body/eval_jaxpr/ppermute | solution.py:19
  472.5 18.4 %collective-permute-start = (f32[16,128,128]{2,1,0:T(8,128)}, f32[16,128,128]{2,1,0:T(8,128)S(1)}, u32[]{:S(2)}, u32[]{:S(2)}) collective-permute-start(f32[16,128,128]{2,1,0:T(8,128)} %convolution_add_fusion.7), channel_id=1, source_target_pairs={{0,1},{1,2},{2,3},{3,4},{4,5},{5,6},{6,7},{7,8},{8,9},{9,10},{10,1... | collective-permute-start | bytes 3145736 | tf_op jit(solution)/shard_map/while/body/eval_jaxpr/ppermute | solution.py:19
  497.0 18.4 %collective-permute-start = (f32[16,128,128]{2,1,0:T(8,128)}, f32[16,128,128]{2,1,0:T(8,128)S(1)}, u32[]{:S(2)}, u32[]{:S(2)}) collective-permute-start(f32[16,128,128]{2,1,0:T(8,128)} %convolution_add_fusion.7), channel_id=1, source_target_pairs={{0,1},{1,2},{2,3},{3,4},{4,5},{5,6},{6,7},{7,8},{8,9},{9,10},{10,1... | collective-permute-start | bytes 3145736 | tf_op jit(solution)/shard_map/while/body/eval_jaxpr/ppermute | solution.py:19
  521.5 18.4 %collective-permute-start = (f32[16,128,128]{2,1,0:T(8,128)}, f32[16,128,128]{2,1,0:T(8,128)S(1)}, u32[]{:S(2)}, u32[]{:S(2)}) collective-permute-start(f32[16,128,128]{2,1,0:T(8,128)} %convolution_add_fusion.7), channel_id=1, source_target_pairs={{0,1},{1,2},{2,3},{3,4},{4,5},{5,6},{6,7},{7,8},{8,9},{9,10},{10,1... | collective-permute-start | bytes 3145736 | tf_op jit(solution)/shard_map/while/body/eval_jaxpr/ppermute | solution.py:19
  546.0 18.4 %collective-permute-start = (f32[16,128,128]{2,1,0:T(8,128)}, f32[16,128,128]{2,1,0:T(8,128)S(1)}, u32[]{:S(2)}, u32[]{:S(2)}) collective-permute-start(f32[16,128,128]{2,1,0:T(8,128)} %convolution_add_fusion.7), channel_id=1, source_target_pairs={{0,1},{1,2},{2,3},{3,4},{4,5},{5,6},{6,7},{7,8},{8,9},{9,10},{10,1... | collective-permute-start | bytes 3145736 | tf_op jit(solution)/shard_map/while/body/eval_jaxpr/ppermute | solution.py:19
  570.5 18.4 %collective-permute-start = (f32[16,128,128]{2,1,0:T(8,128)}, f32[16,128,128]{2,1,0:T(8,128)S(1)}, u32[]{:S(2)}, u32[]{:S(2)}) collective-permute-start(f32[16,128,128]{2,1,0:T(8,128)} %convolution_add_fusion.7), channel_id=1, source_target_pairs={{0,1},{1,2},{2,3},{3,4},{4,5},{5,6},{6,7},{7,8},{8,9},{9,10},{10,1... | collective-permute-start | bytes 3145736 | tf_op jit(solution)/shard_map/while/body/eval_jaxpr/ppermute | solution.py:19
  594.9 18.4 %collective-permute-start = (f32[16,128,128]{2,1,0:T(8,128)}, f32[16,128,128]{2,1,0:T(8,128)S(1)}, u32[]{:S(2)}, u32[]{:S(2)}) collective-permute-start(f32[16,128,128]{2,1,0:T(8,128)} %convolution_add_fusion.7), channel_id=1, source_target_pairs={{0,1},{1,2},{2,3},{3,4},{4,5},{5,6},{6,7},{7,8},{8,9},{9,10},{10,1... | collective-permute-start | bytes 3145736 | tf_op jit(solution)/shard_map/while/body/eval_jaxpr/ppermute | solution.py:19
  619.4 18.4 %collective-permute-start = (f32[16,128,128]{2,1,0:T(8,128)}, f32[16,128,128]{2,1,0:T(8,128)S(1)}, u32[]{:S(2)}, u32[]{:S(2)}) collective-permute-start(f32[16,128,128]{2,1,0:T(8,128)} %convolution_add_fusion.7), channel_id=1, source_target_pairs={{0,1},{1,2},{2,3},{3,4},{4,5},{5,6},{6,7},{7,8},{8,9},{9,10},{10,1... | collective-permute-start | bytes 3145736 | tf_op jit(solution)/shard_map/while/body/eval_jaxpr/ppermute | solution.py:19
  643.9 18.4 %collective-permute-start = (f32[16,128,128]{2,1,0:T(8,128)}, f32[16,128,128]{2,1,0:T(8,128)S(1)}, u32[]{:S(2)}, u32[]{:S(2)}) collective-permute-start(f32[16,128,128]{2,1,0:T(8,128)} %convolution_add_fusion.7), channel_id=1, source_target_pairs={{0,1},{1,2},{2,3},{3,4},{4,5},{5,6},{6,7},{7,8},{8,9},{9,10},{10,1... | collective-permute-start | bytes 3145736 | tf_op jit(solution)/shard_map/while/body/eval_jaxpr/ppermute | solution.py:19
  668.4 18.4 %collective-permute-start = (f32[16,128,128]{2,1,0:T(8,128)}, f32[16,128,128]{2,1,0:T(8,128)S(1)}, u32[]{:S(2)}, u32[]{:S(2)}) collective-permute-start(f32[16,128,128]{2,1,0:T(8,128)} %convolution_add_fusion.7), channel_id=1, source_target_pairs={{0,1},{1,2},{2,3},{3,4},{4,5},{5,6},{6,7},{7,8},{8,9},{9,10},{10,1... | collective-permute-start | bytes 3145736 | tf_op jit(solution)/shard_map/while/body/eval_jaxpr/ppermute | solution.py:19
  692.9 18.4 %collective-permute-start = (f32[16,128,128]{2,1,0:T(8,128)}, f32[16,128,128]{2,1,0:T(8,128)S(1)}, u32[]{:S(2)}, u32[]{:S(2)}) collective-permute-start(f32[16,128,128]{2,1,0:T(8,128)} %convolution_add_fusion.7), channel_id=1, source_target_pairs={{0,1},{1,2},{2,3},{3,4},{4,5},{5,6},{6,7},{7,8},{8,9},{9,10},{10,1... | collective-permute-start | bytes 3145736 | tf_op jit(solution)/shard_map/while/body/eval_jaxpr/ppermute | solution.py:19
  717.4 18.4 %collective-permute-start = (f32[16,128,128]{2,1,0:T(8,128)}, f32[16,128,128]{2,1,0:T(8,128)S(1)}, u32[]{:S(2)}, u32[]{:S(2)}) collective-permute-start(f32[16,128,128]{2,1,0:T(8,128)} %convolution_add_fusion.7), channel_id=1, source_target_pairs={{0,1},{1,2},{2,3},{3,4},{4,5},{5,6},{6,7},{7,8},{8,9},{9,10},{10,1... | collective-permute-start | bytes 3145736 | tf_op jit(solution)/shard_map/while/body/eval_jaxpr/ppermute | solution.py:19
  741.8 18.4 %collective-permute-start = (f32[16,128,128]{2,1,0:T(8,128)}, f32[16,128,128]{2,1,0:T(8,128)S(1)}, u32[]{:S(2)}, u32[]{:S(2)}) collective-permute-start(f32[16,128,128]{2,1,0:T(8,128)} %convolution_add_fusion.7), channel_id=1, source_target_pairs={{0,1},{1,2},{2,3},{3,4},{4,5},{5,6},{6,7},{7,8},{8,9},{9,10},{10,1... | collective-permute-start | bytes 3145736 | tf_op jit(solution)/shard_map/while/body/eval_jaxpr/ppermute | solution.py:19
  766.3 18.4 %collective-permute-start = (f32[16,128,128]{2,1,0:T(8,128)}, f32[16,128,128]{2,1,0:T(8,128)S(1)}, u32[]{:S(2)}, u32[]{:S(2)}) collective-permute-start(f32[16,128,128]{2,1,0:T(8,128)} %convolution_add_fusion.7), channel_id=1, source_target_pairs={{0,1},{1,2},{2,3},{3,4},{4,5},{5,6},{6,7},{7,8},{8,9},{9,10},{10,1... | collective-permute-start | bytes 3145736 | tf_op jit(solution)/shard_map/while/body/eval_jaxpr/ppermute | solution.py:19
  790.8 18.4 %collective-permute-start = (f32[16,128,128]{2,1,0:T(8,128)}, f32[16,128,128]{2,1,0:T(8,128)S(1)}, u32[]{:S(2)}, u32[]{:S(2)}) collective-permute-start(f32[16,128,128]{2,1,0:T(8,128)} %convolution_add_fusion.7), channel_id=1, source_target_pairs={{0,1},{1,2},{2,3},{3,4},{4,5},{5,6},{6,7},{7,8},{8,9},{9,10},{10,1... | collective-permute-start | bytes 3145736 | tf_op jit(solution)/shard_map/while/body/eval_jaxpr/ppermute | solution.py:19
  815.3 18.4 %collective-permute-start = (f32[16,128,128]{2,1,0:T(8,128)}, f32[16,128,128]{2,1,0:T(8,128)S(1)}, u32[]{:S(2)}, u32[]{:S(2)}) collective-permute-start(f32[16,128,128]{2,1,0:T(8,128)} %convolution_add_fusion.7), channel_id=1, source_target_pairs={{0,1},{1,2},{2,3},{3,4},{4,5},{5,6},{6,7},{7,8},{8,9},{9,10},{10,1... | collective-permute-start | bytes 3145736 | tf_op jit(solution)/shard_map/while/body/eval_jaxpr/ppermute | solution.py:19
  839.8 18.4 %collective-permute-start = (f32[16,128,128]{2,1,0:T(8,128)}, f32[16,128,128]{2,1,0:T(8,128)S(1)}, u32[]{:S(2)}, u32[]{:S(2)}) collective-permute-start(f32[16,128,128]{2,1,0:T(8,128)} %convolution_add_fusion.7), channel_id=1, source_target_pairs={{0,1},{1,2},{2,3},{3,4},{4,5},{5,6},{6,7},{7,8},{8,9},{9,10},{10,1... | collective-permute-start | bytes 3145736 | tf_op jit(solution)/shard_map/while/body/eval_jaxpr/ppermute | solution.py:19
  864.2 18.4 %collective-permute-start = (f32[16,128,128]{2,1,0:T(8,128)}, f32[16,128,128]{2,1,0:T(8,128)S(1)}, u32[]{:S(2)}, u32[]{:S(2)}) collective-permute-start(f32[16,128,128]{2,1,0:T(8,128)} %convolution_add_fusion.7), channel_id=1, source_target_pairs={{0,1},{1,2},{2,3},{3,4},{4,5},{5,6},{6,7},{7,8},{8,9},{9,10},{10,1... | collective-permute-start | bytes 3145736 | tf_op jit(solution)/shard_map/while/body/eval_jaxpr/ppermute | solution.py:19
  888.7 18.4 %collective-permute-start = (f32[16,128,128]{2,1,0:T(8,128)}, f32[16,128,128]{2,1,0:T(8,128)S(1)}, u32[]{:S(2)}, u32[]{:S(2)}) collective-permute-start(f32[16,128,128]{2,1,0:T(8,128)} %convolution_add_fusion.7), channel_id=1, source_target_pairs={{0,1},{1,2},{2,3},{3,4},{4,5},{5,6},{6,7},{7,8},{8,9},{9,10},{10,1... | collective-permute-start | bytes 3145736 | tf_op jit(solution)/shard_map/while/body/eval_jaxpr/ppermute | solution.py:19
  913.2 18.4 %collective-permute-start = (f32[16,128,128]{2,1,0:T(8,128)}, f32[16,128,128]{2,1,0:T(8,128)S(1)}, u32[]{:S(2)}, u32[]{:S(2)}) collective-permute-start(f32[16,128,128]{2,1,0:T(8,128)} %convolution_add_fusion.7), channel_id=1, source_target_pairs={{0,1},{1,2},{2,3},{3,4},{4,5},{5,6},{6,7},{7,8},{8,9},{9,10},{10,1... | collective-permute-start | bytes 3145736 | tf_op jit(solution)/shard_map/while/body/eval_jaxpr/ppermute | solution.py:19
  937.7 18.4 %collective-permute-start = (f32[16,128,128]{2,1,0:T(8,128)}, f32[16,128,128]{2,1,0:T(8,128)S(1)}, u32[]{:S(2)}, u32[]{:S(2)}) collective-permute-start(f32[16,128,128]{2,1,0:T(8,128)} %convolution_add_fusion.7), channel_id=1, source_target_pairs={{0,1},{1,2},{2,3},{3,4},{4,5},{5,6},{6,7},{7,8},{8,9},{9,10},{10,1... | collective-permute-start | bytes 3145736 | tf_op jit(solution)/shard_map/while/body/eval_jaxpr/ppermute | solution.py:19
  963.0 10.5 %collective-permute-start.1 = (f32[128,1024]{1,0:T(8,128)S(1)}, f32[128,1024]{1,0:T(8,128)S(1)}, u32[]{:S(2)}, u32[]{:S(2)}) collective-permute-start(f32[128,1024]{1,0:T(8,128)S(1)} %fusion.20), channel_id=1, source_target_pairs={{96,0},{0,32},{32,64},{64,96},{97,1},{1,33},{33,65},{65,97},{98,2}... | collective-permute-start | bytes 1572872 | tf_op jit(solution)/shard_map/ppermute | solution.py:25
  (50 other events, 844.3 us)
where the time goes:
time: 978 us; the launch traced here: 974 us
  waiting for transfers between devices  519 us (53%)
  other arithmetic  209 us (21%)
  matrix products  146 us (15%)
  starting transfers between devices  60.7 us (6%)
  local copies, waits for them, and re-layouts  37.6 us (4%)
    ppermute x31, waiting for transfers between devices, from_behind(): lax.ppermute(value, axis, [(source, source + steps) for source in range(l...  512 us
    another operation x4, other arithmetic, block_parts(): lax.linalg.triangular_solve(system, right_side, left_side=True, lower=Tru...  159 us
    dot_general x34, matrix products, apply_move(): return jnp.einsum('hde,hef->hdf', move_piece, current, precision=highest)  121 us
    ppermute x31, starting transfers between devices, from_behind(): lax.ppermute(value, axis, [(source, source + steps) for source in range(l...  59.1 us
    select_n x31, other arithmetic, handoff_turn(): return jnp.where(position == 0, initial, arrived)  41.6 us
    while x62, local copies, waits for them, and re-layouts  31 us
  transfers between devices with their start and end apart: 32, of which 32 were waited for; matrix products, arithmetic and copies ran while one was open for 0% of the time, Pallas kernels for 0%

commit v1 on v0

v1 whole, which is shorter than its diff:
```python
import functools

import jax
import jax.numpy as jnp
from jax import lax
from jax.experimental import pallas as pl
from jax.experimental.pallas import tpu as pltpu
from jax.sharding import PartitionSpec as P

KH = 8
VH = 16
DK = 128
DV = 128
T = 128
HALF = 64
GROUP = 8
f32 = jnp.float32
bf16 = jnp.bfloat16
HIGHEST = lax.Precision.HIGHEST
VMEM_LIMIT = 56 * 2**20


def parts(values):
    high = values.astype(bf16)
    return high, (values - high.astype(f32)).astype(bf16)


def left_parts(values):
    return jnp.concatenate(parts(values), axis=1)


def right_parts(values):
    both = jnp.concatenate(parts(values), axis=1)
    return jnp.concatenate([both, both], axis=0)


def right_parts_t(values):
    high, low = parts(values)
    return jnp.concatenate(
        [jnp.concatenate([high, high], axis=1), jnp.concatenate([low, low], axis=1)], axis=0
    )


def mm_parts(left, right):
    both = jnp.dot(left, right, preferred_element_type=f32)
    columns = both.shape[1] // 2
    return both[:, :columns] + both[:, columns:]


def mm(left, right):
    return mm_parts(left_parts(left), right_parts(right))


def mm_t(left, right):
    both = lax.dot_general(
        left_parts(left), right_parts_t(right), (((1,), (1,)), ((), ())), preferred_element_type=f32
    )
    columns = both.shape[1] // 2
    return both[:, :columns] + both[:, columns:]


def sigmoid(values):
    return 1.0 / (1.0 + jnp.exp(-values))


def silu(values):
    return values * sigmoid(values)


def softplus(values):
    return jnp.maximum(values, 0.0) + jnp.log1p(jnp.exp(-jnp.abs(values)))


def unit(values):
    return values * lax.rsqrt(jnp.sum(values * values, axis=-1, keepdims=True) + 1e-06)


def square_iotas():
    rows = lax.broadcasted_iota(jnp.int32, (T, T), 0)
    columns = lax.broadcasted_iota(jnp.int32, (T, T), 1)
    return rows, columns


def upper_inverses(uppers):
    rows, columns = square_iotas()
    identity = (rows == columns).astype(f32)
    inside = (rows >> 3) == (columns >> 3)
    small = [jnp.where(inside, u, 0.0) for u in uppers]
    squares = [mm(n, n) for n in small]
    stacked = [mm(jnp.concatenate([s, n], axis=0), s) for s, n in zip(squares, small)]
    firsts = [identity - n + s - z[T:] for n, s, z in zip(small, squares, stacked)]
    result = [p + mm(p, z[:T]) for p, z in zip(firsts, stacked)]
    for shift in (3, 4, 5, 6):
        off = ((rows >> (shift + 1)) == (columns >> (shift + 1))) & (
            (rows >> shift) != (columns >> shift)
        )
        lefts = [left_parts(w) for w in result]
        rights = [right_parts(w) for w in result]
        middles = [
            mm_parts(left_parts(jnp.where(off, u, 0.0)), r) for u, r in zip(uppers, rights)
        ]
        result = [
            w - mm_parts(left, right_parts(m)) for w, left, m in zip(result, lefts, middles)
        ]
    return result


def maps_kernel(
    x_ref,
    gain_ref,
    wk_ref,
    wv_ref,
    wb_ref,
    wd_ref,
    rate_ref,
    dtb_ref,
    bb_ref,
    maps_ref,
    kt_ref,
    yt_ref,
    rt_ref,
    rb_ref,
    normed_ref,
    bt_s,
):
    step = pl.program_id(0)
    rows, columns = square_iotas()

    @pl.when(step == 0)
    def _():
        x = x_ref[...]
        mean_square = jnp.mean(x * x, axis=-1, keepdims=True)
        normed = (x * lax.rsqrt(mean_square + 1e-06) * gain_ref[...]).astype(bf16)
        normed_ref[...] = normed
        beta = sigmoid(jnp.dot(normed, wb_ref[...], preferred_element_type=f32) + bb_ref[...])
        log_decay = -jnp.exp(rate_ref[...]) * softplus(
            jnp.dot(normed, wd_ref[...], preferred_element_type=f32) + dtb_ref[...]
        )
        contract0 = (((0,), (0,)), ((), ()))
        lower = (rows >= columns).astype(f32)
        upper = (rows <= columns).astype(f32)
        identity = (rows == columns).astype(f32)
        running = jnp.dot(lower, log_decay, precision=HIGHEST, preferred_element_type=f32)
        rt_ref[...] = lax.dot_general(
            log_decay, upper, contract0, precision=HIGHEST, preferred_element_type=f32
        )
        bt_s[...] = lax.dot_general(
            beta, identity, contract0, precision=HIGHEST, preferred_element_type=f32
        )
        for h in range(VH):
            rb_ref[h] = jnp.broadcast_to(running[:, h : h + 1], (T, T))

    normed = normed_ref[...]
    key_all = silu(jnp.dot(normed, wk_ref[...], preferred_element_type=f32))
    value_all = silu(jnp.dot(normed, wv_ref[...], preferred_element_type=f32))
    keys = [unit(key_all[:, i * DK : (i + 1) * DK]) for i in range(GROUP // 2)]
    keys_t = [k.T for k in keys]
    for i, kt in enumerate(keys_t):
        kt_ref[i] = kt
    grams = [mm(k, kt) for k, kt in zip(keys, keys_t)]
    key_rights = [right_parts(k) for k in keys]
    strict = rows < columns
    r_rows = [rt_ref[pl.ds(step * GROUP + i, 1), :] for i in range(GROUP)]
    b_rows = [bt_s[pl.ds(step * GROUP + i, 1), :] for i in range(GROUP)]
    uppers = []
    for i in range(GROUP):
        spread = jnp.minimum(r_rows[i] - rb_ref[step * GROUP + i], 0.0)
        uppers.append(jnp.where(strict, b_rows[i] * jnp.exp(spread) * grams[i // 2], 0.0))
    inverses = upper_inverses(uppers)
    solved = []
    for i in range(GROUP):
        value_t = value_all[:, i * DV : (i + 1) * DV].T
        right_t = jnp.concatenate(
            [b_rows[i] * value_t, (b_rows[i] * jnp.exp(r_rows[i])) * keys_t[i // 2]], axis=0
        )
        solved.append(mm(right_t, inverses[i]))
        yt_ref[i] = solved[i]
    identity = rows == columns
    for i in range(GROUP):
        end = r_rows[i][:, T - 1 : T]
        both = mm_parts(left_parts(solved[i] * jnp.exp(end - r_rows[i])), key_rights[i // 2])
        maps_ref[i, 0:DK] = jnp.where(identity, jnp.exp(end), 0.0) - both[DV:]
        maps_ref[i, DK : DK + DV] = both[:DV]


def make_maps(x, gain, wk, wv, wb, wd, rate, dtb, bb):
    steps = VH // GROUP
    whole = lambda a: pl.BlockSpec(a.shape, lambda s: (0,) * a.ndim)
    return pl.pallas_call(
        maps_kernel,
        grid=(steps,),
        in_specs=[
            whole(x),
            whole(gain),
            pl.BlockSpec((wk.shape[0], KH * DK // steps), lambda s: (0, s)),
            pl.BlockSpec((wv.shape[0], VH * DV // steps), lambda s: (0, s)),
            whole(wb),
            whole(wd),
            whole(rate),
            whole(dtb),
            whole(bb),
        ],
        out_specs=[
            pl.BlockSpec((GROUP, DK + DV, DK), lambda s: (s, 0, 0)),
            pl.BlockSpec((GROUP // 2, DK, T), lambda s: (s, 0, 0)),
            pl.BlockSpec((GROUP, DK + DV, T), lambda s: (s, 0, 0)),
            pl.BlockSpec((VH, T), lambda s: (0, 0)),
            pl.BlockSpec((VH, T, T), lambda s: (0, 0, 0)),
            pl.BlockSpec((T, x.shape[1]), lambda s: (0, 0)),
        ],
        out_shape=[
            jax.ShapeDtypeStruct((VH, DK + DV, DK), f32),
            jax.ShapeDtypeStruct((KH, DK, T), f32),
            jax.ShapeDtypeStruct((VH, DK + DV, T), f32),
            jax.ShapeDtypeStruct((VH, T), f32),
            jax.ShapeDtypeStruct((VH, T, T), f32),
            jax.ShapeDtypeStruct((T, x.shape[1]), bf16),
        ],
        scratch_shapes=[pltpu.VMEM((VH, T), f32)],
        compiler_params=pltpu.CompilerParams(vmem_limit_bytes=VMEM_LIMIT),
        cost_estimate=pl.CostEstimate(
            flops=4 * 10**9, bytes_accessed=14 * 2**20, transcendentals=10**6
        ),
        name="block_maps",
    )(x, gain, wk, wv, wb, wd, rate, dtb, bb)


def readers_kernel(normed_ref, wq_ref, kt_ref, yt_ref, rt_ref, rb_ref, local_ref, reader_ref):
    step = pl.program_id(0)
    rows, columns = square_iotas()
    inclusive = rows >= columns
    query_all = silu(jnp.dot(normed_ref[...], wq_ref[...], preferred_element_type=f32))
    queries = [
        unit(query_all[:, i * DK : (i + 1) * DK]) * DK ** (-0.5) for i in range(GROUP // 2)
    ]
    products = [mm(q, kt_ref[i]) for i, q in enumerate(queries)]
    scores = []
    for i in range(GROUP):
        spread = jnp.minimum(rb_ref[i] - rt_ref[pl.ds(step * GROUP + i, 1), :], 0.0)
        scores.append(jnp.where(inclusive, jnp.exp(spread) * products[i // 2], 0.0))
    for i in range(GROUP):
        both = mm_t(scores[i], yt_ref[i])
        local_ref[i] = both[:, :DV]
        reader_ref[i] = jnp.exp(rb_ref[i]) * queries[i // 2] - both[:, DV:]


def make_readers(normed, wq, kt, yt, rt, rb):
    steps = VH // GROUP
    square = pl.BlockSpec((GROUP, T, T), lambda s: (s, 0, 0))
    return pl.pallas_call(
        readers_kernel,
        grid=(steps,),
        in_specs=[
            pl.BlockSpec(normed.shape, lambda s: (0, 0)),
            pl.BlockSpec((wq.shape[0], KH * DK // steps), lambda s: (0, s)),
            pl.BlockSpec((GROUP // 2, DK, T), lambda s: (s, 0, 0)),
            pl.BlockSpec((GROUP, DK + DV, T), lambda s: (s, 0, 0)),
            pl.BlockSpec(rt.shape, lambda s: (0, 0)),
            square,
        ],
        out_specs=[square, square],
        out_shape=[jax.ShapeDtypeStruct((VH, T, T), f32)] * 2,
        compiler_params=pltpu.CompilerParams(vmem_limit_bytes=VMEM_LIMIT),
        cost_estimate=pl.CostEstimate(
            flops=2 * 10**9, bytes_accessed=8 * 2**20, transcendentals=10**6
        ),
        name="readers",
    )(normed, wq, kt, yt, rt, rb)


def on_each_core(core_ref, body):
    for core in (0, 1):

        @pl.when(core_ref[0] == core)
        def _(core=core):
            body(core)


def compose_kernel(core_ref, own_ref, other_ref, out_ref):

    def body(core):
        first, second = (own_ref, other_ref) if core == 0 else (other_ref, own_ref)
        a_rows = slice(core * HALF, core * HALF + HALF)
        b_rows = slice(DK + core * HALF, DK + core * HALF + HALF)
        for h in range(VH):
            left = jnp.concatenate([first[h, a_rows], first[h, b_rows]], axis=0)
            both = mm(left, second[h, 0:DK])
            out_ref[h, 0:HALF] = both[:HALF]
            out_ref[h, HALF : 2 * HALF] = both[HALF:] + second[h, b_rows]

    on_each_core(core_ref, body)


def scan_kernel(core_ref, map_ref, other_ref, initial_ref, out_ref):

    def body(core):
        current = initial_ref[core * HALF : core * HALF + HALF]
        count = map_ref.shape[0]
        rights = []
        for p in range(count - 1):
            halves = [map_ref[p, 0:HALF], other_ref[p]]
            rights.append(right_parts(jnp.concatenate(halves if core == 0 else halves[::-1], axis=0)))
        for p in range(count):
            out_ref[p] = current
            if p < count - 1:
                current = mm_parts(left_parts(current), rights[p]) + map_ref[p, HALF : 2 * HALF]

    on_each_core(core_ref, body)


def enter_kernel(core_ref, state_ref, own_ref, other_ref, keep_ref, send_ref):

    def body(core):
        first = own_ref if core == 0 else other_ref
        given, moved = (keep_ref, send_ref) if core == 0 else (send_ref, keep_ref)
        b_rows = slice(DK + core * HALF, DK + core * HALF + HALF)
        for h in range(VH):
            state = state_ref[h]
            given[h] = state
            moved[h] = mm(state, first[h, 0:DK]) + first[h, b_rows]

    on_each_core(core_ref, body)


def entering_of(core_ref, keep_ref, got_ref, h):
    keep, got = keep_ref[h], got_ref[h]
    first = core_ref[0] == 0
    return jnp.concatenate([jnp.where(first, keep, got), jnp.where(first, got, keep)], axis=0)


def output_kernel(
    core_ref, keep_ref, got_ref, local_ref, reader_ref, gain_ref, x_ref, wo_ref, out_ref, wo_s, sem
):
    copy = pltpu.make_async_copy(wo_ref, wo_s, sem)
    copy.start()
    heads = []
    for h in range(VH):
        entering = entering_of(core_ref, keep_ref, got_ref, h)
        core = local_ref[h] + mm_t(reader_ref[h], entering)
        mean_square = jnp.mean(core * core, axis=-1, keepdims=True)
        heads.append((core * lax.rsqrt(mean_square + 1e-06) * gain_ref[...]).astype(bf16))
    copy.wait()
    out_ref[...] = x_ref[...] + jnp.dot(
        jnp.concatenate(heads, axis=1), wo_s[...], preferred_element_type=f32
    )


def boundary_kernel(core_ref, keep_ref, got_ref, own_ref, out_ref):
    for h in range(VH):
        entering = entering_of(core_ref, keep_ref, got_ref, h)
        out_ref[h] = (mm(entering, own_ref[h, 0:DK]) + own_ref[h, DK : DK + DV]).T


def plain_call(kernel, name, outputs, flops, bytes_accessed, arguments, in_hbm=(), scratch=()):
    vmem = pl.BlockSpec(memory_space=pltpu.VMEM)
    specs = [pl.BlockSpec(memory_space=pltpu.SMEM)] + [
        pl.BlockSpec(memory_space=pl.ANY) if i in in_hbm else vmem
        for i in range(1, len(arguments))
    ]
    several = isinstance(outputs, list)
    return pl.pallas_call(
        kernel,
        in_specs=specs,
        out_specs=[vmem] * len(outputs) if several else vmem,
        out_shape=outputs,
        scratch_shapes=scratch,
        compiler_params=pltpu.CompilerParams(vmem_limit_bytes=VMEM_LIMIT),
        cost_estimate=pl.CostEstimate(
            flops=flops, bytes_accessed=bytes_accessed, transcendentals=0
        ),
        name=name,
    )(*arguments)


def on_device(
    stream,
    norm_gain,
    w_query,
    w_key,
    w_value,
    w_beta,
    w_decay,
    a_log,
    dt_bias,
    beta_bias,
    head_gain,
    w_output,
    carry_state,
):
    count = lax.axis_size("seq")
    position = lax.axis_index("seq")
    core = (position % 2).astype(jnp.int32)[None]
    chips = count // 2
    pairs = [(i, i ^ 1) for i in range(count)]
    groups = [[2 * i + c for i in range(chips)] for c in range(2)]
    x = stream[0]
    shape = lambda *dims: jax.ShapeDtypeStruct(dims, f32)

    maps, kt, yt, rt, rb, normed = make_maps(
        x, norm_gain, w_key[0], w_value[0], w_beta[0], w_decay[0], a_log, dt_bias, beta_bias
    )
    maps_other = lax.ppermute(maps, "seq", pairs)
    local, reader = make_readers(normed, w_query[0], kt, yt, rt, rb)

    chip_maps = plain_call(
        compose_kernel, "compose", shape(VH, 2 * HALF, DK), 10**9, 5 * 2**20, (core, maps, maps_other)
    )
    gathered = lax.all_to_all(chip_maps, "seq", 0, 0, axis_index_groups=groups)
    gathered_other = lax.ppermute(gathered[:, :HALF], "seq", pairs)
    initial = lax.dynamic_index_in_dim(carry_state[0], position // 2, 0, keepdims=False).T
    states = plain_call(
        scan_kernel,
        "scan_chips",
        shape(chips, HALF, DK),
        10**8,
        2 * 2**20,
        (core, gathered, gathered_other, initial),
    )
    returned = lax.all_to_all(states, "seq", 0, 0, axis_index_groups=groups)
    keep, send = plain_call(
        enter_kernel,
        "enter",
        [shape(VH, HALF, DK)] * 2,
        10**9,
        5 * 2**20,
        (core, returned, maps, maps_other),
    )
    got = lax.ppermute(send, "seq", pairs)
    rows_out = plain_call(
        output_kernel,
        "output_rows",
        shape(*x.shape),
        3 * 10**9,
        8 * 2**20,
        (core, keep, got, local, reader, head_gain, x, w_output[0]),
        in_hbm=(7,),
        scratch=[pltpu.VMEM(w_output.shape[1:], bf16), pltpu.SemaphoreType.DMA],
    )
    sections = lax.axis_size("section")
    next_rows = lax.ppermute(rows_out, "section", [(i, (i + 1) % sections) for i in range(sections)])
    boundary = plain_call(
        boundary_kernel, "boundary", shape(VH, DK, DV), 10**9, 4 * 2**20, (core, keep, got, maps)
    )
    return (next_rows[None], boundary[None, None])


def solution(mesh):
    placed = (
        P("section", "seq", None),
        P("section", None),
        P("section", None, None),
        P("section", None, None),
        P("section", None, None),
        P("section", None, None),
        P("section", None, None),
        P("section", None),
        P("section", None),
        P("section", None),
        P("section", None),
        P("section", None, None),
        P("section", None, None, None),
    )
    return jax.shard_map(
        on_device,
        mesh=mesh,
        in_specs=placed,
        out_specs=(P("section", "seq", None), P("section", "seq", None, None, None)),
        check_vma=False,
    )
```

time: 978 us -> 109 us (0.11)
  the two profiles are of different devices: /device:TPU:64 before, /device:TPU:1 now
where the time goes in v1:
time: 109 us; the launch traced here: 108 us
  blocking collectives  39.4 us (36%)
  Pallas kernels  38.9 us (36%)
  waiting for transfers between devices  15.1 us (14%)
  local copies, waits for them, and re-layouts  7.82 us (7%)
  starting transfers between devices  6.14 us (6%)
    all_to_all x1, blocking collectives, on_device(): gathered = lax.all_to_all(chip_maps, 'seq', 0, 0, axis_index_groups=groups)  24.2 us
    pallas_call x5, Pallas kernels, plain_call(): pl.pallas_call(kernel, in_specs=specs, out_specs=[vmem] * len(outputs) if...  20.8 us
    all_to_all x1, blocking collectives, on_device(): returned = lax.all_to_all(states, 'seq', 0, 0, axis_index_groups=groups)  15.2 us
    pallas_call x1, Pallas kernels, make_maps(): pl.pallas_call(maps_kernel, grid=(steps,), in_specs=[whole(x), whole(gain...  12.5 us
    ppermute x1, waiting for transfers between devices, on_device(): lax.ppermute(rows_out, 'section', [(i, (i + 1) % sections) for i in range...  10.3 us
    unnamed x13, local copies, waits for them, and re-layouts  7.06 us
    pallas_call x1, Pallas kernels, make_readers(): pl.pallas_call(readers_kernel, grid=(steps,), in_specs=[pl.BlockSpec(norm...  5.68 us
    ppermute x1, waiting for transfers between devices, on_device(): maps_other = lax.ppermute(maps, 'seq', pairs)  4 us
  transfers between devices with their start and end apart: 4, of which 3 were waited for; matrix products, arithmetic and copies ran while one was open for 1% of the time, Pallas kernels for 8%

profile of v1, /device:TPU:1, one launch (start us, length us, event | category | flops | bytes accessed | tf_op | source)
XLA Modules:
  0.0 108.1 jit_solution(2163105494564196056)
XLA Ops:
  0.6 0.0 copy-start
  0.6 1.7 %copy.15 = bf16[1,1024,16]{2,1,0:T(8,128)(2,1)} copy(bf16[1,1024,16]{1,2,0:T(8,128)(2,1)} %param.18) | data formatting | bytes 65536 | tf_op args[5]
  2.3 1.6 %copy.16 = bf16[1,1024,16]{2,1,0:T(8,128)(2,1)} copy(bf16[1,1024,16]{1,2,0:T(8,128)(2,1)} %param.19) | data formatting | bytes 65536 | tf_op args[6]
  3.9 12.5 %block_maps.1 = (f32[16,256,128]{2,1,0:T(8,128)}, f32[8,128,128]{2,1,0:T(8,128)}, f32[16,256,128]{2,1,0:T(8,128)}, f32[16,128]{1,0:T(8,128)}, f32[16,128,128]{2,1,0:T(8,128)}, /*index=5*/bf16[128,1024]{1,0:T(8,128)(2,1)}) custom-call(f32[128,1024]{1,0:T(8,128)} %bitcast.22, f32[1,1024]{1,0:T(1,128)} %gain_ref.2, bf16[1024,1024]{1,0:T(8,128)(2,1)} %bitcast.20, ...), custom_call_target="tpu_custom_call" | custom-call | flops 4000000000 | bytes 14680064 | tf_op jit(solution)/shard_map/block_maps/pallas_call | solution.py:189
  16.4 1.5 %collective-permute-start = (f32[16,256,128]{2,1,0:T(8,128)}, f32[16,256,128]{2,1,0:T(8,128)S(1)}, u32[]{:S(2)}, u32[]{:S(2)}) collective-permute-start(f32[16,256,128]{2,1,0:T(8,128)} %get-tuple-element.12.own_ref), channel_id=1, source_target_pairs={{0,1},{1,0},{2,3},{3,2},{4,5},{5,4},{6,7},{7,6},{8,9},{9,8},{10,11... | collective-permute-start | bytes 6291464 | tf_op jit(solution)/shard_map/ppermute | solution.py:402
  18.0 4.0 %collective-permute-done.other_ref = f32[16,256,128]{2,1,0:T(8,128)S(1)} collective-permute-done((f32[16,256,128]{2,1,0:T(8,128)}, f32[16,256,128]{2,1,0:T(8,128)S(1)}, u32[]{:S(2)}, u32[]{:S(2)}) %collective-permute-start) | collective-permute-done | bytes 2097184 | tf_op jit(solution)/shard_map/ppermute | solution.py:402
  21.9 0.0 copy-start.1
  21.9 1.3 %copy-done.1 = f32[16,256,128]{2,1,0:T(8,128)} copy-done((f32[16,256,128]{2,1,0:T(8,128)}, f32[16,256,128]{2,1,0:T(8,128)S(1)}, u32[]{:S(2)}) %copy-start.1) | copy-done | bytes 2097176
  23.3 3.7 %compose.1 = f32[16,128,128]{2,1,0:T(8,128)} custom-call(s32[1]{0:T(128)} %bitcast.core_ref, f32[16,256,128]{2,1,0:T(8,128)} %get-tuple-element.12.own_ref, f32[16,256,128]{2,1,0:T(8,128)} %copy-done.1), custom_call_target="tpu_custom_call" | custom-call | flops 1000000000 | bytes 5242880 | tf_op jit(solution)/shard_map/compose/pallas_call | solution.py:361
  26.9 24.2 %all_to_all.10.map_ref = f32[16,128,128]{2,1,0:T(8,128)S(1)} all-to-all(f32[16,128,128]{2,1,0:T(8,128)} %compose.1), channel_id=1, replica_groups={{0,2,4,6,8,10,12,14,16,18,20,22,24,26,28,30},{1,3,5,7,9,11,13,15,17,19,..., dimensions={0} | all-to-all | bytes 2097152 | tf_op jit(solution)/shard_map/all_to_all | solution.py:408
  51.1 0.0 copy-start.2
  51.2 1.9 %collective-permute-start.1 = (f32[16,64,128]{2,1,0:T(8,128)S(1)}, f32[16,64,128]{2,1,0:T(8,128)S(1)}, u32[]{:S(2)}, u32[]{:S(2)}) collective-permute-start(f32[16,64,128]{2,1,0:T(8,128)S(1)} %slice.4), channel_id=1, source_target_pairs={{0,1},{1,0},{2,3},{3,2},{4,5},{5,4},{6,7},{7,6},{8,9},{9,8},{10,11... | collective-permute-start | bytes 1572872 | tf_op jit(solution)/shard_map/ppermute | solution.py:409
  53.0 0.0 copy-done
  53.0 0.7 copy.17
  53.8 0.8 collective-permute-done.1.other_ref
  54.6 0.0 copy-start.3
  54.6 0.0 copy-done.2
  54.6 0.8 copy-done.3
  55.4 4.1 %scan_chips.1 = f32[16,64,128]{2,1,0:T(8,128)} custom-call(s32[1]{0:T(128)} %bitcast.core_ref, f32[16,128,128]{2,1,0:T(8,128)} %copy-done.2, f32[16,64,128]{2,1,0:T(8,128)} %copy-done.3, f32[128,128]{1,0:T(8,128)} %bitcast.15), custom_call_target="tpu_custom_call" | custom-call | flops 100000000 | bytes 2097152 | tf_op jit(solution)/shard_map/scan_chips/pallas_call | solution.py:361
  59.5 15.2 %all_to_all.11.state_ref = f32[16,64,128]{2,1,0:T(8,128)} all-to-all(f32[16,64,128]{2,1,0:T(8,128)} %scan_chips.1), channel_id=1, replica_groups={{0,2,4,6,8,10,12,14,16,18,20,22,24,26,28,30},{1,3,5,7,9,11,13,15,17,19,..., dimensions={0} | all-to-all | bytes 1048576 | tf_op jit(solution)/shard_map/all_to_all | solution.py:419
  74.7 3.9 %enter.1 = (f32[16,64,128]{2,1,0:T(8,128)}, f32[16,64,128]{2,1,0:T(8,128)}) custom-call(s32[1]{0:T(128)} %bitcast.core_ref, f32[16,64,128]{2,1,0:T(8,128)} %all_to_all.11.state_ref, f32[16,256,128]{2,1,0:T(8,128)} %get-tuple-element.12.own_ref, f32[16,256,128]{2,1,0:T(8,128)} %copy-done.1), custom_call_target="tpu_custom_call" | custom-call | flops 1000000000 | bytes 5242880 | tf_op jit(solution)/shard_map/enter/pallas_call | solution.py:361
  78.6 1.5 %collective-permute-start.2 = (f32[16,64,128]{2,1,0:T(8,128)}, f32[16,64,128]{2,1,0:T(8,128)S(1)}, u32[]{:S(2)}, u32[]{:S(2)}) collective-permute-start(f32[16,64,128]{2,1,0:T(8,128)} %get-tuple-element.14), channel_id=1, source_target_pairs={{0,1},{1,0},{2,3},{3,2},{4,5},{5,4},{6,7},{7,6},{8,9},{9,8},{10,11... | collective-permute-start | bytes 1572872 | tf_op jit(solution)/shard_map/ppermute | solution.py:428
  80.1 5.7 %readers.1 = (f32[16,128,128]{2,1,0:T(8,128)}, f32[16,128,128]{2,1,0:T(8,128)}) custom-call(bf16[128,1024]{1,0:T(8,128)(2,1)} %get-tuple-element.15.normed_ref, bf16[1024,1024]{1,0:T(8,128)(2,1)} %bitcast.21, f32[8,128,128]{2,1,0:T(8,128)} %get-tuple-element.16.kt_ref, f32[16,256,128]{2,1,0:T(8,128)} %get-tuple-element.17.yt_ref, ...), custom_call_target="tpu_custom_call" | custom-call | flops 2000000000 | bytes 8388608 | tf_op jit(solution)/shard_map/readers/pallas_call | solution.py:250
  85.8 0.0 collective-permute-done.2.got_ref
  85.8 0.0 copy-start.4
  85.8 0.8 copy-done.4
  86.6 5.7 %output_rows.1 = f32[128,1024]{1,0:T(8,128)} custom-call(s32[1]{0:T(128)} %bitcast.core_ref, f32[16,64,128]{2,1,0:T(8,128)} %get-tuple-element.13.keep_ref, f32[16,64,128]{2,1,0:T(8,128)} %copy-done.4, f32[16,128,128]{2,1,0:T(8,128)} %get-tuple-element.20.local_ref, f32[16,128,128]{2,1,0:T(8,128)} %get-tuple-element.21.reader_ref, f32[1,128]{1,0:T(1,128)} %gain_ref.3, ...), custom_call_target="tpu_custom_call" | custom-call | flops 3000000000 | bytes 8388608 | tf_op jit(solution)/shard_map/output_rows/pallas_call | solution.py:361
  92.3 1.3 %collective-permute-start.3 = (f32[128,1024]{1,0:T(8,128)}, f32[128,1024]{1,0:T(8,128)S(1)}, u32[]{:S(2)}, u32[]{:S(2)}) collective-permute-start(f32[128,1024]{1,0:T(8,128)} %output_rows.1), channel_id=1, source_target_pairs={{0,32},{32,64},{64,96},{96,0},{1,33},{33,65},{65,97},{97,1},{2,34}... | collective-permute-start | bytes 1572872 | tf_op jit(solution)/shard_map/ppermute | solution.py:440
  93.5 3.4 %boundary.1 = f32[16,128,128]{2,1,0:T(8,128)} custom-call(s32[1]{0:T(128)} %bitcast.core_ref, f32[16,64,128]{2,1,0:T(8,128)} %get-tuple-element.13.keep_ref, f32[16,64,128]{2,1,0:T(8,128)} %copy-done.4, f32[16,256,128]{2,1,0:T(8,128)} %get-tuple-element.12.own_ref), custom_call_target="tpu_custom_call" | custom-call | flops 1000000000 | bytes 4194304 | tf_op jit(solution)/shard_map/boundary/pallas_call | solution.py:361
  97.0 10.3 %collective-permute-done.3 = f32[128,1024]{1,0:T(8,128)S(1)} collective-permute-done((f32[128,1024]{1,0:T(8,128)}, f32[128,1024]{1,0:T(8,128)S(1)}, u32[]{:S(2)}, u32[]{:S(2)}) %collective-permute-start.3) | collective-permute-done | bytes 524320 | tf_op jit(solution)/shard_map/ppermute | solution.py:440
  107.3 0.8 copy.19
  (2 shorter events, 0.0 us)
Async XLA Ops:
  0.6 52.4 %copy-start = (f32[1,16,128,128]{3,2,1,0:T(8,128)S(1)}, f32[1,16,128,128]{3,2,1,0:T(8,128)}, u32[]{:S(2)}) copy-start(f32[1,16,128,128]{3,2,1,0:T(8,128)} %param.25) | copy-start | bytes 3145732
  16.4 5.5 %collective-permute-start = (f32[16,256,128]{2,1,0:T(8,128)}, f32[16,256,128]{2,1,0:T(8,128)S(1)}, u32[]{:S(2)}, u32[]{:S(2)}) collective-permute-start(f32[16,256,128]{2,1,0:T(8,128)} %get-tuple-element.12.own_ref), channel_id=1, source_target_pairs={{0,1},{1,0},{2,3},{3,2},{4,5},{5,4},{6,7},{7,6},{8,9},{9,8},{10,11... | collective-permute-start | bytes 6291464 | tf_op jit(solution)/shard_map/ppermute | solution.py:402
  21.9 1.3 %copy-start.1 = (f32[16,256,128]{2,1,0:T(8,128)}, f32[16,256,128]{2,1,0:T(8,128)S(1)}, u32[]{:S(2)}) copy-start(f32[16,256,128]{2,1,0:T(8,128)S(1)} %collective-permute-done.other_ref) | copy-start | bytes 6291460
  51.1 3.5 %copy-start.2 = (f32[16,128,128]{2,1,0:T(8,128)}, f32[16,128,128]{2,1,0:T(8,128)S(1)}, u32[]{:S(2)}) copy-start(f32[16,128,128]{2,1,0:T(8,128)S(1)} %all_to_all.10.map_ref) | copy-start | bytes 3145732
  51.2 3.4 %collective-permute-start.1 = (f32[16,64,128]{2,1,0:T(8,128)S(1)}, f32[16,64,128]{2,1,0:T(8,128)S(1)}, u32[]{:S(2)}, u32[]{:S(2)}) collective-permute-start(f32[16,64,128]{2,1,0:T(8,128)S(1)} %slice.4), channel_id=1, source_target_pairs={{0,1},{1,0},{2,3},{3,2},{4,5},{5,4},{6,7},{7,6},{8,9},{9,8},{10,11... | collective-permute-start | bytes 1572872 | tf_op jit(solution)/shard_map/ppermute | solution.py:409
  54.6 0.8 copy-start.3
  78.6 7.2 %collective-permute-start.2 = (f32[16,64,128]{2,1,0:T(8,128)}, f32[16,64,128]{2,1,0:T(8,128)S(1)}, u32[]{:S(2)}, u32[]{:S(2)}) collective-permute-start(f32[16,64,128]{2,1,0:T(8,128)} %get-tuple-element.14), channel_id=1, source_target_pairs={{0,1},{1,0},{2,3},{3,2},{4,5},{5,4},{6,7},{7,6},{8,9},{9,8},{10,11... | collective-permute-start | bytes 1572872 | tf_op jit(solution)/shard_map/ppermute | solution.py:428
  85.8 0.8 copy-start.4
  92.3 15.0 %collective-permute-start.3 = (f32[128,1024]{1,0:T(8,128)}, f32[128,1024]{1,0:T(8,128)S(1)}, u32[]{:S(2)}, u32[]{:S(2)}) collective-permute-start(f32[128,1024]{1,0:T(8,128)} %output_rows.1), channel_id=1, source_target_pairs={{0,32},{32,64},{64,96},{96,0},{1,33},{33,65},{65,97},{97,1},{2,34}... | collective-permute-start | bytes 1572872 | tf_op jit(solution)/shard_map/ppermute | solution.py:440

commit v2 on v1

v2 whole, which is shorter than its diff:
```python
import functools

import jax
import jax.numpy as jnp
from jax import lax
from jax.experimental import pallas as pl
from jax.experimental.pallas import tpu as pltpu
from jax.sharding import PartitionSpec as P

KH = 8
VH = 16
DK = 128
DV = 128
T = 128
HALF = 64
CHUNKS = 4
f32 = jnp.float32
bf16 = jnp.bfloat16
HIGHEST = lax.Precision.HIGHEST
MIB = 2**20
BATCH = 4


def parts(values):
    high = values.astype(bf16)
    return high, (values - high.astype(f32)).astype(bf16)


def left_parts(values):
    return jnp.concatenate(parts(values), axis=1)


def right_parts(values):
    both = jnp.concatenate(parts(values), axis=1)
    return jnp.concatenate([both, both], axis=0)


def right_parts_t(values):
    high, low = parts(values)
    return jnp.concatenate(
        [jnp.concatenate([high, high], axis=1), jnp.concatenate([low, low], axis=1)], axis=0
    )


def mm_parts(left, right):
    both = jnp.dot(left, right, preferred_element_type=f32)
    columns = both.shape[1] // 2
    return both[:, :columns] + both[:, columns:]


def mm(left, right):
    return mm_parts(left_parts(left), right_parts(right))


def mm_t(left, right):
    both = lax.dot_general(
        left_parts(left), right_parts_t(right), (((1,), (1,)), ((), ())), preferred_element_type=f32
    )
    columns = both.shape[1] // 2
    return both[:, :columns] + both[:, columns:]


def dot_t(left, right):
    return lax.dot_general(left, right, (((1,), (1,)), ((), ())), preferred_element_type=f32)


def sigmoid(values):
    return 1.0 / (1.0 + jnp.exp(-values))


def silu(values):
    return values * sigmoid(values)


def softplus(values):
    return jnp.maximum(values, 0.0) + jnp.log1p(jnp.exp(-jnp.abs(values)))


def unit(values):
    return values * lax.rsqrt(jnp.sum(values * values, axis=-1, keepdims=True) + 1e-06)


def square_iotas():
    rows = lax.broadcasted_iota(jnp.int32, (T, T), 0)
    columns = lax.broadcasted_iota(jnp.int32, (T, T), 1)
    return rows, columns


def upper_inverses(uppers):
    rows, columns = square_iotas()
    identity = (rows == columns).astype(f32)
    inside = (rows >> 3) == (columns >> 3)
    small = [jnp.where(inside, u, 0.0) for u in uppers]
    squares = [mm(n, n) for n in small]
    stacked = [mm(jnp.concatenate([s, n], axis=0), s) for s, n in zip(squares, small)]
    firsts = [identity - n + s - z[T:] for n, s, z in zip(small, squares, stacked)]
    result = [p + mm(p, z[:T]) for p, z in zip(firsts, stacked)]
    for shift in (3, 4, 5, 6):
        off = ((rows >> (shift + 1)) == (columns >> (shift + 1))) & (
            (rows >> shift) != (columns >> shift)
        )
        lefts = [left_parts(w) for w in result]
        rights = [right_parts(w) for w in result]
        middles = [
            mm_parts(left_parts(jnp.where(off, u, 0.0)), r) for u, r in zip(uppers, rights)
        ]
        result = [
            w - mm_parts(left, right_parts(m)) for w, left, m in zip(result, lefts, middles)
        ]
    return result


def column_of(row_ref):
    rows = lax.broadcasted_iota(jnp.int32, (VH, VH), 0)
    columns = lax.broadcasted_iota(jnp.int32, (VH, VH), 1)
    return jnp.sum(jnp.where(rows == columns, row_ref[...], 0.0), axis=1, keepdims=True)


def maps_kernel(
    core_ref,
    x_ref,
    gain_ref,
    wk_ref,
    wv_ref,
    wb_ref,
    wd_ref,
    rate_ref,
    dtb_ref,
    bb_ref,
    send_ref,
    own_ref,
    kt_ref,
    yt_ref,
    rt_ref,
    rb_ref,
    normed_ref,
):
    rows, columns = square_iotas()
    x = x_ref[...]
    mean_square = jnp.mean(x * x, axis=-1, keepdims=True)
    normed = (x * lax.rsqrt(mean_square + 1e-06) * gain_ref[...]).astype(bf16)
    normed_ref[...] = normed
    beta = sigmoid(dot_t(wb_ref[...], normed) + column_of(bb_ref))
    log_decay = -jnp.exp(column_of(rate_ref)) * softplus(
        dot_t(wd_ref[...], normed) + column_of(dtb_ref)
    )
    upper = (rows <= columns).astype(f32)
    running = jnp.dot(log_decay, upper, precision=HIGHEST, preferred_element_type=f32)
    rt_ref[...] = running
    r_rows = [running[h : h + 1] for h in range(VH)]
    b_rows = [beta[h : h + 1] for h in range(VH)]
    key_all = silu(jnp.dot(normed, wk_ref[...], preferred_element_type=f32))
    keys = [unit(key_all[:, i * DK : (i + 1) * DK]) for i in range(KH)]
    keys_t = [k.T for k in keys]
    for i, kt in enumerate(keys_t):
        kt_ref[i] = kt
    grams = [mm(k, kt) for k, kt in zip(keys, keys_t)]
    strict = rows < columns
    uppers = []
    for h in range(VH):
        r_columns = jnp.broadcast_to(r_rows[h], (T, T)).T
        rb_ref[h] = r_columns
        spread = jnp.minimum(r_rows[h] - r_columns, 0.0)
        uppers.append(jnp.where(strict, b_rows[h] * jnp.exp(spread) * grams[h // 2], 0.0))
    inverses = upper_inverses(uppers)
    value_all = silu(jnp.dot(normed, wv_ref[...], preferred_element_type=f32))
    solved = []
    for h in range(VH):
        value_t = value_all[:, h * DV : (h + 1) * DV].T
        right_t = jnp.concatenate(
            [b_rows[h] * value_t, (b_rows[h] * jnp.exp(r_rows[h])) * keys_t[h // 2]], axis=0
        )
        solved.append(mm(right_t, inverses[h]))
        yt_ref[h] = solved[h]
    key_rights = [right_parts(k) for k in keys]
    identity = rows == columns
    other_rows = pl.ds(pl.multiple_of((1 - core_ref[0]) * HALF, HALF), HALF)
    for h in range(VH):
        end = r_rows[h][:, T - 1 : T]
        both = mm_parts(left_parts(solved[h] * jnp.exp(end - r_rows[h])), key_rights[h // 2])
        own_ref[h] = both[:DV]
        send_ref[h, 0:DK] = jnp.where(identity, jnp.exp(end), 0.0) - both[DV:]
        send_ref[h, DK : DK + HALF] = own_ref[h, other_rows, :]


def make_maps(core, *arguments):
    x = arguments[0]
    vmem = pl.BlockSpec(memory_space=pltpu.VMEM)
    return pl.pallas_call(
        maps_kernel,
        in_specs=[pl.BlockSpec(memory_space=pltpu.SMEM)]
        + [vmem] * len(arguments),
        out_specs=[vmem] * 7,
        out_shape=[
            jax.ShapeDtypeStruct((VH, DK + HALF, DK), f32),
            jax.ShapeDtypeStruct((VH, DV, DK), f32),
            jax.ShapeDtypeStruct((KH, DK, T), f32),
            jax.ShapeDtypeStruct((VH, DK + DV, T), f32),
            jax.ShapeDtypeStruct((VH, T), f32),
            jax.ShapeDtypeStruct((VH, T, T), f32),
            jax.ShapeDtypeStruct((T, x.shape[1]), bf16),
        ],
        compiler_params=pltpu.CompilerParams(vmem_limit_bytes=20 * MIB),
        cost_estimate=pl.CostEstimate(
            flops=4 * 10**9, bytes_accessed=14 * 2**20, transcendentals=10**6
        ),
        name="block_maps",
    )(core, *arguments)


def readers_kernel(
    normed_ref, wq_hbm, kt_ref, yt_ref, rt_ref, rb_ref, local_ref, reader_ref, wq_s, sem
):
    copy = pltpu.make_async_copy(wq_hbm, wq_s, sem)
    copy.start()
    rows, columns = square_iotas()
    inclusive = rows >= columns
    copy.wait()
    query_all = silu(jnp.dot(normed_ref[...], wq_s[...], preferred_element_type=f32))
    for i in range(KH):
        query = unit(query_all[:, i * DK : (i + 1) * DK]) * DK ** (-0.5)
        product = mm(query, kt_ref[i])
        for h in (2 * i, 2 * i + 1):
            spread = jnp.minimum(rb_ref[h] - rt_ref[h : h + 1], 0.0)
            both = mm_t(jnp.where(inclusive, jnp.exp(spread) * product, 0.0), yt_ref[h])
            local_ref[h] = both[:, :DV]
            reader_ref[h] = jnp.exp(rb_ref[h]) * query - both[:, DV:]


def make_readers(normed, wq, *arguments):
    vmem = pl.BlockSpec(memory_space=pltpu.VMEM)
    return pl.pallas_call(
        readers_kernel,
        in_specs=[vmem, pl.BlockSpec(memory_space=pltpu.HBM)] + [vmem] * len(arguments),
        out_specs=[vmem, vmem],
        out_shape=[jax.ShapeDtypeStruct((VH, T, T), f32)] * 2,
        scratch_shapes=[pltpu.VMEM(wq.shape, wq.dtype), pltpu.SemaphoreType.DMA],
        compiler_params=pltpu.CompilerParams(vmem_limit_bytes=8 * MIB),
        cost_estimate=pl.CostEstimate(
            flops=2 * 10**9, bytes_accessed=8 * 2**20, transcendentals=10**6
        ),
        name="readers",
    )(normed, wq, *arguments)


def on_each_core(core_ref, body):
    for core in (0, 1):

        @pl.when(core_ref[0] == core)
        def _(core=core):
            body(core)


def initial_kernel(place_ref, carry_ref, out_ref):
    state = carry_ref[place_ref[0]].T

    @pl.when(place_ref[1] == 0)
    def _():
        out_ref[...] = state[:HALF]

    @pl.when(place_ref[1] == 1)
    def _():
        out_ref[...] = state[HALF:]


def compose_kernel(core_ref, sent_ref, own_ref, got_ref, out_ref):

    def body(core):
        mine = slice(core * HALF, core * HALF + HALF)
        for h in range(VH):
            own_b, got_b = own_ref[h, mine], got_ref[h, DK : DK + HALF]
            if core == 0:
                first_a, first_b, second_a, second_b = sent_ref, own_b, got_ref, got_b
            else:
                first_a, first_b, second_a, second_b = got_ref, got_b, sent_ref, own_b
            both = mm(jnp.concatenate([first_a[h, mine], first_b], axis=0), second_a[h, 0:DK])
            out_ref[h, 0:HALF] = both[:HALF]
            out_ref[h, HALF : 2 * HALF] = both[HALF:] + second_b

    on_each_core(core_ref, body)


def scan_kernel(core_ref, map_hbm, other_hbm, initial_ref, out_ref, map_ref, other_ref, sems):
    count = map_ref.shape[0]
    batches = [slice(p, p + BATCH) for p in range(0, count, BATCH)]
    copies = []
    for i, batch in enumerate(batches):
        copies.append(
            (
                pltpu.make_async_copy(map_hbm.at[batch], map_ref.at[batch], sems.at[2 * i]),
                pltpu.make_async_copy(
                    other_hbm.at[batch, 0:HALF], other_ref.at[batch], sems.at[2 * i + 1]
                ),
            )
        )
        for copy in copies[-1]:
            copy.start()

    def body(core):
        current = initial_ref[...]
        for p in range(count):
            if p % BATCH == 0:
                for copy in copies[p // BATCH]:
                    copy.wait()
            out_ref[p] = current
            if p < count - 1:
                halves = [map_ref[p, 0:HALF], other_ref[p]]
                right = jnp.concatenate(halves if core == 0 else halves[::-1], axis=0)
                current = mm(current, right) + map_ref[p, HALF : 2 * HALF]

    on_each_core(core_ref, body)


def enter_kernel(core_ref, state_ref, sent_ref, own_ref, got_ref, keep_ref, send_ref):

    def body(core):
        given, moved = (keep_ref, send_ref) if core == 0 else (send_ref, keep_ref)
        for h in range(VH):
            state = state_ref[h]
            given[h] = state
            if core == 0:
                moved[h] = mm(state, sent_ref[h, 0:DK]) + own_ref[h, 0:HALF]
            else:
                moved[h] = mm(state, got_ref[h, 0:DK]) + got_ref[h, DK : DK + HALF]

    on_each_core(core_ref, body)


def entering_of(core_ref, keep_ref, got_ref, h):
    keep, got = keep_ref[h], got_ref[h]
    first = core_ref[0] == 0
    return jnp.concatenate([jnp.where(first, keep, got), jnp.where(first, got, keep)], axis=0)


def output_kernel(
    core_ref, keep_ref, got_ref, local_ref, reader_ref, gain_ref, x_ref, wo_ref, out_ref, wo_s, sem
):
    copy = pltpu.make_async_copy(wo_ref, wo_s, sem)
    copy.start()
    heads = []
    for h in range(VH):
        entering = entering_of(core_ref, keep_ref, got_ref, h)
        core = local_ref[h] + mm_t(reader_ref[h], entering)
        mean_square = jnp.mean(core * core, axis=-1, keepdims=True)
        heads.append((core * lax.rsqrt(mean_square + 1e-06) * gain_ref[...]).astype(bf16))
    copy.wait()
    out_ref[...] = x_ref[...] + jnp.dot(
        jnp.concatenate(heads, axis=1), wo_s[...], preferred_element_type=f32
    )


def boundary_kernel(core_ref, keep_ref, got_ref, sent_ref, own_ref, out_ref):
    for h in range(VH):
        entering = entering_of(core_ref, keep_ref, got_ref, h)
        out_ref[h] = (mm(entering, sent_ref[h, 0:DK]) + own_ref[h]).T


def plain_call(kernel, name, outputs, flops, bytes_accessed, arguments, in_hbm=(), scratch=()):
    vmem = pl.BlockSpec(memory_space=pltpu.VMEM)
    specs = [pl.BlockSpec(memory_space=pltpu.SMEM)] + [
        pl.BlockSpec(memory_space=pl.ANY) if i in in_hbm else vmem
        for i in range(1, len(arguments))
    ]
    several = isinstance(outputs, list)
    return pl.pallas_call(
        kernel,
        in_specs=specs,
        out_specs=[vmem] * len(outputs) if several else vmem,
        out_shape=outputs,
        scratch_shapes=scratch,
        compiler_params=pltpu.CompilerParams(vmem_limit_bytes=6 * MIB),
        cost_estimate=pl.CostEstimate(
            flops=flops, bytes_accessed=bytes_accessed, transcendentals=0
        ),
        name=name,
    )(*arguments)


def on_device(
    stream,
    norm_gain,
    w_query,
    w_key,
    w_value,
    w_beta,
    w_decay,
    a_log,
    dt_bias,
    beta_bias,
    head_gain,
    w_output,
    carry_state,
):
    count = lax.axis_size("seq")
    position = lax.axis_index("seq")
    core = (position % 2).astype(jnp.int32)[None]
    chips = count // 2
    pairs = [(i, i ^ 1) for i in range(count)]
    groups = [[2 * i + c for i in range(chips)] for c in range(2)]
    x = stream[0]
    shape = lambda *dims: jax.ShapeDtypeStruct(dims, f32)

    place = jnp.stack([position // 2, position % 2]).astype(jnp.int32)
    initial = plain_call(
        initial_kernel, "initial_state", shape(HALF, DK), 10**11, 200 * 2**20, (place, carry_state[0])
    )
    core, initial = lax.optimization_barrier((core, initial))
    maps, drives, kt, yt, rt, rb, normed = make_maps(
        core,
        x,
        norm_gain,
        w_key[0],
        w_value[0],
        w_beta[0].T,
        w_decay[0].T,
        a_log,
        dt_bias,
        beta_bias,
    )
    maps_other = lax.ppermute(maps, "seq", pairs)
    local, reader = make_readers(normed, w_query[0], kt, yt, rt, rb)
    maps_other, local, reader = lax.optimization_barrier((maps_other, local, reader))

    chip_maps = plain_call(
        compose_kernel,
        "compose",
        shape(VH, 2 * HALF, DK),
        10**9,
        5 * 2**20,
        (core, maps, drives, maps_other),
    )
    gathered = lax.all_to_all(chip_maps, "seq", 0, 0, axis_index_groups=groups)
    gathered_other = lax.ppermute(gathered, "seq", pairs)
    states = plain_call(
        scan_kernel,
        "scan_chips",
        shape(chips, HALF, DK),
        10**8,
        30 * 2**20,
        (core, gathered, gathered_other, initial),
        in_hbm=(1, 2),
        scratch=[
            pltpu.VMEM((chips, 2 * HALF, DK), f32),
            pltpu.VMEM((chips, HALF, DK), f32),
            pltpu.SemaphoreType.DMA((2 * chips // BATCH,)),
        ],
    )
    returned = lax.all_to_all(states, "seq", 0, 0, axis_index_groups=groups)
    keep, send = plain_call(
        enter_kernel,
        "enter",
        [shape(VH, HALF, DK)] * 2,
        10**9,
        30 * 2**20,
        (core, returned, maps, drives, maps_other),
    )
    got = lax.ppermute(send, "seq", pairs)
    rows_out = plain_call(
        output_kernel,
        "output_rows",
        shape(*x.shape),
        3 * 10**9,
        8 * 2**20,
        (core, keep, got, local, reader, head_gain, x, w_output[0]),
        in_hbm=(7,),
        scratch=[pltpu.VMEM(w_output.shape[1:], bf16), pltpu.SemaphoreType.DMA],
    )
    sections = lax.axis_size("section")
    onward = [(i, (i + 1) % sections) for i in range(sections)]
    chunk = T // CHUNKS
    next_rows = jnp.concatenate(
        [lax.ppermute(rows_out[i * chunk : (i + 1) * chunk], "section", onward) for i in range(CHUNKS)]
    )
    boundary = plain_call(
        boundary_kernel, "boundary", shape(VH, DK, DV), 10**9, 4 * 2**20, (core, keep, got, maps, drives)
    )
    return (next_rows[None], boundary[None, None])


def solution(mesh):
    placed = (
        P("section", "seq", None),
        P("section", None),
        P("section", None, None),
        P("section", None, None),
        P("section", None, None),
        P("section", None, None),
        P("section", None, None),
        P("section", None),
        P("section", None),
        P("section", None),
        P("section", None),
        P("section", None, None),
        P("section", None, None, None),
    )
    return jax.shard_map(
        on_device,
        mesh=mesh,
        in_specs=placed,
        out_specs=(P("section", "seq", None), P("section", "seq", None, None, None)),
        check_vma=False,
    )
```

time: 109 us -> 82.7 us (0.76)
  Pallas kernels: 38.9 us -> 17.8 us
  local copies, waits for them, and re-layouts: 7.82 us -> 3.52 us
  starting transfers between devices: 6.14 us -> 8.74 us
  blocking collectives: 39.4 us -> 37.4 us
  waiting for transfers between devices: 15.1 us -> 13.3 us
    pallas_call x5 -> x6, Pallas kernels: 20.8 us -> 7.67 us  [plain_call(): pl.pallas_call(kernel, in_specs=specs, out_specs=[vmem] * len(outputs) if...]
    pallas_call x2, Pallas kernels: 18.2 us -> 10.2 us  [the longest x1 7.34 us: make_maps(): pl.pallas_call(maps_kernel, in_specs=[pl.BlockSpec(memory_space=pltpu.SME...]
    ppermute x1, waiting for transfers between devices: 4 us -> 0.21 us  [on_device(): maps_other = lax.ppermute(maps, 'seq', pairs)]
    unnamed x13 -> x26, local copies, waits for them, and re-layouts: 7.06 us -> 3.48 us
    ppermute x2 -> x5, starting transfers between devices: 3.13 us -> 5.39 us  [the longest x4 3.61 us: on_device(): lax.ppermute(rows_out[i * chunk:(i + 1) * chunk], 'section', onward)]
    all_to_all x1, blocking collectives: 15.2 us -> 13.4 us  [on_device(): returned = lax.all_to_all(states, 'seq', 0, 0, axis_index_groups=groups)]
    ppermute x1, waiting for transfers between devices: 0.01 us -> 1.54 us  [on_device(): got = lax.ppermute(send, 'seq', pairs)]
    ppermute x2 -> x5, waiting for transfers between devices: 11.1 us -> 11.5 us  [the longest x4 9.23 us: on_device(): lax.ppermute(rows_out[i * chunk:(i + 1) * chunk], 'section', onward)]
  transfers between devices with their start and end apart: 4 -> 7, of which waited for: 3 -> 7; matrix products, arithmetic and copies ran while one was open for 1% -> 0% of each run, Pallas kernels for 8% -> 5%
where the time goes in v2:
time: 82.7 us; the launch traced here: 82.4 us
  blocking collectives  37.4 us (45%)
  Pallas kernels  17.8 us (22%)
  waiting for transfers between devices  13.3 us (16%)
  starting transfers between devices  8.74 us (11%)
  local copies, waits for them, and re-layouts  3.52 us (4%)
  other arithmetic  0.92 us (1%)
    all_to_all x1, blocking collectives, on_device(): gathered = lax.all_to_all(chip_maps, 'seq', 0, 0, axis_index_groups=groups)  24 us
    all_to_all x1, blocking collectives, on_device(): returned = lax.all_to_all(states, 'seq', 0, 0, axis_index_groups=groups)  13.4 us
    ppermute x4, waiting for transfers between devices, on_device(): lax.ppermute(rows_out[i * chunk:(i + 1) * chunk], 'section', onward)  9.23 us
    pallas_call x6, Pallas kernels, plain_call(): pl.pallas_call(kernel, in_specs=specs, out_specs=[vmem] * len(outputs) if...  7.67 us
    pallas_call x1, Pallas kernels, make_maps(): pl.pallas_call(maps_kernel, in_specs=[pl.BlockSpec(memory_space=pltpu.SME...  7.34 us
    ppermute x4, starting transfers between devices, on_device(): lax.ppermute(rows_out[i * chunk:(i + 1) * chunk], 'section', onward)  3.61 us
    unnamed x26, local copies, waits for them, and re-layouts  3.48 us
    pallas_call x1, Pallas kernels, make_readers(): pl.pallas_call(readers_kernel, in_specs=[vmem, pl.BlockSpec(memory_space=...  2.81 us
  transfers between devices with their start and end apart: 7, of which 7 were waited for; matrix products, arithmetic and copies ran while one was open for 0% of the time, Pallas kernels for 5%

profile of v2, /device:TPU:1, one launch (start us, length us, event | category | flops | bytes accessed | tf_op | source)
XLA Modules:
  0.0 82.4 jit_solution(14409508401455654453)
XLA Ops:
  0.6 0.1 pad_add_fusion.place_ref
  0.7 1.2 %copy-done.4 = f32[1,16,128,128]{3,2,1,0:T(8,128)S(1)} copy-done((f32[1,16,128,128]{3,2,1,0:T(8,128)S(1)}, f32[1,16,128,128]{3,2,1,0:T(8,128)}, u32[]{:S(2)}) %copy-start.4) | copy-done | bytes 1048600
  2.0 0.0 copy-start.9
  2.0 0.0 copy-start.10
  2.0 0.6 initial_state.1.initial_ref
  2.7 1.5 %copy-done = bf16[1,1024,2048]{2,1,0:T(8,128)(2,1)S(1)} copy-done((bf16[1,1024,2048]{2,1,0:T(8,128)(2,1)S(1)}, bf16[1,1024,2048]{2,1,0:T(8,128)(2,1)}, u32[]{:S(2)}) %copy-start) | copy-done | bytes 4194328
  4.1 0.7 copy-done.2
  4.8 0.0 copy-done.5
  4.9 7.3 %block_maps.1 = (f32[16,192,128]{2,1,0:T(8,128)S(1)}, f32[16,128,128]{2,1,0:T(8,128)S(1)}, f32[8,128,128]{2,1,0:T(8,128)S(1)}, f32[16,256,128]{2,1,0:T(8,128)S(1...) custom-call(s32[1]{0:T(128)} %bitcast.core_ref, f32[128,1024]{1,0:T(8,128)S(1)} %bitcast.22, ...), custom_call_target="tpu_custom_call" | custom-call | flops 4000000000 | bytes 14680064 | tf_op jit(solution)/shard_map/block_maps/pallas_call | solution.py:189
  12.2 1.5 %collective-permute-start = (f32[16,192,128]{2,1,0:T(8,128)S(1)}, f32[16,192,128]{2,1,0:T(8,128)S(1)}, u32[]{:S(2)}, u32[]{:S(2)}) collective-permute-start(f32[16,192,128]{2,1,0:T(8,128)S(1)} %get-tuple-element.19.sent_ref), channel_id=1, source_target_pairs={{0,1},{1,0},{2,3},{3,2},{4,5},{5,4},{6,7},{7,6},{8,9},{9,8},{10,11... | collective-permute-start | bytes 4718600 | tf_op jit(solution)/shard_map/ppermute | solution.py:420
  13.8 2.8 %readers.1 = (f32[16,128,128]{2,1,0:T(8,128)S(1)}, f32[16,128,128]{2,1,0:T(8,128)S(1)}) custom-call(bf16[128,1024]{1,0:T(8,128)(2,1)S(1)} %get-tuple-element.21.normed_ref, bf16[1024,1024]{1,0:T(8,128)(2,1)S(1)} %bitcast.20, f32[8,128,128]{2,1,0:T(8,128)S(1)} %get-tuple-element.22.kt_ref, f32[16,256,128]{2,1,0:T(8,128)S(1)} %get-tuple-element.23.yt_ref, ...), custom_call_target="tpu_custom_call" | custom-call | flops 2000000000 | bytes 8388608 | tf_op jit(solution)/shard_map/readers/pallas_call | solution.py:232
  16.6 0.2 collective-permute-done.got_ref
  16.8 0.5 compose.1
  17.3 24.0 %all_to_all.10.map_hbm = f32[16,128,128]{2,1,0:T(8,128)S(1)} all-to-all(f32[16,128,128]{2,1,0:T(8,128)S(1)} %compose.1), channel_id=1, replica_groups={{0,2,4,6,8,10,12,14,16,18,20,22,24,26,28,30},{1,3,5,7,9,11,13,15,17,19,..., dimensions={0} | all-to-all | bytes 2097152 | tf_op jit(solution)/shard_map/all_to_all | solution.py:432
  41.3 1.8 %collective-permute-start.1 = (f32[16,128,128]{2,1,0:T(8,128)S(1)}, f32[16,128,128]{2,1,0:T(8,128)S(1)}, u32[]{:S(2)}, u32[]{:S(2)}) collective-permute-start(f32[16,128,128]{2,1,0:T(8,128)S(1)} %all_to_all.10.map_hbm), channel_id=1, source_target_pairs={{0,1},{1,0},{2,3},{3,2},{4,5},{5,4},{6,7},{7,6},{8,9},{9,8},{10,11... | collective-permute-start | bytes 3145736 | tf_op jit(solution)/shard_map/ppermute | solution.py:433
  43.0 2.3 %collective-permute-done.1.other_hbm = f32[16,128,128]{2,1,0:T(8,128)S(1)} collective-permute-done((f32[16,128,128]{2,1,0:T(8,128)S(1)}, f32[16,128,128]{2,1,0:T(8,128)S(1)}, u32[]{:S(2)}, u32[]{:S(2)}) %collective-permute-start.1) | collective-permute-done | bytes 1048608 | tf_op jit(solution)/shard_map/ppermute | solution.py:433
  45.3 2.5 %scan_chips.1 = f32[16,64,128]{2,1,0:T(8,128)S(1)} custom-call(s32[1]{0:T(128)} %bitcast.core_ref, f32[16,128,128]{2,1,0:T(8,128)S(1)} %all_to_all.10.map_hbm, f32[16,128,128]{2,1,0:T(8,128)S(1)} %collective-permute-done.1.other_hbm, f32[64,128]{1,0:T(8,128)S(1)} %initial_state.1.initial_ref), custom_call_target="tpu_custom_call" | custom-call | flops 100000000 | bytes 31457280 | tf_op jit(solution)/shard_map/scan_chips/pallas_call | solution.py:365
  47.9 13.4 %all_to_all.11.state_ref = f32[16,64,128]{2,1,0:T(8,128)S(1)} all-to-all(f32[16,64,128]{2,1,0:T(8,128)S(1)} %scan_chips.1), channel_id=1, replica_groups={{0,2,4,6,8,10,12,14,16,18,20,22,24,26,28,30},{1,3,5,7,9,11,13,15,17,19,..., dimensions={0} | all-to-all | bytes 1048576 | tf_op jit(solution)/shard_map/all_to_all | solution.py:448
  61.3 0.5 enter.1
  61.8 1.8 %collective-permute-start.2 = (f32[16,64,128]{2,1,0:T(8,128)S(1)}, f32[16,64,128]{2,1,0:T(8,128)S(1)}, u32[]{:S(2)}, u32[]{:S(2)}) collective-permute-start(f32[16,64,128]{2,1,0:T(8,128)S(1)} %get-tuple-element.31), channel_id=1, source_target_pairs={{0,1},{1,0},{2,3},{3,2},{4,5},{5,4},{6,7},{7,6},{8,9},{9,8},{10,11... | collective-permute-start | bytes 1572872 | tf_op jit(solution)/shard_map/ppermute | solution.py:457
  63.6 1.5 %collective-permute-done.2.got_ref = f32[16,64,128]{2,1,0:T(8,128)S(1)} collective-permute-done((f32[16,64,128]{2,1,0:T(8,128)S(1)}, f32[16,64,128]{2,1,0:T(8,128)S(1)}, u32[]{:S(2)}, u32[]{:S(2)}) %collective-permute-start.2) | collective-permute-done | bytes 524320 | tf_op jit(solution)/shard_map/ppermute | solution.py:457
  65.1 2.0 %output_rows.1 = f32[128,1024]{1,0:T(8,128)S(1)} custom-call(s32[1]{0:T(128)} %bitcast.core_ref, f32[16,64,128]{2,1,0:T(8,128)S(1)} %get-tuple-element.30.keep_ref, f32[16,64,128]{2,1,0:T(8,128)S(1)} %collective-permute-done.2.got_ref, f32[16,128,128]{2,1,0:T(8,128)S(1)} %get-tuple-element.32.local_ref, f32[16,128,128]{2,1,0:T(8,128)S(1)} %get-tuple-element.33.reader_ref, ...), custom_call_target="tpu_custom_call" | custom-call | flops 3000000000 | bytes 8388608 | tf_op jit(solution)/shard_map/output_rows/pallas_call | solution.py:365
  67.2 1.3 %collective-permute-start.3 = (f32[32,1024]{1,0:T(8,128)S(1)}, f32[32,1024]{1,0:T(8,128)S(1)}, u32[]{:S(2)}, u32[]{:S(2)}) collective-permute-start(f32[32,1024]{1,0:T(8,128)S(1)} %get-tuple-element.34), channel_id=1, source_target_pairs={{0,32},{32,64},{64,96},{96,0},{1,33},{33,65},{65,97},{97,1},{2,34}... | collective-permute-start | bytes 393224 | tf_op jit(solution)/shard_map/ppermute | solution.py:472
  68.5 1.2 %collective-permute-start.6 = (f32[32,1024]{1,0:T(8,128)S(1)}, f32[32,1024]{1,0:T(8,128)S(1)}, u32[]{:S(2)}, u32[]{:S(2)}) collective-permute-start(f32[32,1024]{1,0:T(8,128)S(1)} %get-tuple-element.35), channel_id=1, source_target_pairs={{0,32},{32,64},{64,96},{96,0},{1,33},{33,65},{65,97},{97,1},{2,34}... | collective-permute-start | bytes 393224 | tf_op jit(solution)/shard_map/ppermute | solution.py:472
  69.7 0.9 %collective-permute-start.5 = (f32[32,1024]{1,0:T(8,128)S(1)}, f32[32,1024]{1,0:T(8,128)S(1)}, u32[]{:S(2)}, u32[]{:S(2)}) collective-permute-start(f32[32,1024]{1,0:T(8,128)S(1)} %get-tuple-element.36), channel_id=1, source_target_pairs={{0,32},{32,64},{64,96},{96,0},{1,33},{33,65},{65,97},{97,1},{2,34}... | collective-permute-start | bytes 393224 | tf_op jit(solution)/shard_map/ppermute | solution.py:472
  70.6 0.2 collective-permute-start.4
  70.8 1.6 %boundary.1 = f32[16,128,128]{2,1,0:T(8,128)} custom-call(s32[1]{0:T(128)} %bitcast.core_ref, f32[16,64,128]{2,1,0:T(8,128)S(1)} %get-tuple-element.30.keep_ref, f32[16,64,128]{2,1,0:T(8,128)S(1)} %collective-permute-done.2.got_ref, f32[16,192,128]{2,1,0:T(8,128)S(1)} %get-tuple-element.19.sent_ref, f32[16,128,128]{2,1,0:T(8,128)S(1)} %get-tuple-element.20.own_ref), custom_call_target="tpu_custom_call" | custom-call | flops 1000000000 | bytes 4194304 | tf_op jit(solution)/shard_map/boundary/pallas_call | solution.py:365
  72.4 0.8 collective-permute-done.3
  73.2 2.8 %collective-permute-done.6 = f32[32,1024]{1,0:T(8,128)S(1)} collective-permute-done((f32[32,1024]{1,0:T(8,128)S(1)}, f32[32,1024]{1,0:T(8,128)S(1)}, u32[]{:S(2)}, u32[]{:S(2)}) %collective-permute-start.6) | collective-permute-done | bytes 131104 | tf_op jit(solution)/shard_map/ppermute | solution.py:472
  76.0 2.8 %collective-permute-done.5 = f32[32,1024]{1,0:T(8,128)S(1)} collective-permute-done((f32[32,1024]{1,0:T(8,128)S(1)}, f32[32,1024]{1,0:T(8,128)S(1)}, u32[]{:S(2)}, u32[]{:S(2)}) %collective-permute-start.5) | collective-permute-done | bytes 131104 | tf_op jit(solution)/shard_map/ppermute | solution.py:472
  78.8 2.8 %collective-permute-done.4 = f32[32,1024]{1,0:T(8,128)S(1)} collective-permute-done((f32[32,1024]{1,0:T(8,128)S(1)}, f32[32,1024]{1,0:T(8,128)S(1)}, u32[]{:S(2)}, u32[]{:S(2)}) %collective-permute-start.4) | collective-permute-done | bytes 131104 | tf_op jit(solution)/shard_map/ppermute | solution.py:472
  81.6 0.8 %maximum_bitcast_fusion = f32[1,128,1024]{2,1,0:T(8,128)} fusion(f32[32,1024]{1,0:T(8,128)S(1)} %collective-permute-done.6, f32[32,1024]{1,0:T(8,128)S(1)} %collective-permute-done.5, f32[32,1024]{1,0:T(8,128)S(1)} %collective-permute-done.4, f32[32,1024]{1,0:T(8,128)S(1)} %collective-permute-done.3), kind=kLoop, calls=%fused_computation | loop fusion | flops 393216 | bytes 1048576 | tf_op jit(solution)/shard_map/broadcast_in_dim | solution.py:477
  (21 shorter events, 0.1 us)
Async XLA Ops:
  0.7 1.2 %copy-start.4 = (f32[1,16,128,128]{3,2,1,0:T(8,128)S(1)}, f32[1,16,128,128]{3,2,1,0:T(8,128)}, u32[]{:S(2)}) copy-start(f32[1,16,128,128]{3,2,1,0:T(8,128)} %param.25) | copy-start | bytes 3145732
  1.9 2.2 %copy-start = (bf16[1,1024,2048]{2,1,0:T(8,128)(2,1)S(1)}, bf16[1,1024,2048]{2,1,0:T(8,128)(2,1)}, u32[]{:S(2)}) copy-start(bf16[1,1024,2048]{2,1,0:T(8,128)(2,1)} %param.17) | copy-start | bytes 12582916
  2.0 2.9 %copy-start.2 = (bf16[1,1024,1024]{2,1,0:T(8,128)(2,1)S(1)}, bf16[1,1024,1024]{2,1,0:T(8,128)(2,1)}, u32[]{:S(2)}) copy-start(bf16[1,1024,1024]{2,1,0:T(8,128)(2,1)} %param.16) | copy-start | bytes 6291460
  2.0 2.9 %copy-start.5 = (f32[1,128,1024]{2,1,0:T(8,128)S(1)}, f32[1,128,1024]{2,1,0:T(8,128)}, u32[]{:S(2)}) copy-start(f32[1,128,1024]{2,1,0:T(8,128)} %param.13) | copy-start | bytes 1572868
  2.0 2.9 %copy-start.6 = (bf16[1,1024,16]{1,2,0:T(8,128)(2,1)S(1)}, bf16[1,1024,16]{1,2,0:T(8,128)(2,1)}, u32[]{:S(2)}) copy-start(bf16[1,1024,16]{1,2,0:T(8,128)(2,1)} %param.18) | copy-start | bytes 98308
  2.0 2.9 %copy-start.7 = (bf16[1,1024,16]{1,2,0:T(8,128)(2,1)S(1)}, bf16[1,1024,16]{1,2,0:T(8,128)(2,1)}, u32[]{:S(2)}) copy-start(bf16[1,1024,16]{1,2,0:T(8,128)(2,1)} %param.19) | copy-start | bytes 98308
  2.0 2.9 %copy-start.8 = (f32[1,1024]{1,0:T(1,128)S(1)}, f32[1,1024]{1,0:T(1,128)}, u32[]{:S(2)}) copy-start(f32[1,1024]{1,0:T(1,128)} %gain_ref.2) | copy-start | bytes 12292
  2.0 2.9 %copy-start.9 = (f32[1,16]{1,0:T(1,128)S(1)}, f32[1,16]{1,0:T(1,128)}, u32[]{:S(2)}) copy-start(f32[1,16]{1,0:T(1,128)} %rate_ref.1) | copy-start | bytes 196
  2.0 2.9 %copy-start.10 = (f32[1,16]{1,0:T(1,128)S(1)}, f32[1,16]{1,0:T(1,128)}, u32[]{:S(2)}) copy-start(f32[1,16]{1,0:T(1,128)} %dtb_ref.1) | copy-start | bytes 196
  2.0 2.9 %copy-start.11 = (f32[1,16]{1,0:T(1,128)S(1)}, f32[1,16]{1,0:T(1,128)}, u32[]{:S(2)}) copy-start(f32[1,16]{1,0:T(1,128)} %bb_ref.1) | copy-start | bytes 196
  4.9 8.9 %copy-start.3 = (bf16[1,1024,1024]{2,1,0:T(8,128)(2,1)S(1)}, bf16[1,1024,1024]{2,1,0:T(8,128)(2,1)}, u32[]{:S(2)}) copy-start(bf16[1,1024,1024]{2,1,0:T(8,128)(2,1)} %param.15) | copy-start | bytes 6291460
  12.2 4.5 %collective-permute-start = (f32[16,192,128]{2,1,0:T(8,128)S(1)}, f32[16,192,128]{2,1,0:T(8,128)S(1)}, u32[]{:S(2)}, u32[]{:S(2)}) collective-permute-start(f32[16,192,128]{2,1,0:T(8,128)S(1)} %get-tuple-element.19.sent_ref), channel_id=1, source_target_pairs={{0,1},{1,0},{2,3},{3,2},{4,5},{5,4},{6,7},{7,6},{8,9},{9,8},{10,11... | collective-permute-start | bytes 4718600 | tf_op jit(solution)/shard_map/ppermute | solution.py:420
  41.3 4.1 %collective-permute-start.1 = (f32[16,128,128]{2,1,0:T(8,128)S(1)}, f32[16,128,128]{2,1,0:T(8,128)S(1)}, u32[]{:S(2)}, u32[]{:S(2)}) collective-permute-start(f32[16,128,128]{2,1,0:T(8,128)S(1)} %all_to_all.10.map_hbm), channel_id=1, source_target_pairs={{0,1},{1,0},{2,3},{3,2},{4,5},{5,4},{6,7},{7,6},{8,9},{9,8},{10,11... | collective-permute-start | bytes 3145736 | tf_op jit(solution)/shard_map/ppermute | solution.py:433
  61.2 3.9 %copy-start.1 = (bf16[1,2048,1024]{2,1,0:T(8,128)(2,1)S(1)}, bf16[1,2048,1024]{2,1,0:T(8,128)(2,1)}, u32[]{:S(2)}) copy-start(bf16[1,2048,1024]{2,1,0:T(8,128)(2,1)} %param.24) | copy-start | bytes 12582916
  61.2 3.9 %copy-start.12 = (f32[1,128]{1,0:T(1,128)S(1)}, f32[1,128]{1,0:T(1,128)}, u32[]{:S(2)}) copy-start(f32[1,128]{1,0:T(1,128)} %gain_ref.3) | copy-start | bytes 1540
  61.8 3.4 %collective-permute-start.2 = (f32[16,64,128]{2,1,0:T(8,128)S(1)}, f32[16,64,128]{2,1,0:T(8,128)S(1)}, u32[]{:S(2)}, u32[]{:S(2)}) collective-permute-start(f32[16,64,128]{2,1,0:T(8,128)S(1)} %get-tuple-element.31), channel_id=1, source_target_pairs={{0,1},{1,0},{2,3},{3,2},{4,5},{5,4},{6,7},{7,6},{8,9},{9,8},{10,11... | collective-permute-start | bytes 1572872 | tf_op jit(solution)/shard_map/ppermute | solution.py:457
  67.2 6.0 %collective-permute-start.3 = (f32[32,1024]{1,0:T(8,128)S(1)}, f32[32,1024]{1,0:T(8,128)S(1)}, u32[]{:S(2)}, u32[]{:S(2)}) collective-permute-start(f32[32,1024]{1,0:T(8,128)S(1)} %get-tuple-element.34), channel_id=1, source_target_pairs={{0,32},{32,64},{64,96},{96,0},{1,33},{33,65},{65,97},{97,1},{2,34}... | collective-permute-start | bytes 393224 | tf_op jit(solution)/shard_map/ppermute | solution.py:472
  68.5 7.5 %collective-permute-start.6 = (f32[32,1024]{1,0:T(8,128)S(1)}, f32[32,1024]{1,0:T(8,128)S(1)}, u32[]{:S(2)}, u32[]{:S(2)}) collective-permute-start(f32[32,1024]{1,0:T(8,128)S(1)} %get-tuple-element.35), channel_id=1, source_target_pairs={{0,32},{32,64},{64,96},{96,0},{1,33},{33,65},{65,97},{97,1},{2,34}... | collective-permute-start | bytes 393224 | tf_op jit(solution)/shard_map/ppermute | solution.py:472
  69.7 9.1 %collective-permute-start.5 = (f32[32,1024]{1,0:T(8,128)S(1)}, f32[32,1024]{1,0:T(8,128)S(1)}, u32[]{:S(2)}, u32[]{:S(2)}) collective-permute-start(f32[32,1024]{1,0:T(8,128)S(1)} %get-tuple-element.36), channel_id=1, source_target_pairs={{0,32},{32,64},{64,96},{96,0},{1,33},{33,65},{65,97},{97,1},{2,34}... | collective-permute-start | bytes 393224 | tf_op jit(solution)/shard_map/ppermute | solution.py:472
  70.6 11.0 %collective-permute-start.4 = (f32[32,1024]{1,0:T(8,128)S(1)}, f32[32,1024]{1,0:T(8,128)S(1)}, u32[]{:S(2)}, u32[]{:S(2)}) collective-permute-start(f32[32,1024]{1,0:T(8,128)S(1)} %get-tuple-element.37), channel_id=1, source_target_pairs={{0,32},{32,64},{64,96},{96,0},{1,33},{33,65},{65,97},{97,1},{2,34}... | collective-permute-start | bytes 393224 | tf_op jit(solution)/shard_map/ppermute | solution.py:472

commit v3 on v2

--- a/solution.py
+++ b/solution.py
@@ -35,13 +35,6 @@
     return jnp.concatenate([both, both], axis=0)
 
 
-def right_parts_t(values):
-    high, low = parts(values)
-    return jnp.concatenate(
-        [jnp.concatenate([high, high], axis=1), jnp.concatenate([low, low], axis=1)], axis=0
-    )
-
-
 def mm_parts(left, right):
     both = jnp.dot(left, right, preferred_element_type=f32)
     columns = both.shape[1] // 2
@@ -53,11 +46,12 @@
 
 
 def mm_t(left, right):
-    both = lax.dot_general(
-        left_parts(left), right_parts_t(right), (((1,), (1,)), ((), ())), preferred_element_type=f32
-    )
-    columns = both.shape[1] // 2
-    return both[:, :columns] + both[:, columns:]
+    high, low = parts(left)
+    right_high, right_low = parts(right)
+    return dot_t(
+        jnp.concatenate([high, low, high], axis=1),
+        jnp.concatenate([right_high, right_high, right_low], axis=1),
+    )
 
 
 def dot_t(left, right):
@@ -95,117 +89,114 @@
     stacked = [mm(jnp.concatenate([s, n], axis=0), s) for s, n in zip(squares, small)]
     firsts = [identity - n + s - z[T:] for n, s, z in zip(small, squares, stacked)]
     result = [p + mm(p, z[:T]) for p, z in zip(firsts, stacked)]
+    upper_lefts = [left_parts(u) for u in uppers]
+    rows, columns = jnp.concatenate([rows, rows], axis=1), jnp.concatenate([columns, columns], axis=1)
     for shift in (3, 4, 5, 6):
         off = ((rows >> (shift + 1)) == (columns >> (shift + 1))) & (
             (rows >> shift) != (columns >> shift)
         )
+        off = off.astype(f32).astype(bf16)
         lefts = [left_parts(w) for w in result]
         rights = [right_parts(w) for w in result]
-        middles = [
-            mm_parts(left_parts(jnp.where(off, u, 0.0)), r) for u, r in zip(uppers, rights)
-        ]
+        middles = [mm_parts(off * u, r) for u, r in zip(upper_lefts, rights)]
         result = [
             w - mm_parts(left, right_parts(m)) for w, left, m in zip(result, lefts, middles)
         ]
     return result
 
 
+def masks_kernel(core_ref, out_ref):
+    rows, columns = square_iotas()
+    out_ref[0] = (rows <= columns).astype(f32)
+    out_ref[1] = (rows == columns).astype(f32)
+
+
 def column_of(row_ref):
     rows = lax.broadcasted_iota(jnp.int32, (VH, VH), 0)
     columns = lax.broadcasted_iota(jnp.int32, (VH, VH), 1)
     return jnp.sum(jnp.where(rows == columns, row_ref[...], 0.0), axis=1, keepdims=True)
 
 
-def maps_kernel(
+def norm_kernel(
     core_ref,
+    mask_ref,
     x_ref,
     gain_ref,
-    wk_ref,
-    wv_ref,
     wb_ref,
     wd_ref,
     rate_ref,
     dtb_ref,
     bb_ref,
-    send_ref,
-    own_ref,
-    kt_ref,
-    yt_ref,
+    normed_ref,
+    bt_ref,
     rt_ref,
     rb_ref,
-    normed_ref,
-):
-    rows, columns = square_iotas()
+):
     x = x_ref[...]
     mean_square = jnp.mean(x * x, axis=-1, keepdims=True)
     normed = (x * lax.rsqrt(mean_square + 1e-06) * gain_ref[...]).astype(bf16)
     normed_ref[...] = normed
-    beta = sigmoid(dot_t(wb_ref[...], normed) + column_of(bb_ref))
+    bt_ref[...] = sigmoid(dot_t(wb_ref[...], normed) + column_of(bb_ref))
     log_decay = -jnp.exp(column_of(rate_ref)) * softplus(
         dot_t(wd_ref[...], normed) + column_of(dtb_ref)
     )
-    upper = (rows <= columns).astype(f32)
-    running = jnp.dot(log_decay, upper, precision=HIGHEST, preferred_element_type=f32)
+    running = jnp.dot(log_decay, mask_ref[0], precision=HIGHEST, preferred_element_type=f32)
     rt_ref[...] = running
-    r_rows = [running[h : h + 1] for h in range(VH)]
-    b_rows = [beta[h : h + 1] for h in range(VH)]
-    key_all = silu(jnp.dot(normed, wk_ref[...], preferred_element_type=f32))
+    for h in range(VH):
+        rb_ref[h] = jnp.broadcast_to(running[h : h + 1], (T, T)).T
+
+
+def inverses_kernel(
+    core_ref, normed_ref, bt_ref, rt_ref, rb_ref, wk_ref, keys_ref, kt_ref, inverse_ref
+):
+    rows, columns = square_iotas()
+    key_all = silu(jnp.dot(normed_ref[...], wk_ref[...], preferred_element_type=f32))
     keys = [unit(key_all[:, i * DK : (i + 1) * DK]) for i in range(KH)]
     keys_t = [k.T for k in keys]
-    for i, kt in enumerate(keys_t):
-        kt_ref[i] = kt
+    for i in range(KH):
+        keys_ref[i] = keys[i]
+        kt_ref[i] = keys_t[i]
     grams = [mm(k, kt) for k, kt in zip(keys, keys_t)]
     strict = rows < columns
     uppers = []
     for h in range(VH):
-        r_columns = jnp.broadcast_to(r_rows[h], (T, T)).T
-        rb_ref[h] = r_columns
-        spread = jnp.minimum(r_rows[h] - r_columns, 0.0)
-        uppers.append(jnp.where(strict, b_rows[h] * jnp.exp(spread) * grams[h // 2], 0.0))
-    inverses = upper_inverses(uppers)
-    value_all = silu(jnp.dot(normed, wv_ref[...], preferred_element_type=f32))
-    solved = []
-    for h in range(VH):
-        value_t = value_all[:, h * DV : (h + 1) * DV].T
-        right_t = jnp.concatenate(
-            [b_rows[h] * value_t, (b_rows[h] * jnp.exp(r_rows[h])) * keys_t[h // 2]], axis=0
-        )
-        solved.append(mm(right_t, inverses[h]))
-        yt_ref[h] = solved[h]
-    key_rights = [right_parts(k) for k in keys]
-    identity = rows == columns
+        spread = jnp.minimum(rt_ref[h : h + 1] - rb_ref[h], 0.0)
+        uppers.append(jnp.where(strict, bt_ref[h : h + 1] * jnp.exp(spread) * grams[h // 2], 0.0))
+    for h, inverse in enumerate(upper_inverses(uppers)):
+        inverse_ref[h] = inverse
+
+
+def maps_kernel(
+    core_ref,
+    mask_ref,
+    normed_ref,
+    bt_ref,
+    rt_ref,
+    wv_ref,
+    keys_ref,
+    kt_ref,
+    inverse_ref,
+    send_ref,
+    own_ref,
+    yt_ref,
+):
+    value_all = silu(jnp.dot(normed_ref[...], wv_ref[...], preferred_element_type=f32))
     other_rows = pl.ds(pl.multiple_of((1 - core_ref[0]) * HALF, HALF), HALF)
-    for h in range(VH):
-        end = r_rows[h][:, T - 1 : T]
-        both = mm_parts(left_parts(solved[h] * jnp.exp(end - r_rows[h])), key_rights[h // 2])
-        own_ref[h] = both[:DV]
-        send_ref[h, 0:DK] = jnp.where(identity, jnp.exp(end), 0.0) - both[DV:]
-        send_ref[h, DK : DK + HALF] = own_ref[h, other_rows, :]
-
-
-def make_maps(core, *arguments):
-    x = arguments[0]
-    vmem = pl.BlockSpec(memory_space=pltpu.VMEM)
-    return pl.pallas_call(
-        maps_kernel,
-        in_specs=[pl.BlockSpec(memory_space=pltpu.SMEM)]
-        + [vmem] * len(arguments),
-        out_specs=[vmem] * 7,
-        out_shape=[
-            jax.ShapeDtypeStruct((VH, DK + HALF, DK), f32),
-            jax.ShapeDtypeStruct((VH, DV, DK), f32),
-            jax.ShapeDtypeStruct((KH, DK, T), f32),
-            jax.ShapeDtypeStruct((VH, DK + DV, T), f32),
-            jax.ShapeDtypeStruct((VH, T), f32),
-            jax.ShapeDtypeStruct((VH, T, T), f32),
-            jax.ShapeDtypeStruct((T, x.shape[1]), bf16),
-        ],
-        compiler_params=pltpu.CompilerParams(vmem_limit_bytes=20 * MIB),
-        cost_estimate=pl.CostEstimate(
-            flops=4 * 10**9, bytes_accessed=14 * 2**20, transcendentals=10**6
-        ),
-        name="block_maps",
-    )(core, *arguments)
+    for i in range(KH):
+        key_right = right_parts(keys_ref[i])
+        for h in (2 * i, 2 * i + 1):
+            r_row, b_row = rt_ref[h : h + 1], bt_ref[h : h + 1]
+            value_t = value_all[:, h * DV : (h + 1) * DV].T
+            right_t = jnp.concatenate(
+                [b_row * value_t, (b_row * jnp.exp(r_row)) * kt_ref[i]], axis=0
+            )
+            solved = mm(right_t, inverse_ref[h])
+            yt_ref[h] = solved
+            end = r_row[:, T - 1 : T]
+            both = mm_parts(left_parts(solved * jnp.exp(end - r_row)), key_right)
+            own_ref[h] = both[:DV]
+            send_ref[h, 0:DK] = jnp.exp(end) * mask_ref[1] - both[DV:]
+            send_ref[h, DK : DK + HALF] = own_ref[h, other_rows, :]
 
 
 def readers_kernel(
@@ -280,28 +271,12 @@
     on_each_core(core_ref, body)
 
 
-def scan_kernel(core_ref, map_hbm, other_hbm, initial_ref, out_ref, map_ref, other_ref, sems):
-    count = map_ref.shape[0]
-    batches = [slice(p, p + BATCH) for p in range(0, count, BATCH)]
-    copies = []
-    for i, batch in enumerate(batches):
-        copies.append(
-            (
-                pltpu.make_async_copy(map_hbm.at[batch], map_ref.at[batch], sems.at[2 * i]),
-                pltpu.make_async_copy(
-                    other_hbm.at[batch, 0:HALF], other_ref.at[batch], sems.at[2 * i + 1]
-                ),
-            )
-        )
-        for copy in copies[-1]:
-            copy.start()
+def scan_kernel(core_ref, map_ref, other_ref, initial_ref, out_ref):
 
     def body(core):
         current = initial_ref[...]
+        count = map_ref.shape[0]
         for p in range(count):
-            if p % BATCH == 0:
-                for copy in copies[p // BATCH]:
-                    copy.wait()
             out_ref[p] = current
             if p < count - 1:
                 halves = [map_ref[p, 0:HALF], other_ref[p]]
@@ -355,7 +330,7 @@
         out_ref[h] = (mm(entering, sent_ref[h, 0:DK]) + own_ref[h]).T
 
 
-def plain_call(kernel, name, outputs, flops, bytes_accessed, arguments, in_hbm=(), scratch=()):
+def plain_call(kernel, name, outputs, flops, bytes_accessed, arguments, in_hbm=(), scratch=(), limit=6 * MIB):
     vmem = pl.BlockSpec(memory_space=pltpu.VMEM)
     specs = [pl.BlockSpec(memory_space=pltpu.SMEM)] + [
         pl.BlockSpec(memory_space=pl.ANY) if i in in_hbm else vmem
@@ -368,7 +343,7 @@
         out_specs=[vmem] * len(outputs) if several else vmem,
         out_shape=outputs,
         scratch_shapes=scratch,
-        compiler_params=pltpu.CompilerParams(vmem_limit_bytes=6 * MIB),
+        compiler_params=pltpu.CompilerParams(vmem_limit_bytes=limit),
         cost_estimate=pl.CostEstimate(
             flops=flops, bytes_accessed=bytes_accessed, transcendentals=0
         ),
@@ -400,22 +375,47 @@
     x = stream[0]
     shape = lambda *dims: jax.ShapeDtypeStruct(dims, f32)
 
+    masks = plain_call(masks_kernel, "masks", shape(2, T, T), 10**11, 200 * 2**20, (core,))
+    normed, bt, rt, rb = plain_call(
+        norm_kernel,
+        "norm_and_gates",
+        [jax.ShapeDtypeStruct(x.shape, bf16), shape(VH, T), shape(VH, T), shape(VH, T, T)],
+        10**9,
+        100 * 2**20,
+        (
+            core,
+            masks,
+            x,
+            norm_gain,
+            w_beta[0].T,
+            w_decay[0].T,
+            a_log,
+            dt_bias,
+            beta_bias,
+        ),
+    )
     place = jnp.stack([position // 2, position % 2]).astype(jnp.int32)
+    place, normed = lax.optimization_barrier((place, normed))
     initial = plain_call(
-        initial_kernel, "initial_state", shape(HALF, DK), 10**11, 200 * 2**20, (place, carry_state[0])
-    )
-    core, initial = lax.optimization_barrier((core, initial))
-    maps, drives, kt, yt, rt, rb, normed = make_maps(
-        core,
-        x,
-        norm_gain,
-        w_key[0],
-        w_value[0],
-        w_beta[0].T,
-        w_decay[0].T,
-        a_log,
-        dt_bias,
-        beta_bias,
+        initial_kernel, "initial_state", shape(HALF, DK), 10**6, 2**20, (place, carry_state[0])
+    )
+    keys, kt, inverses = plain_call(
+        inverses_kernel,
+        "inverses",
+        [shape(KH, T, DK), shape(KH, DK, T), shape(VH, T, T)],
+        2 * 10**9,
+        20 * 2**20,
+        (core, normed, bt, rt, rb, w_key[0]),
+        limit=20 * MIB,
+    )
+    maps, drives, yt = plain_call(
+        maps_kernel,
+        "block_maps",
+        [shape(VH, DK + HALF, DK), shape(VH, DV, DK), shape(VH, DK + DV, T)],
+        2 * 10**9,
+        10 * 2**20,
+        (core, masks, normed, bt, rt, w_value[0], keys, kt, inverses),
+        limit=10 * MIB,
     )
     maps_other = lax.ppermute(maps, "seq", pairs)
     local, reader = make_readers(normed, w_query[0], kt, yt, rt, rb)
@@ -430,7 +430,7 @@
         (core, maps, drives, maps_other),
     )
     gathered = lax.all_to_all(chip_maps, "seq", 0, 0, axis_index_groups=groups)
-    gathered_other = lax.ppermute(gathered, "seq", pairs)
+    gathered_other = lax.ppermute(gathered[:, :HALF], "seq", pairs)
     states = plain_call(
         scan_kernel,
         "scan_chips",
@@ -438,12 +438,6 @@
         10**8,
         30 * 2**20,
         (core, gathered, gathered_other, initial),
-        in_hbm=(1, 2),
-        scratch=[
-            pltpu.VMEM((chips, 2 * HALF, DK), f32),
-            pltpu.VMEM((chips, HALF, DK), f32),
-            pltpu.SemaphoreType.DMA((2 * chips // BATCH,)),
-        ],
     )
     returned = lax.all_to_all(states, "seq", 0, 0, axis_index_groups=groups)
     keep, send = plain_call(

time: 82.7 us -> 79 us (0.955)
  local copies, waits for them, and re-layouts: 3.52 us -> 0.99 us
  waiting for transfers between devices: 13.3 us -> 12.2 us
    pallas_call x1 -> x0, Pallas kernels: 7.34 us -> none  [make_maps(): pl.pallas_call(maps_kernel, in_specs=[pl.BlockSpec(memory_space=pltpu.SME...]
    pallas_call x6 -> x10, Pallas kernels: 7.67 us -> 15 us  [plain_call(): pl.pallas_call(kernel, in_specs=specs, out_specs=[vmem] * len(outputs) if...]
    unnamed x26, local copies, waits for them, and re-layouts: 3.48 us -> 0.91 us
    ppermute x1, waiting for transfers between devices: 2.29 us -> 0.9 us  [on_device(): gathered_other = lax.ppermute(gathered[:, :HALF], 'seq', pairs)]
  transfers between devices with their start and end apart: 7 -> 7, of which waited for: 7 -> 7; matrix products, arithmetic and copies ran while one was open for 0% -> 0% of each run, Pallas kernels for 5% -> 6%
where the time goes in v3:
time: 79 us; the launch traced here: 78.8 us
  blocking collectives  37.5 us (47%)
  Pallas kernels  17.5 us (22%)
  waiting for transfers between devices  12.2 us (15%)
  starting transfers between devices  8.85 us (11%)
  local copies, waits for them, and re-layouts  0.99 us (1%)
  other arithmetic  0.91 us (1%)
  between operations  0.89 us (1%)
    all_to_all x1, blocking collectives, on_device(): gathered = lax.all_to_all(chip_maps, 'seq', 0, 0, axis_index_groups=groups)  24.1 us
    pallas_call x10, Pallas kernels, plain_call(): pl.pallas_call(kernel, in_specs=specs, out_specs=[vmem] * len(outputs) if...  15 us
    all_to_all x1, blocking collectives, on_device(): returned = lax.all_to_all(states, 'seq', 0, 0, axis_index_groups=groups)  13.4 us
    ppermute x4, waiting for transfers between devices, on_device(): lax.ppermute(rows_out[i * chunk:(i + 1) * chunk], 'section', onward)  9.23 us
    ppermute x4, starting transfers between devices, on_device(): lax.ppermute(rows_out[i * chunk:(i + 1) * chunk], 'section', onward)  3.61 us
    pallas_call x1, Pallas kernels, make_readers(): pl.pallas_call(readers_kernel, in_specs=[vmem, pl.BlockSpec(memory_space=...  2.51 us
    ppermute x1, starting transfers between devices, on_device(): got = lax.ppermute(send, 'seq', pairs)  1.87 us
    ppermute x1, starting transfers between devices, on_device(): gathered_other = lax.ppermute(gathered[:, :HALF], 'seq', pairs)  1.87 us
  transfers between devices with their start and end apart: 7, of which 7 were waited for; matrix products, arithmetic and copies ran while one was open for 0% of the time, Pallas kernels for 6%

profile of v3, /device:TPU:1, one launch (start us, length us, event | category | flops | bytes accessed | tf_op | source)
XLA Modules:
  0.0 78.8 jit_solution(15181496854599148420)
XLA Ops:
  0.7 0.0 copy-start.3
  0.8 0.1 pad_add_fusion.place_ref
  0.8 0.8 %copy-done.5 = f32[1,128,1024]{2,1,0:T(8,128)S(1)} copy-done((f32[1,128,1024]{2,1,0:T(8,128)S(1)}, f32[1,128,1024]{2,1,0:T(8,128)}, u32[]{:S(2)}) %copy-start.5) | copy-done | bytes 524312
  1.7 0.9 %norm_and_gates.1 = (bf16[128,1024]{1,0:T(8,128)(2,1)S(1)}, f32[16,128]{1,0:T(8,128)S(1)}, f32[16,128]{1,0:T(8,128)S(1)}, f32[16,128,128]{2,1,0:T(8,128)S(1)}) custom-call(s32[1]{0:T(128)} %bitcast.core_ref, f32[2,128,128]{2,1,0:T(8,128)S(1)} %masks.1.mask_ref, f32[128,1024]{1,0:T(8,128)S(1)} %bitcast.22, f32[1,1024]{1,0:T(1,128)S(1)} %copy-done.8, ...), custom_call_target="tpu_custom_call" | custom-call | flops 1000000000 | bytes 104857600 | tf_op jit(solution)/shard_map/norm_and_gates/pallas_call | solution.py:340
  2.7 0.0 copy-start.1
  2.7 5.0 %inverses.1 = (f32[8,128,128]{2,1,0:T(8,128)S(1)}, f32[8,128,128]{2,1,0:T(8,128)S(1)}, f32[16,128,128]{2,1,0:T(8,128)S(1)}) custom-call(s32[1]{0:T(128)} %bitcast.core_ref, bf16[128,1024]{1,0:T(8,128)(2,1)S(1)} %get-tuple-element.22.normed_ref, f32[16,128]{1,0:T(8,128)S(1)} %get-tuple-element.23.bt_ref, f32[16,128]{1,0:T(8,128)S(1)} %get-tuple-element.24.rt_ref, ...), custom_call_target="tpu_custom_call" | custom-call | flops 2000000000 | bytes 20971520 | tf_op jit(solution)/shard_map/inverses/pallas_call | solution.py:340
  7.7 0.0 copy-start.4
  7.7 2.1 %block_maps.1 = (f32[16,192,128]{2,1,0:T(8,128)S(1)}, f32[16,128,128]{2,1,0:T(8,128)S(1)}, f32[16,256,128]{2,1,0:T(8,128)S(1)}) custom-call(s32[1]{0:T(128)} %bitcast.core_ref, f32[2,128,128]{2,1,0:T(8,128)S(1)} %masks.1.mask_ref, bf16[128,1024]{1,0:T(8,128)(2,1)S(1)} %get-tuple-element.22.normed_ref, f32[16,128]{1,0:T(8,128)S(1)} %get-tuple-element.23.bt_ref, ...), custom_call_target="tpu_custom_call" | custom-call | flops 2000000000 | bytes 10485760 | tf_op jit(solution)/shard_map/block_maps/pallas_call | solution.py:340
  9.8 1.5 %collective-permute-start = (f32[16,192,128]{2,1,0:T(8,128)S(1)}, f32[16,192,128]{2,1,0:T(8,128)S(1)}, u32[]{:S(2)}, u32[]{:S(2)}) collective-permute-start(f32[16,192,128]{2,1,0:T(8,128)S(1)} %get-tuple-element.29.sent_ref), channel_id=1, source_target_pairs={{0,1},{1,0},{2,3},{3,2},{4,5},{5,4},{6,7},{7,6},{8,9},{9,8},{10,11... | collective-permute-start | bytes 4718600 | tf_op jit(solution)/shard_map/ppermute | solution.py:420
  11.3 2.5 %readers.1 = (f32[16,128,128]{2,1,0:T(8,128)S(1)}, f32[16,128,128]{2,1,0:T(8,128)S(1)}) custom-call(bf16[128,1024]{1,0:T(8,128)(2,1)S(1)} %get-tuple-element.22.normed_ref, bf16[1024,1024]{1,0:T(8,128)(2,1)S(1)} %bitcast.21, f32[8,128,128]{2,1,0:T(8,128)S(1)} %get-tuple-element.27.kt_ref, f32[16,256,128]{2,1,0:T(8,128)S(1)} %get-tuple-element.31.yt_ref, ...), custom_call_target="tpu_custom_call" | custom-call | flops 2000000000 | bytes 8388608 | tf_op jit(solution)/shard_map/readers/pallas_call | solution.py:223
  13.8 0.5 collective-permute-done.got_ref
  14.4 0.5 compose.1
  14.8 24.1 %all_to_all.10.map_ref = f32[16,128,128]{2,1,0:T(8,128)S(1)} all-to-all(f32[16,128,128]{2,1,0:T(8,128)S(1)} %compose.1), channel_id=1, replica_groups={{0,2,4,6,8,10,12,14,16,18,20,22,24,26,28,30},{1,3,5,7,9,11,13,15,17,19,..., dimensions={0} | all-to-all | bytes 2097152 | tf_op jit(solution)/shard_map/all_to_all | solution.py:432
  39.0 1.9 %collective-permute-start.1 = (f32[16,64,128]{2,1,0:T(8,128)S(1)}, f32[16,64,128]{2,1,0:T(8,128)S(1)}, u32[]{:S(2)}, u32[]{:S(2)}) collective-permute-start(f32[16,64,128]{2,1,0:T(8,128)S(1)} %slice.20), channel_id=1, source_target_pairs={{0,1},{1,0},{2,3},{3,2},{4,5},{5,4},{6,7},{7,6},{8,9},{9,8},{10,11... | collective-permute-start | bytes 1572872 | tf_op jit(solution)/shard_map/ppermute | solution.py:433
  40.9 0.6 initial_state.1.initial_ref
  41.5 0.9 %collective-permute-done.1.other_ref = f32[16,64,128]{2,1,0:T(8,128)S(1)} collective-permute-done((f32[16,64,128]{2,1,0:T(8,128)S(1)}, f32[16,64,128]{2,1,0:T(8,128)S(1)}, u32[]{:S(2)}, u32[]{:S(2)}) %collective-permute-start.1) | collective-permute-done | bytes 524320 | tf_op jit(solution)/shard_map/ppermute | solution.py:433
  42.4 1.9 %scan_chips.1 = f32[16,64,128]{2,1,0:T(8,128)S(1)} custom-call(s32[1]{0:T(128)} %bitcast.core_ref, f32[16,128,128]{2,1,0:T(8,128)S(1)} %all_to_all.10.map_ref, f32[16,64,128]{2,1,0:T(8,128)S(1)} %collective-permute-done.1.other_ref, f32[64,128]{1,0:T(8,128)S(1)} %initial_state.1.initial_ref), custom_call_target="tpu_custom_call" | custom-call | flops 100000000 | bytes 31457280 | tf_op jit(solution)/shard_map/scan_chips/pallas_call | solution.py:340
  44.3 13.4 %all_to_all.11.state_ref = f32[16,64,128]{2,1,0:T(8,128)S(1)} all-to-all(f32[16,64,128]{2,1,0:T(8,128)S(1)} %scan_chips.1), channel_id=1, replica_groups={{0,2,4,6,8,10,12,14,16,18,20,22,24,26,28,30},{1,3,5,7,9,11,13,15,17,19,..., dimensions={0} | all-to-all | bytes 1048576 | tf_op jit(solution)/shard_map/all_to_all | solution.py:442
  57.6 0.5 enter.1
  58.1 1.9 %collective-permute-start.2 = (f32[16,64,128]{2,1,0:T(8,128)S(1)}, f32[16,64,128]{2,1,0:T(8,128)S(1)}, u32[]{:S(2)}, u32[]{:S(2)}) collective-permute-start(f32[16,64,128]{2,1,0:T(8,128)S(1)} %get-tuple-element.37), channel_id=1, source_target_pairs={{0,1},{1,0},{2,3},{3,2},{4,5},{5,4},{6,7},{7,6},{8,9},{9,8},{10,11... | collective-permute-start | bytes 1572872 | tf_op jit(solution)/shard_map/ppermute | solution.py:451
  60.0 1.5 %collective-permute-done.2.got_ref = f32[16,64,128]{2,1,0:T(8,128)S(1)} collective-permute-done((f32[16,64,128]{2,1,0:T(8,128)S(1)}, f32[16,64,128]{2,1,0:T(8,128)S(1)}, u32[]{:S(2)}, u32[]{:S(2)}) %collective-permute-start.2) | collective-permute-done | bytes 524320 | tf_op jit(solution)/shard_map/ppermute | solution.py:451
  61.6 1.9 %output_rows.1 = f32[128,1024]{1,0:T(8,128)S(1)} custom-call(s32[1]{0:T(128)} %bitcast.core_ref, f32[16,64,128]{2,1,0:T(8,128)S(1)} %get-tuple-element.36.keep_ref, f32[16,64,128]{2,1,0:T(8,128)S(1)} %collective-permute-done.2.got_ref, f32[16,128,128]{2,1,0:T(8,128)S(1)} %get-tuple-element.38.local_ref, f32[16,128,128]{2,1,0:T(8,128)S(1)} %get-tuple-element.39.reader_ref, ...), custom_call_target="tpu_custom_call" | custom-call | flops 3000000000 | bytes 8388608 | tf_op jit(solution)/shard_map/output_rows/pallas_call | solution.py:340
  63.5 1.3 %collective-permute-start.3 = (f32[32,1024]{1,0:T(8,128)S(1)}, f32[32,1024]{1,0:T(8,128)S(1)}, u32[]{:S(2)}, u32[]{:S(2)}) collective-permute-start(f32[32,1024]{1,0:T(8,128)S(1)} %get-tuple-element.40), channel_id=1, source_target_pairs={{0,32},{32,64},{64,96},{96,0},{1,33},{33,65},{65,97},{97,1},{2,34}... | collective-permute-start | bytes 393224 | tf_op jit(solution)/shard_map/ppermute | solution.py:466
  64.8 1.2 %collective-permute-start.4 = (f32[32,1024]{1,0:T(8,128)S(1)}, f32[32,1024]{1,0:T(8,128)S(1)}, u32[]{:S(2)}, u32[]{:S(2)}) collective-permute-start(f32[32,1024]{1,0:T(8,128)S(1)} %get-tuple-element.43), channel_id=1, source_target_pairs={{0,32},{32,64},{64,96},{96,0},{1,33},{33,65},{65,97},{97,1},{2,34}... | collective-permute-start | bytes 393224 | tf_op jit(solution)/shard_map/ppermute | solution.py:466
  66.0 0.9 %collective-permute-start.5 = (f32[32,1024]{1,0:T(8,128)S(1)}, f32[32,1024]{1,0:T(8,128)S(1)}, u32[]{:S(2)}, u32[]{:S(2)}) collective-permute-start(f32[32,1024]{1,0:T(8,128)S(1)} %get-tuple-element.42), channel_id=1, source_target_pairs={{0,32},{32,64},{64,96},{96,0},{1,33},{33,65},{65,97},{97,1},{2,34}... | collective-permute-start | bytes 393224 | tf_op jit(solution)/shard_map/ppermute | solution.py:466
  66.9 0.2 collective-permute-start.6
  67.1 1.6 %boundary.1 = f32[16,128,128]{2,1,0:T(8,128)} custom-call(s32[1]{0:T(128)} %bitcast.core_ref, f32[16,64,128]{2,1,0:T(8,128)S(1)} %get-tuple-element.36.keep_ref, f32[16,64,128]{2,1,0:T(8,128)S(1)} %collective-permute-done.2.got_ref, f32[16,192,128]{2,1,0:T(8,128)S(1)} %get-tuple-element.29.sent_ref, f32[16,128,128]{2,1,0:T(8,128)S(1)} %get-tuple-element.30.own_ref), custom_call_target="tpu_custom_call" | custom-call | flops 1000000000 | bytes 4194304 | tf_op jit(solution)/shard_map/boundary/pallas_call | solution.py:340
  68.7 0.8 %collective-permute-done.3 = f32[32,1024]{1,0:T(8,128)S(1)} collective-permute-done((f32[32,1024]{1,0:T(8,128)S(1)}, f32[32,1024]{1,0:T(8,128)S(1)}, u32[]{:S(2)}, u32[]{:S(2)}) %collective-permute-start.3) | collective-permute-done | bytes 131104 | tf_op jit(solution)/shard_map/ppermute | solution.py:466
  69.5 2.8 %collective-permute-done.4 = f32[32,1024]{1,0:T(8,128)S(1)} collective-permute-done((f32[32,1024]{1,0:T(8,128)S(1)}, f32[32,1024]{1,0:T(8,128)S(1)}, u32[]{:S(2)}, u32[]{:S(2)}) %collective-permute-start.4) | collective-permute-done | bytes 131104 | tf_op jit(solution)/shard_map/ppermute | solution.py:466
  72.3 2.8 %collective-permute-done.5 = f32[32,1024]{1,0:T(8,128)S(1)} collective-permute-done((f32[32,1024]{1,0:T(8,128)S(1)}, f32[32,1024]{1,0:T(8,128)S(1)}, u32[]{:S(2)}, u32[]{:S(2)}) %collective-permute-start.5) | collective-permute-done | bytes 131104 | tf_op jit(solution)/shard_map/ppermute | solution.py:466
  75.1 2.8 %collective-permute-done.6 = f32[32,1024]{1,0:T(8,128)S(1)} collective-permute-done((f32[32,1024]{1,0:T(8,128)S(1)}, f32[32,1024]{1,0:T(8,128)S(1)}, u32[]{:S(2)}, u32[]{:S(2)}) %collective-permute-start.6) | collective-permute-done | bytes 131104 | tf_op jit(solution)/shard_map/ppermute | solution.py:466
  77.9 0.8 %maximum_bitcast_fusion = f32[1,128,1024]{2,1,0:T(8,128)} fusion(f32[32,1024]{1,0:T(8,128)S(1)} %collective-permute-done.6, f32[32,1024]{1,0:T(8,128)S(1)} %collective-permute-done.5, f32[32,1024]{1,0:T(8,128)S(1)} %collective-permute-done.4, f32[32,1024]{1,0:T(8,128)S(1)} %collective-permute-done.3), kind=kLoop, calls=%fused_computation | loop fusion | flops 393216 | bytes 1048576 | tf_op jit(solution)/shard_map/broadcast_in_dim | solution.py:471
  (25 shorter events, 0.1 us)
Async XLA Ops:
  0.6 1.0 %copy-start.5 = (f32[1,128,1024]{2,1,0:T(8,128)S(1)}, f32[1,128,1024]{2,1,0:T(8,128)}, u32[]{:S(2)}) copy-start(f32[1,128,1024]{2,1,0:T(8,128)} %param.13) | copy-start | bytes 1572868
  0.7 1.0 %copy-start.6 = (bf16[1,1024,16]{1,2,0:T(8,128)(2,1)S(1)}, bf16[1,1024,16]{1,2,0:T(8,128)(2,1)}, u32[]{:S(2)}) copy-start(bf16[1,1024,16]{1,2,0:T(8,128)(2,1)} %param.18) | copy-start | bytes 98308
  0.7 1.0 %copy-start.7 = (bf16[1,1024,16]{1,2,0:T(8,128)(2,1)S(1)}, bf16[1,1024,16]{1,2,0:T(8,128)(2,1)}, u32[]{:S(2)}) copy-start(bf16[1,1024,16]{1,2,0:T(8,128)(2,1)} %param.19) | copy-start | bytes 98308
  0.7 1.0 %copy-start.8 = (f32[1,1024]{1,0:T(1,128)S(1)}, f32[1,1024]{1,0:T(1,128)}, u32[]{:S(2)}) copy-start(f32[1,1024]{1,0:T(1,128)} %gain_ref.2) | copy-start | bytes 12292
  0.7 1.0 %copy-start.9 = (f32[1,16]{1,0:T(1,128)S(1)}, f32[1,16]{1,0:T(1,128)}, u32[]{:S(2)}) copy-start(f32[1,16]{1,0:T(1,128)} %rate_ref.1) | copy-start | bytes 196
  0.7 1.0 %copy-start.10 = (f32[1,16]{1,0:T(1,128)S(1)}, f32[1,16]{1,0:T(1,128)}, u32[]{:S(2)}) copy-start(f32[1,16]{1,0:T(1,128)} %dtb_ref.1) | copy-start | bytes 196
  0.7 1.0 %copy-start.11 = (f32[1,16]{1,0:T(1,128)S(1)}, f32[1,16]{1,0:T(1,128)}, u32[]{:S(2)}) copy-start(f32[1,16]{1,0:T(1,128)} %bb_ref.1) | copy-start | bytes 196
  0.7 1.9 %copy-start.3 = (bf16[1,1024,1024]{2,1,0:T(8,128)(2,1)S(1)}, bf16[1,1024,1024]{2,1,0:T(8,128)(2,1)}, u32[]{:S(2)}) copy-start(bf16[1,1024,1024]{2,1,0:T(8,128)(2,1)} %param.16) | copy-start | bytes 6291460
  2.7 5.0 %copy-start.1 = (bf16[1,1024,2048]{2,1,0:T(8,128)(2,1)S(1)}, bf16[1,1024,2048]{2,1,0:T(8,128)(2,1)}, u32[]{:S(2)}) copy-start(bf16[1,1024,2048]{2,1,0:T(8,128)(2,1)} %param.17) | copy-start | bytes 12582916
  7.7 3.6 %copy-start.4 = (bf16[1,1024,1024]{2,1,0:T(8,128)(2,1)S(1)}, bf16[1,1024,1024]{2,1,0:T(8,128)(2,1)}, u32[]{:S(2)}) copy-start(bf16[1,1024,1024]{2,1,0:T(8,128)(2,1)} %param.15) | copy-start | bytes 6291460
  9.8 4.5 %collective-permute-start = (f32[16,192,128]{2,1,0:T(8,128)S(1)}, f32[16,192,128]{2,1,0:T(8,128)S(1)}, u32[]{:S(2)}, u32[]{:S(2)}) collective-permute-start(f32[16,192,128]{2,1,0:T(8,128)S(1)} %get-tuple-element.29.sent_ref), channel_id=1, source_target_pairs={{0,1},{1,0},{2,3},{3,2},{4,5},{5,4},{6,7},{7,6},{8,9},{9,8},{10,11... | collective-permute-start | bytes 4718600 | tf_op jit(solution)/shard_map/ppermute | solution.py:420
  14.8 26.0 %copy-start = (f32[1,16,128,128]{3,2,1,0:T(8,128)S(1)}, f32[1,16,128,128]{3,2,1,0:T(8,128)}, u32[]{:S(2)}) copy-start(f32[1,16,128,128]{3,2,1,0:T(8,128)} %param.25) | copy-start | bytes 3145732
  39.0 3.4 %collective-permute-start.1 = (f32[16,64,128]{2,1,0:T(8,128)S(1)}, f32[16,64,128]{2,1,0:T(8,128)S(1)}, u32[]{:S(2)}, u32[]{:S(2)}) collective-permute-start(f32[16,64,128]{2,1,0:T(8,128)S(1)} %slice.20), channel_id=1, source_target_pairs={{0,1},{1,0},{2,3},{3,2},{4,5},{5,4},{6,7},{7,6},{8,9},{9,8},{10,11... | collective-permute-start | bytes 1572872 | tf_op jit(solution)/shard_map/ppermute | solution.py:433
  57.6 3.9 %copy-start.2 = (bf16[1,2048,1024]{2,1,0:T(8,128)(2,1)S(1)}, bf16[1,2048,1024]{2,1,0:T(8,128)(2,1)}, u32[]{:S(2)}) copy-start(bf16[1,2048,1024]{2,1,0:T(8,128)(2,1)} %param.24) | copy-start | bytes 12582916
  57.6 3.9 %copy-start.12 = (f32[1,128]{1,0:T(1,128)S(1)}, f32[1,128]{1,0:T(1,128)}, u32[]{:S(2)}) copy-start(f32[1,128]{1,0:T(1,128)} %gain_ref.3) | copy-start | bytes 1540
  58.1 3.4 %collective-permute-start.2 = (f32[16,64,128]{2,1,0:T(8,128)S(1)}, f32[16,64,128]{2,1,0:T(8,128)S(1)}, u32[]{:S(2)}, u32[]{:S(2)}) collective-permute-start(f32[16,64,128]{2,1,0:T(8,128)S(1)} %get-tuple-element.37), channel_id=1, source_target_pairs={{0,1},{1,0},{2,3},{3,2},{4,5},{5,4},{6,7},{7,6},{8,9},{9,8},{10,11... | collective-permute-start | bytes 1572872 | tf_op jit(solution)/shard_map/ppermute | solution.py:451
  63.5 6.0 %collective-permute-start.3 = (f32[32,1024]{1,0:T(8,128)S(1)}, f32[32,1024]{1,0:T(8,128)S(1)}, u32[]{:S(2)}, u32[]{:S(2)}) collective-permute-start(f32[32,1024]{1,0:T(8,128)S(1)} %get-tuple-element.40), channel_id=1, source_target_pairs={{0,32},{32,64},{64,96},{96,0},{1,33},{33,65},{65,97},{97,1},{2,34}... | collective-permute-start | bytes 393224 | tf_op jit(solution)/shard_map/ppermute | solution.py:466
  64.8 7.5 %collective-permute-start.4 = (f32[32,1024]{1,0:T(8,128)S(1)}, f32[32,1024]{1,0:T(8,128)S(1)}, u32[]{:S(2)}, u32[]{:S(2)}) collective-permute-start(f32[32,1024]{1,0:T(8,128)S(1)} %get-tuple-element.43), channel_id=1, source_target_pairs={{0,32},{32,64},{64,96},{96,0},{1,33},{33,65},{65,97},{97,1},{2,34}... | collective-permute-start | bytes 393224 | tf_op jit(solution)/shard_map/ppermute | solution.py:466
  66.0 9.1 %collective-permute-start.5 = (f32[32,1024]{1,0:T(8,128)S(1)}, f32[32,1024]{1,0:T(8,128)S(1)}, u32[]{:S(2)}, u32[]{:S(2)}) collective-permute-start(f32[32,1024]{1,0:T(8,128)S(1)} %get-tuple-element.42), channel_id=1, source_target_pairs={{0,32},{32,64},{64,96},{96,0},{1,33},{33,65},{65,97},{97,1},{2,34}... | collective-permute-start | bytes 393224 | tf_op jit(solution)/shard_map/ppermute | solution.py:466
  66.9 11.0 %collective-permute-start.6 = (f32[32,1024]{1,0:T(8,128)S(1)}, f32[32,1024]{1,0:T(8,128)S(1)}, u32[]{:S(2)}, u32[]{:S(2)}) collective-permute-start(f32[32,1024]{1,0:T(8,128)S(1)} %get-tuple-element.41), channel_id=1, source_target_pairs={{0,32},{32,64},{64,96},{96,0},{1,33},{33,65},{65,97},{97,1},{2,34}... | collective-permute-start | bytes 393224 | tf_op jit(solution)/shard_map/ppermute | solution.py:466

commit v4 on v3

--- a/solution.py
+++ b/solution.py
@@ -14,6 +14,8 @@
 T = 128
 HALF = 64
 CHUNKS = 4
+PARTS = 1
+SPLIT = 2
 f32 = jnp.float32
 bf16 = jnp.bfloat16
 HIGHEST = lax.Precision.HIGHEST
@@ -167,6 +169,7 @@
 
 
 def maps_kernel(
+    part,
     core_ref,
     mask_ref,
     normed_ref,
@@ -180,40 +183,44 @@
     own_ref,
     yt_ref,
 ):
-    value_all = silu(jnp.dot(normed_ref[...], wv_ref[...], preferred_element_type=f32))
+    span = VH // SPLIT
+    columns = slice(part * span * DV, (part + 1) * span * DV)
+    value_all = silu(jnp.dot(normed_ref[...], wv_ref[:, columns], preferred_element_type=f32))
     other_rows = pl.ds(pl.multiple_of((1 - core_ref[0]) * HALF, HALF), HALF)
-    for i in range(KH):
+    for n in range(span):
+        h = part * span + n
+        i = h // 2
         key_right = right_parts(keys_ref[i])
-        for h in (2 * i, 2 * i + 1):
-            r_row, b_row = rt_ref[h : h + 1], bt_ref[h : h + 1]
-            value_t = value_all[:, h * DV : (h + 1) * DV].T
-            right_t = jnp.concatenate(
-                [b_row * value_t, (b_row * jnp.exp(r_row)) * kt_ref[i]], axis=0
-            )
-            solved = mm(right_t, inverse_ref[h])
-            yt_ref[h] = solved
-            end = r_row[:, T - 1 : T]
-            both = mm_parts(left_parts(solved * jnp.exp(end - r_row)), key_right)
-            own_ref[h] = both[:DV]
-            send_ref[h, 0:DK] = jnp.exp(end) * mask_ref[1] - both[DV:]
-            send_ref[h, DK : DK + HALF] = own_ref[h, other_rows, :]
+        r_row, b_row = rt_ref[h : h + 1], bt_ref[h : h + 1]
+        value_t = value_all[:, n * DV : (n + 1) * DV].T
+        right_t = jnp.concatenate([b_row * value_t, (b_row * jnp.exp(r_row)) * kt_ref[i]], axis=0)
+        solved = mm(right_t, inverse_ref[h])
+        yt_ref[n] = solved
+        end = r_row[:, T - 1 : T]
+        both = mm_parts(left_parts(solved * jnp.exp(end - r_row)), key_right)
+        own_ref[n] = both[:DV]
+        send_ref[n, 0:DK] = jnp.exp(end) * mask_ref[1] - both[DV:]
+        send_ref[n, DK : DK + HALF] = own_ref[n, other_rows, :]
+
+
+def of_head(refs, h):
+    span = VH // len(refs)
+    return refs[h // span].at[h % span]
 
 
 def readers_kernel(
-    normed_ref, wq_hbm, kt_ref, yt_ref, rt_ref, rb_ref, local_ref, reader_ref, wq_s, sem
+    normed_ref, wq_ref, kt_ref, rt_ref, rb_ref, *refs
 ):
-    copy = pltpu.make_async_copy(wq_hbm, wq_s, sem)
-    copy.start()
+    yt_refs, (local_ref, reader_ref) = refs[:SPLIT], refs[SPLIT:]
     rows, columns = square_iotas()
     inclusive = rows >= columns
-    copy.wait()
-    query_all = silu(jnp.dot(normed_ref[...], wq_s[...], preferred_element_type=f32))
+    query_all = silu(jnp.dot(normed_ref[...], wq_ref[...], preferred_element_type=f32))
     for i in range(KH):
         query = unit(query_all[:, i * DK : (i + 1) * DK]) * DK ** (-0.5)
         product = mm(query, kt_ref[i])
         for h in (2 * i, 2 * i + 1):
             spread = jnp.minimum(rb_ref[h] - rt_ref[h : h + 1], 0.0)
-            both = mm_t(jnp.where(inclusive, jnp.exp(spread) * product, 0.0), yt_ref[h])
+            both = mm_t(jnp.where(inclusive, jnp.exp(spread) * product, 0.0), of_head(yt_refs, h)[...])
             local_ref[h] = both[:, :DV]
             reader_ref[h] = jnp.exp(rb_ref[h]) * query - both[:, DV:]
 
@@ -222,10 +229,9 @@
     vmem = pl.BlockSpec(memory_space=pltpu.VMEM)
     return pl.pallas_call(
         readers_kernel,
-        in_specs=[vmem, pl.BlockSpec(memory_space=pltpu.HBM)] + [vmem] * len(arguments),
+        in_specs=[vmem] * (2 + len(arguments)),
         out_specs=[vmem, vmem],
         out_shape=[jax.ShapeDtypeStruct((VH, T, T), f32)] * 2,
-        scratch_shapes=[pltpu.VMEM(wq.shape, wq.dtype), pltpu.SemaphoreType.DMA],
         compiler_params=pltpu.CompilerParams(vmem_limit_bytes=8 * MIB),
         cost_estimate=pl.CostEstimate(
             flops=2 * 10**9, bytes_accessed=8 * 2**20, transcendentals=10**6
@@ -254,17 +260,20 @@
         out_ref[...] = state[HALF:]
 
 
-def compose_kernel(core_ref, sent_ref, own_ref, got_ref, out_ref):
+def compose_kernel(core_ref, *refs):
+    sent_refs, own_refs, got_refs = (refs[n * SPLIT : (n + 1) * SPLIT] for n in range(3))
+    out_ref = refs[-1]
 
     def body(core):
         mine = slice(core * HALF, core * HALF + HALF)
         for h in range(VH):
-            own_b, got_b = own_ref[h, mine], got_ref[h, DK : DK + HALF]
+            sent, own, got = (of_head(r, h) for r in (sent_refs, own_refs, got_refs))
+            own_b, got_b = own[mine], got[DK : DK + HALF]
             if core == 0:
-                first_a, first_b, second_a, second_b = sent_ref, own_b, got_ref, got_b
+                first_a, first_b, second_a, second_b = sent, own_b, got, got_b
             else:
-                first_a, first_b, second_a, second_b = got_ref, got_b, sent_ref, own_b
-            both = mm(jnp.concatenate([first_a[h, mine], first_b], axis=0), second_a[h, 0:DK])
+                first_a, first_b, second_a, second_b = got, got_b, sent, own_b
+            both = mm(jnp.concatenate([first_a[mine], first_b], axis=0), second_a[0:DK])
             out_ref[h, 0:HALF] = both[:HALF]
             out_ref[h, HALF : 2 * HALF] = both[HALF:] + second_b
 
@@ -274,29 +283,41 @@
 def scan_kernel(core_ref, map_ref, other_ref, initial_ref, out_ref):
 
     def body(core):
+        count = map_ref.shape[0]
+
+        def full(p):
+            halves = [map_ref[p, 0:HALF], other_ref[p]]
+            return jnp.concatenate(halves if core == 0 else halves[::-1], axis=0)
+
+        drive = lambda p: map_ref[p, HALF : 2 * HALF]
+        pairs = []
+        for p in range(0, count - 2, 2):
+            both = mm(jnp.concatenate([full(p), drive(p)], axis=0), full(p + 1))
+            pairs.append((both[:DK], both[DK:] + drive(p + 1)))
         current = initial_ref[...]
-        count = map_ref.shape[0]
-        for p in range(count):
+        for p in range(0, count, 2):
             out_ref[p] = current
-            if p < count - 1:
-                halves = [map_ref[p, 0:HALF], other_ref[p]]
-                right = jnp.concatenate(halves if core == 0 else halves[::-1], axis=0)
-                current = mm(current, right) + map_ref[p, HALF : 2 * HALF]
+            out_ref[p + 1] = mm(current, full(p)) + drive(p)
+            if p < count - 2:
+                current = mm(current, pairs[p // 2][0]) + pairs[p // 2][1]
 
     on_each_core(core_ref, body)
 
 
-def enter_kernel(core_ref, state_ref, sent_ref, own_ref, got_ref, keep_ref, send_ref):
+def enter_kernel(core_ref, state_ref, *refs):
+    sent_refs, own_refs, got_refs = (refs[n * SPLIT : (n + 1) * SPLIT] for n in range(3))
+    keep_ref, send_ref = refs[3 * SPLIT :]
 
     def body(core):
         given, moved = (keep_ref, send_ref) if core == 0 else (send_ref, keep_ref)
         for h in range(VH):
+            sent, own, got = (of_head(r, h) for r in (sent_refs, own_refs, got_refs))
             state = state_ref[h]
             given[h] = state
             if core == 0:
-                moved[h] = mm(state, sent_ref[h, 0:DK]) + own_ref[h, 0:HALF]
+                moved[h] = mm(state, sent[0:DK]) + own[0:HALF]
             else:
-                moved[h] = mm(state, got_ref[h, 0:DK]) + got_ref[h, DK : DK + HALF]
+                moved[h] = mm(state, got[0:DK]) + got[DK : DK + HALF]
 
     on_each_core(core_ref, body)
 
@@ -308,41 +329,37 @@
 
 
 def output_kernel(
-    core_ref, keep_ref, got_ref, local_ref, reader_ref, gain_ref, x_ref, wo_ref, out_ref, wo_s, sem
+    part, core_ref, keep_ref, got_ref, local_ref, reader_ref, gain_ref, x_ref, wo_ref, out_ref
 ):
-    copy = pltpu.make_async_copy(wo_ref, wo_s, sem)
-    copy.start()
+    rows = slice(part * T // PARTS, (part + 1) * T // PARTS)
     heads = []
     for h in range(VH):
         entering = entering_of(core_ref, keep_ref, got_ref, h)
-        core = local_ref[h] + mm_t(reader_ref[h], entering)
+        core = local_ref[h, rows] + mm_t(reader_ref[h, rows], entering)
         mean_square = jnp.mean(core * core, axis=-1, keepdims=True)
         heads.append((core * lax.rsqrt(mean_square + 1e-06) * gain_ref[...]).astype(bf16))
-    copy.wait()
-    out_ref[...] = x_ref[...] + jnp.dot(
-        jnp.concatenate(heads, axis=1), wo_s[...], preferred_element_type=f32
-    )
-
-
-def boundary_kernel(core_ref, keep_ref, got_ref, sent_ref, own_ref, out_ref):
+    out_ref[...] = x_ref[rows] + jnp.dot(
+        jnp.concatenate(heads, axis=1), wo_ref[...], preferred_element_type=f32
+    )
+
+
+def boundary_kernel(core_ref, keep_ref, got_ref, *refs):
+    sent_refs, own_refs, out_ref = refs[:SPLIT], refs[SPLIT : 2 * SPLIT], refs[-1]
     for h in range(VH):
         entering = entering_of(core_ref, keep_ref, got_ref, h)
-        out_ref[h] = (mm(entering, sent_ref[h, 0:DK]) + own_ref[h]).T
-
-
-def plain_call(kernel, name, outputs, flops, bytes_accessed, arguments, in_hbm=(), scratch=(), limit=6 * MIB):
+        sent, own = of_head(sent_refs, h), of_head(own_refs, h)
+        out_ref[h] = (mm(entering, sent[0:DK]) + own[...]).T
+
+
+def plain_call(kernel, name, outputs, flops, bytes_accessed, arguments, limit=6 * MIB):
     vmem = pl.BlockSpec(memory_space=pltpu.VMEM)
-    specs = [pl.BlockSpec(memory_space=pltpu.SMEM)] + [
-        pl.BlockSpec(memory_space=pl.ANY) if i in in_hbm else vmem
-        for i in range(1, len(arguments))
-    ]
+    specs = [pl.BlockSpec(memory_space=pltpu.SMEM)] + [vmem] * (len(arguments) - 1)
     several = isinstance(outputs, list)
     return pl.pallas_call(
         kernel,
         in_specs=specs,
         out_specs=[vmem] * len(outputs) if several else vmem,
         out_shape=outputs,
-        scratch_shapes=scratch,
         compiler_params=pltpu.CompilerParams(vmem_limit_bytes=limit),
         cost_estimate=pl.CostEstimate(
             flops=flops, bytes_accessed=bytes_accessed, transcendentals=0
@@ -408,17 +425,23 @@
         (core, normed, bt, rt, rb, w_key[0]),
         limit=20 * MIB,
     )
-    maps, drives, yt = plain_call(
-        maps_kernel,
-        "block_maps",
-        [shape(VH, DK + HALF, DK), shape(VH, DV, DK), shape(VH, DK + DV, T)],
-        2 * 10**9,
-        10 * 2**20,
-        (core, masks, normed, bt, rt, w_value[0], keys, kt, inverses),
-        limit=10 * MIB,
-    )
-    maps_other = lax.ppermute(maps, "seq", pairs)
-    local, reader = make_readers(normed, w_query[0], kt, yt, rt, rb)
+    span = VH // SPLIT
+    maps, drives, solved, maps_other = [], [], [], []
+    for part in range(SPLIT):
+        sent, own, yt = plain_call(
+            functools.partial(maps_kernel, part),
+            "block_maps",
+            [shape(span, DK + HALF, DK), shape(span, DV, DK), shape(span, DK + DV, T)],
+            2 * 10**9,
+            10 * 2**20,
+            (core, masks, normed, bt, rt, w_value[0], keys, kt, inverses),
+            limit=10 * MIB,
+        )
+        maps.append(sent)
+        drives.append(own)
+        solved.append(yt)
+        maps_other.append(lax.ppermute(sent, "seq", pairs))
+    local, reader = make_readers(normed, w_query[0], kt, rt, rb, *solved)
     maps_other, local, reader = lax.optimization_barrier((maps_other, local, reader))
 
     chip_maps = plain_call(
@@ -427,7 +450,7 @@
         shape(VH, 2 * HALF, DK),
         10**9,
         5 * 2**20,
-        (core, maps, drives, maps_other),
+        (core, *maps, *drives, *maps_other),
     )
     gathered = lax.all_to_all(chip_maps, "seq", 0, 0, axis_index_groups=groups)
     gathered_other = lax.ppermute(gathered[:, :HALF], "seq", pairs)
@@ -446,27 +469,27 @@
         [shape(VH, HALF, DK)] * 2,
         10**9,
         30 * 2**20,
-        (core, returned, maps, drives, maps_other),
+        (core, returned, *maps, *drives, *maps_other),
     )
     got = lax.ppermute(send, "seq", pairs)
-    rows_out = plain_call(
-        output_kernel,
-        "output_rows",
-        shape(*x.shape),
-        3 * 10**9,
-        8 * 2**20,
-        (core, keep, got, local, reader, head_gain, x, w_output[0]),
-        in_hbm=(7,),
-        scratch=[pltpu.VMEM(w_output.shape[1:], bf16), pltpu.SemaphoreType.DMA],
-    )
     sections = lax.axis_size("section")
     onward = [(i, (i + 1) % sections) for i in range(sections)]
     chunk = T // CHUNKS
-    next_rows = jnp.concatenate(
-        [lax.ppermute(rows_out[i * chunk : (i + 1) * chunk], "section", onward) for i in range(CHUNKS)]
-    )
+    arrived = []
+    for part in range(PARTS):
+        rows_out = plain_call(
+            functools.partial(output_kernel, part),
+            "output_rows",
+            shape(T // PARTS, x.shape[1]),
+            10**9,
+            8 * 2**20,
+            (core, keep, got, local, reader, head_gain, x, w_output[0]),
+        )
+        for i in range(0, T // PARTS, chunk):
+            arrived.append(lax.ppermute(rows_out[i : i + chunk], "section", onward))
+    next_rows = jnp.concatenate(arrived)
     boundary = plain_call(
-        boundary_kernel, "boundary", shape(VH, DK, DV), 10**9, 4 * 2**20, (core, keep, got, maps, drives)
+        boundary_kernel, "boundary", shape(VH, DK, DV), 10**9, 4 * 2**20, (core, keep, got, *maps, *drives)
     )
     return (next_rows[None], boundary[None, None])
 

time: 79 us -> 77.7 us (0.984)
  Pallas kernels: 17.5 us -> 16.6 us
    pallas_call x10 -> x11, Pallas kernels: 15 us -> 14.2 us  [plain_call(): pl.pallas_call(kernel, in_specs=specs, out_specs=[vmem] * len(outputs) if...]
    ppermute x5 -> x6, waiting for transfers between devices: 9.75 us -> 9.27 us  [the longest x4 9.26 us: on_device(): arrived.append(lax.ppermute(rows_out[i:i + chunk], 'section', onward))]
    ppermute x5 -> x6, starting transfers between devices: 5.11 us -> 5.21 us  [the longest x4 3.61 us: on_device(): arrived.append(lax.ppermute(rows_out[i:i + chunk], 'section', onward))]
  transfers between devices with their start and end apart: 7 -> 8, of which waited for: 7 -> 6; matrix products, arithmetic and copies ran while one was open for 0% -> 0% of each run, Pallas kernels for 6% -> 7%
where the time goes in v4:
time: 77.7 us; the launch traced here: 77.5 us
  blocking collectives  37.2 us (48%)
  Pallas kernels  16.6 us (21%)
  waiting for transfers between devices  11.7 us (15%)
  starting transfers between devices  9.25 us (12%)
  local copies, waits for them, and re-layouts  0.99 us (1%)
  between operations  0.92 us (1%)
  other arithmetic  0.91 us (1%)
    all_to_all x1, blocking collectives, on_device(): gathered = lax.all_to_all(chip_maps, 'seq', 0, 0, axis_index_groups=groups)  23.8 us
    pallas_call x11, Pallas kernels, plain_call(): pl.pallas_call(kernel, in_specs=specs, out_specs=[vmem] * len(outputs) if...  14.2 us
    all_to_all x1, blocking collectives, on_device(): returned = lax.all_to_all(states, 'seq', 0, 0, axis_index_groups=groups)  13.4 us
    ppermute x4, waiting for transfers between devices, on_device(): arrived.append(lax.ppermute(rows_out[i:i + chunk], 'section', onward))  9.26 us
    ppermute x4, starting transfers between devices, on_device(): arrived.append(lax.ppermute(rows_out[i:i + chunk], 'section', onward))  3.61 us
    pallas_call x1, Pallas kernels, make_readers(): pl.pallas_call(readers_kernel, in_specs=[vmem] * (2 + len(arguments)), ou...  2.33 us
    ppermute x1, starting transfers between devices, on_device(): gathered_other = lax.ppermute(gathered[:, :HALF], 'seq', pairs)  2.17 us
    ppermute x1, starting transfers between devices, on_device(): got = lax.ppermute(send, 'seq', pairs)  1.87 us
  transfers between devices with their start and end apart: 8, of which 6 were waited for; matrix products, arithmetic and copies ran while one was open for 0% of the time, Pallas kernels for 7%

profile of v4, /device:TPU:1, one launch (start us, length us, event | category | flops | bytes accessed | tf_op | source)
XLA Modules:
  0.0 77.5 jit_solution(10134627053679795875)
XLA Ops:
  0.8 0.1 pad_add_fusion.place_ref
  0.8 0.8 %copy-done.2 = f32[1,128,1024]{2,1,0:T(8,128)S(1)} copy-done((f32[1,128,1024]{2,1,0:T(8,128)S(1)}, f32[1,128,1024]{2,1,0:T(8,128)}, u32[]{:S(2)}) %copy-start.2) | copy-done | bytes 524312
  1.7 0.9 %norm_and_gates.1 = (bf16[128,1024]{1,0:T(8,128)(2,1)S(1)}, f32[16,128]{1,0:T(8,128)S(1)}, f32[16,128]{1,0:T(8,128)S(1)}, f32[16,128,128]{2,1,0:T(8,128)S(1)}) custom-call(s32[1]{0:T(128)} %bitcast.core_ref, f32[2,128,128]{2,1,0:T(8,128)S(1)} %masks.1.mask_ref, f32[128,1024]{1,0:T(8,128)S(1)} %bitcast.19, f32[1,1024]{1,0:T(1,128)S(1)} %copy-done.9, ...), custom_call_target="tpu_custom_call" | custom-call | flops 1000000000 | bytes 104857600 | tf_op jit(solution)/shard_map/norm_and_gates/pallas_call | solution.py:358
  2.7 5.0 %inverses.1 = (f32[8,128,128]{2,1,0:T(8,128)S(1)}, f32[8,128,128]{2,1,0:T(8,128)S(1)}, f32[16,128,128]{2,1,0:T(8,128)S(1)}) custom-call(s32[1]{0:T(128)} %bitcast.core_ref, bf16[128,1024]{1,0:T(8,128)(2,1)S(1)} %get-tuple-element.26.normed_ref, f32[16,128]{1,0:T(8,128)S(1)} %get-tuple-element.27.bt_ref, f32[16,128]{1,0:T(8,128)S(1)} %get-tuple-element.28.rt_ref, ...), custom_call_target="tpu_custom_call" | custom-call | flops 2000000000 | bytes 20971520 | tf_op jit(solution)/shard_map/inverses/pallas_call | solution.py:358
  7.7 1.2 %block_maps.3 = (f32[8,192,128]{2,1,0:T(8,128)S(1)}, f32[8,128,128]{2,1,0:T(8,128)S(1)}, f32[8,256,128]{2,1,0:T(8,128)S(1)}) custom-call(s32[1]{0:T(128)} %bitcast.core_ref, f32[2,128,128]{2,1,0:T(8,128)S(1)} %masks.1.mask_ref, bf16[128,1024]{1,0:T(8,128)(2,1)S(1)} %get-tuple-element.26.normed_ref, f32[16,128]{1,0:T(8,128)S(1)} %get-tuple-element.27.bt_ref, ...), custom_call_target="tpu_custom_call" | custom-call | flops 2000000000 | bytes 10485760 | tf_op jit(solution)/shard_map/block_maps/pallas_call | solution.py:358
  8.9 0.0 copy-start.6
  8.9 1.5 %collective-permute-start.1 = (f32[8,192,128]{2,1,0:T(8,128)S(1)}, f32[8,192,128]{2,1,0:T(8,128)S(1)}, u32[]{:S(2)}, u32[]{:S(2)}) collective-permute-start(f32[8,192,128]{2,1,0:T(8,128)S(1)} %get-tuple-element.34.refs_1_), channel_id=1, source_target_pairs={{0,1},{1,0},{2,3},{3,2},{4,5},{5,4},{6,7},{7,6},{8,9},{9,8},{10,11... | collective-permute-start | bytes 2359304 | tf_op jit(solution)/shard_map/ppermute | solution.py:443
  10.4 1.2 %block_maps.2 = (f32[8,192,128]{2,1,0:T(8,128)S(1)}, f32[8,128,128]{2,1,0:T(8,128)S(1)}, f32[8,256,128]{2,1,0:T(8,128)S(1)}) custom-call(s32[1]{0:T(128)} %bitcast.core_ref, f32[2,128,128]{2,1,0:T(8,128)S(1)} %masks.1.mask_ref, bf16[128,1024]{1,0:T(8,128)(2,1)S(1)} %get-tuple-element.26.normed_ref, f32[16,128]{1,0:T(8,128)S(1)} %get-tuple-element.27.bt_ref, ...), custom_call_target="tpu_custom_call" | custom-call | flops 2000000000 | bytes 10485760 | tf_op jit(solution)/shard_map/block_maps/pallas_call | solution.py:358
  11.7 0.1 collective-permute-start
  11.8 2.3 %readers.1 = (f32[16,128,128]{2,1,0:T(8,128)S(1)}, f32[16,128,128]{2,1,0:T(8,128)S(1)}) custom-call(bf16[128,1024]{1,0:T(8,128)(2,1)S(1)} %get-tuple-element.26.normed_ref, bf16[1024,1024]{1,0:T(8,128)(2,1)S(1)} %bitcast.24, f32[8,128,128]{2,1,0:T(8,128)S(1)} %get-tuple-element.31.kt_ref, f32[16,128]{1,0:T(8,128)S(1)} %get-tuple-element.28.rt_ref, ...), custom_call_target="tpu_custom_call" | custom-call | flops 2000000000 | bytes 8388608 | tf_op jit(solution)/shard_map/readers/pallas_call | solution.py:230
  14.1 0.5 compose.1
  14.6 23.8 %all_to_all.10.map_ref = f32[16,128,128]{2,1,0:T(8,128)S(1)} all-to-all(f32[16,128,128]{2,1,0:T(8,128)S(1)} %compose.1), channel_id=1, replica_groups={{0,2,4,6,8,10,12,14,16,18,20,22,24,26,28,30},{1,3,5,7,9,11,13,15,17,19,..., dimensions={0} | all-to-all | bytes 2097152 | tf_op jit(solution)/shard_map/all_to_all | solution.py:455
  38.5 2.2 %collective-permute-start.2 = (f32[16,64,128]{2,1,0:T(8,128)S(1)}, f32[16,64,128]{2,1,0:T(8,128)S(1)}, u32[]{:S(2)}, u32[]{:S(2)}) collective-permute-start(f32[16,64,128]{2,1,0:T(8,128)S(1)} %slice.20), channel_id=1, source_target_pairs={{0,1},{1,0},{2,3},{3,2},{4,5},{5,4},{6,7},{7,6},{8,9},{9,8},{10,11... | collective-permute-start | bytes 1572872 | tf_op jit(solution)/shard_map/ppermute | solution.py:456
  40.7 0.6 initial_state.1.initial_ref
  41.3 0.0 copy-start.3
  41.4 0.9 %collective-permute-done.2.other_ref = f32[16,64,128]{2,1,0:T(8,128)S(1)} collective-permute-done((f32[16,64,128]{2,1,0:T(8,128)S(1)}, f32[16,64,128]{2,1,0:T(8,128)S(1)}, u32[]{:S(2)}, u32[]{:S(2)}) %collective-permute-start.2) | collective-permute-done | bytes 524320 | tf_op jit(solution)/shard_map/ppermute | solution.py:456
  42.2 1.3 %scan_chips.1 = f32[16,64,128]{2,1,0:T(8,128)S(1)} custom-call(s32[1]{0:T(128)} %bitcast.core_ref, f32[16,128,128]{2,1,0:T(8,128)S(1)} %all_to_all.10.map_ref, f32[16,64,128]{2,1,0:T(8,128)S(1)} %collective-permute-done.2.other_ref, f32[64,128]{1,0:T(8,128)S(1)} %initial_state.1.initial_ref), custom_call_target="tpu_custom_call" | custom-call | flops 100000000 | bytes 31457280 | tf_op jit(solution)/shard_map/scan_chips/pallas_call | solution.py:358
  43.5 13.4 %all_to_all.11.state_ref = f32[16,64,128]{2,1,0:T(8,128)S(1)} all-to-all(f32[16,64,128]{2,1,0:T(8,128)S(1)} %scan_chips.1), channel_id=1, replica_groups={{0,2,4,6,8,10,12,14,16,18,20,22,24,26,28,30},{1,3,5,7,9,11,13,15,17,19,..., dimensions={0} | all-to-all | bytes 1048576 | tf_op jit(solution)/shard_map/all_to_all | solution.py:465
  56.9 0.5 enter.1
  57.4 1.9 %collective-permute-start.3 = (f32[16,64,128]{2,1,0:T(8,128)S(1)}, f32[16,64,128]{2,1,0:T(8,128)S(1)}, u32[]{:S(2)}, u32[]{:S(2)}) collective-permute-start(f32[16,64,128]{2,1,0:T(8,128)S(1)} %get-tuple-element.45), channel_id=1, source_target_pairs={{0,1},{1,0},{2,3},{3,2},{4,5},{5,4},{6,7},{7,6},{8,9},{9,8},{10,11... | collective-permute-start | bytes 1572872 | tf_op jit(solution)/shard_map/ppermute | solution.py:474
  59.3 1.5 %collective-permute-done.3.got_ref = f32[16,64,128]{2,1,0:T(8,128)S(1)} collective-permute-done((f32[16,64,128]{2,1,0:T(8,128)S(1)}, f32[16,64,128]{2,1,0:T(8,128)S(1)}, u32[]{:S(2)}, u32[]{:S(2)}) %collective-permute-start.3) | collective-permute-done | bytes 524320 | tf_op jit(solution)/shard_map/ppermute | solution.py:474
  60.8 1.4 %output_rows.1 = f32[128,1024]{1,0:T(8,128)S(1)} custom-call(s32[1]{0:T(128)} %bitcast.core_ref, f32[16,64,128]{2,1,0:T(8,128)S(1)} %get-tuple-element.44.keep_ref, f32[16,64,128]{2,1,0:T(8,128)S(1)} %collective-permute-done.3.got_ref, f32[16,128,128]{2,1,0:T(8,128)S(1)} %get-tuple-element.46.local_ref, f32[16,128,128]{2,1,0:T(8,128)S(1)} %get-tuple-element.47.reader_ref, ...), custom_call_target="tpu_custom_call" | custom-call | flops 1000000000 | bytes 8388608 | tf_op jit(solution)/shard_map/output_rows/pallas_call | solution.py:358
  62.3 1.3 %collective-permute-start.4 = (f32[32,1024]{1,0:T(8,128)S(1)}, f32[32,1024]{1,0:T(8,128)S(1)}, u32[]{:S(2)}, u32[]{:S(2)}) collective-permute-start(f32[32,1024]{1,0:T(8,128)S(1)} %get-tuple-element.48), channel_id=1, source_target_pairs={{0,32},{32,64},{64,96},{96,0},{1,33},{33,65},{65,97},{97,1},{2,34}... | collective-permute-start | bytes 393224 | tf_op jit(solution)/shard_map/ppermute | solution.py:489
  63.6 1.2 %collective-permute-start.5 = (f32[32,1024]{1,0:T(8,128)S(1)}, f32[32,1024]{1,0:T(8,128)S(1)}, u32[]{:S(2)}, u32[]{:S(2)}) collective-permute-start(f32[32,1024]{1,0:T(8,128)S(1)} %get-tuple-element.51), channel_id=1, source_target_pairs={{0,32},{32,64},{64,96},{96,0},{1,33},{33,65},{65,97},{97,1},{2,34}... | collective-permute-start | bytes 393224 | tf_op jit(solution)/shard_map/ppermute | solution.py:489
  64.8 0.9 %collective-permute-start.6 = (f32[32,1024]{1,0:T(8,128)S(1)}, f32[32,1024]{1,0:T(8,128)S(1)}, u32[]{:S(2)}, u32[]{:S(2)}) collective-permute-start(f32[32,1024]{1,0:T(8,128)S(1)} %get-tuple-element.50), channel_id=1, source_target_pairs={{0,32},{32,64},{64,96},{96,0},{1,33},{33,65},{65,97},{97,1},{2,34}... | collective-permute-start | bytes 393224 | tf_op jit(solution)/shard_map/ppermute | solution.py:489
  65.7 0.2 collective-permute-start.7
  65.9 1.5 %boundary.1 = f32[16,128,128]{2,1,0:T(8,128)} custom-call(s32[1]{0:T(128)} %bitcast.core_ref, f32[16,64,128]{2,1,0:T(8,128)S(1)} %get-tuple-element.44.keep_ref, f32[16,64,128]{2,1,0:T(8,128)S(1)} %collective-permute-done.3.got_ref, f32[8,192,128]{2,1,0:T(8,128)S(1)} %get-tuple-element.33.refs_0_, f32[8,192,128]{2,1,0:T(8,128)S(1)} %get-tuple-element.34.refs_1_, ...), custom_call_target="tpu_custom_call" | custom-call | flops 1000000000 | bytes 4194304 | tf_op jit(solution)/shard_map/boundary/pallas_call | solution.py:358
  67.4 0.8 %collective-permute-done.4 = f32[32,1024]{1,0:T(8,128)S(1)} collective-permute-done((f32[32,1024]{1,0:T(8,128)S(1)}, f32[32,1024]{1,0:T(8,128)S(1)}, u32[]{:S(2)}, u32[]{:S(2)}) %collective-permute-start.4) | collective-permute-done | bytes 131104 | tf_op jit(solution)/shard_map/ppermute | solution.py:489
  68.3 2.8 %collective-permute-done.5 = f32[32,1024]{1,0:T(8,128)S(1)} collective-permute-done((f32[32,1024]{1,0:T(8,128)S(1)}, f32[32,1024]{1,0:T(8,128)S(1)}, u32[]{:S(2)}, u32[]{:S(2)}) %collective-permute-start.5) | collective-permute-done | bytes 131104 | tf_op jit(solution)/shard_map/ppermute | solution.py:489
  71.1 2.8 %collective-permute-done.6 = f32[32,1024]{1,0:T(8,128)S(1)} collective-permute-done((f32[32,1024]{1,0:T(8,128)S(1)}, f32[32,1024]{1,0:T(8,128)S(1)}, u32[]{:S(2)}, u32[]{:S(2)}) %collective-permute-start.6) | collective-permute-done | bytes 131104 | tf_op jit(solution)/shard_map/ppermute | solution.py:489
  73.9 2.8 %collective-permute-done.7 = f32[32,1024]{1,0:T(8,128)S(1)} collective-permute-done((f32[32,1024]{1,0:T(8,128)S(1)}, f32[32,1024]{1,0:T(8,128)S(1)}, u32[]{:S(2)}, u32[]{:S(2)}) %collective-permute-start.7) | collective-permute-done | bytes 131104 | tf_op jit(solution)/shard_map/ppermute | solution.py:489
  76.7 0.8 %maximum_bitcast_fusion = f32[1,128,1024]{2,1,0:T(8,128)} fusion(f32[32,1024]{1,0:T(8,128)S(1)} %collective-permute-done.7, f32[32,1024]{1,0:T(8,128)S(1)} %collective-permute-done.6, f32[32,1024]{1,0:T(8,128)S(1)} %collective-permute-done.5, f32[32,1024]{1,0:T(8,128)S(1)} %collective-permute-done.4), kind=kLoop, calls=%fused_computation | loop fusion | flops 393216 | bytes 1048576 | tf_op jit(solution)/shard_map/broadcast_in_dim | solution.py:494
  (28 shorter events, 0.2 us)
Async XLA Ops:
  0.6 1.0 %copy-start.2 = (f32[1,128,1024]{2,1,0:T(8,128)S(1)}, f32[1,128,1024]{2,1,0:T(8,128)}, u32[]{:S(2)}) copy-start(f32[1,128,1024]{2,1,0:T(8,128)} %param.13) | copy-start | bytes 1572868
  0.7 1.0 %copy-start.7 = (bf16[1,1024,16]{1,2,0:T(8,128)(2,1)S(1)}, bf16[1,1024,16]{1,2,0:T(8,128)(2,1)}, u32[]{:S(2)}) copy-start(bf16[1,1024,16]{1,2,0:T(8,128)(2,1)} %param.18) | copy-start | bytes 98308
  0.7 1.0 %copy-start.8 = (bf16[1,1024,16]{1,2,0:T(8,128)(2,1)S(1)}, bf16[1,1024,16]{1,2,0:T(8,128)(2,1)}, u32[]{:S(2)}) copy-start(bf16[1,1024,16]{1,2,0:T(8,128)(2,1)} %param.19) | copy-start | bytes 98308
  0.7 1.0 %copy-start.9 = (f32[1,1024]{1,0:T(1,128)S(1)}, f32[1,1024]{1,0:T(1,128)}, u32[]{:S(2)}) copy-start(f32[1,1024]{1,0:T(1,128)} %gain_ref.2) | copy-start | bytes 12292
  0.7 1.0 %copy-start.10 = (f32[1,16]{1,0:T(1,128)S(1)}, f32[1,16]{1,0:T(1,128)}, u32[]{:S(2)}) copy-start(f32[1,16]{1,0:T(1,128)} %rate_ref.1) | copy-start | bytes 196
  0.7 1.0 %copy-start.11 = (f32[1,16]{1,0:T(1,128)S(1)}, f32[1,16]{1,0:T(1,128)}, u32[]{:S(2)}) copy-start(f32[1,16]{1,0:T(1,128)} %dtb_ref.1) | copy-start | bytes 196
  0.7 1.0 %copy-start.12 = (f32[1,16]{1,0:T(1,128)S(1)}, f32[1,16]{1,0:T(1,128)}, u32[]{:S(2)}) copy-start(f32[1,16]{1,0:T(1,128)} %bb_ref.1) | copy-start | bytes 196
  0.7 1.9 %copy-start.5 = (bf16[1,1024,1024]{2,1,0:T(8,128)(2,1)S(1)}, bf16[1,1024,1024]{2,1,0:T(8,128)(2,1)}, u32[]{:S(2)}) copy-start(bf16[1,1024,1024]{2,1,0:T(8,128)(2,1)} %param.16) | copy-start | bytes 6291460
  2.6 5.0 %copy-start.4 = (bf16[1,1024,2048]{2,1,0:T(8,128)(2,1)S(1)}, bf16[1,1024,2048]{2,1,0:T(8,128)(2,1)}, u32[]{:S(2)}) copy-start(bf16[1,1024,2048]{2,1,0:T(8,128)(2,1)} %param.17) | copy-start | bytes 12582916
  8.9 2.9 %copy-start.6 = (bf16[1,1024,1024]{2,1,0:T(8,128)(2,1)S(1)}, bf16[1,1024,1024]{2,1,0:T(8,128)(2,1)}, u32[]{:S(2)}) copy-start(bf16[1,1024,1024]{2,1,0:T(8,128)(2,1)} %param.15) | copy-start | bytes 6291460
  8.9 5.2 %collective-permute-start.1 = (f32[8,192,128]{2,1,0:T(8,128)S(1)}, f32[8,192,128]{2,1,0:T(8,128)S(1)}, u32[]{:S(2)}, u32[]{:S(2)}) collective-permute-start(f32[8,192,128]{2,1,0:T(8,128)S(1)} %get-tuple-element.34.refs_1_), channel_id=1, source_target_pairs={{0,1},{1,0},{2,3},{3,2},{4,5},{5,4},{6,7},{7,6},{8,9},{9,8},{10,11... | collective-permute-start | bytes 2359304 | tf_op jit(solution)/shard_map/ppermute | solution.py:443
  11.7 2.5 %collective-permute-start = (f32[8,192,128]{2,1,0:T(8,128)S(1)}, f32[8,192,128]{2,1,0:T(8,128)S(1)}, u32[]{:S(2)}, u32[]{:S(2)}) collective-permute-start(f32[8,192,128]{2,1,0:T(8,128)S(1)} %get-tuple-element.33.refs_0_), channel_id=1, source_target_pairs={{0,1},{1,0},{2,3},{3,2},{4,5},{5,4},{6,7},{7,6},{8,9},{9,8},{10,11... | collective-permute-start | bytes 2359304 | tf_op jit(solution)/shard_map/ppermute | solution.py:443
  14.1 26.6 %copy-start.1 = (f32[1,16,128,128]{3,2,1,0:T(8,128)S(1)}, f32[1,16,128,128]{3,2,1,0:T(8,128)}, u32[]{:S(2)}) copy-start(f32[1,16,128,128]{3,2,1,0:T(8,128)} %param.25) | copy-start | bytes 3145732
  38.5 3.7 %collective-permute-start.2 = (f32[16,64,128]{2,1,0:T(8,128)S(1)}, f32[16,64,128]{2,1,0:T(8,128)S(1)}, u32[]{:S(2)}, u32[]{:S(2)}) collective-permute-start(f32[16,64,128]{2,1,0:T(8,128)S(1)} %slice.20), channel_id=1, source_target_pairs={{0,1},{1,0},{2,3},{3,2},{4,5},{5,4},{6,7},{7,6},{8,9},{9,8},{10,11... | collective-permute-start | bytes 1572872 | tf_op jit(solution)/shard_map/ppermute | solution.py:456
  41.3 19.5 %copy-start = (bf16[1,2048,1024]{2,1,0:T(8,128)(2,1)S(1)}, bf16[1,2048,1024]{2,1,0:T(8,128)(2,1)}, u32[]{:S(2)}) copy-start(bf16[1,2048,1024]{2,1,0:T(8,128)(2,1)} %param.24) | copy-start | bytes 12582916
  41.3 19.5 %copy-start.3 = (f32[1,128]{1,0:T(1,128)S(1)}, f32[1,128]{1,0:T(1,128)}, u32[]{:S(2)}) copy-start(f32[1,128]{1,0:T(1,128)} %gain_ref.3) | copy-start | bytes 1540
  57.4 3.4 %collective-permute-start.3 = (f32[16,64,128]{2,1,0:T(8,128)S(1)}, f32[16,64,128]{2,1,0:T(8,128)S(1)}, u32[]{:S(2)}, u32[]{:S(2)}) collective-permute-start(f32[16,64,128]{2,1,0:T(8,128)S(1)} %get-tuple-element.45), channel_id=1, source_target_pairs={{0,1},{1,0},{2,3},{3,2},{4,5},{5,4},{6,7},{7,6},{8,9},{9,8},{10,11... | collective-permute-start | bytes 1572872 | tf_op jit(solution)/shard_map/ppermute | solution.py:474
  62.3 6.0 %collective-permute-start.4 = (f32[32,1024]{1,0:T(8,128)S(1)}, f32[32,1024]{1,0:T(8,128)S(1)}, u32[]{:S(2)}, u32[]{:S(2)}) collective-permute-start(f32[32,1024]{1,0:T(8,128)S(1)} %get-tuple-element.48), channel_id=1, source_target_pairs={{0,32},{32,64},{64,96},{96,0},{1,33},{33,65},{65,97},{97,1},{2,34}... | collective-permute-start | bytes 393224 | tf_op jit(solution)/shard_map/ppermute | solution.py:489
  63.6 7.5 %collective-permute-start.5 = (f32[32,1024]{1,0:T(8,128)S(1)}, f32[32,1024]{1,0:T(8,128)S(1)}, u32[]{:S(2)}, u32[]{:S(2)}) collective-permute-start(f32[32,1024]{1,0:T(8,128)S(1)} %get-tuple-element.51), channel_id=1, source_target_pairs={{0,32},{32,64},{64,96},{96,0},{1,33},{33,65},{65,97},{97,1},{2,34}... | collective-permute-start | bytes 393224 | tf_op jit(solution)/shard_map/ppermute | solution.py:489
  64.8 9.1 %collective-permute-start.6 = (f32[32,1024]{1,0:T(8,128)S(1)}, f32[32,1024]{1,0:T(8,128)S(1)}, u32[]{:S(2)}, u32[]{:S(2)}) collective-permute-start(f32[32,1024]{1,0:T(8,128)S(1)} %get-tuple-element.50), channel_id=1, source_target_pairs={{0,32},{32,64},{64,96},{96,0},{1,33},{33,65},{65,97},{97,1},{2,34}... | collective-permute-start | bytes 393224 | tf_op jit(solution)/shard_map/ppermute | solution.py:489
  65.7 11.0 %collective-permute-start.7 = (f32[32,1024]{1,0:T(8,128)S(1)}, f32[32,1024]{1,0:T(8,128)S(1)}, u32[]{:S(2)}, u32[]{:S(2)}) collective-permute-start(f32[32,1024]{1,0:T(8,128)S(1)} %get-tuple-element.49), channel_id=1, source_target_pairs={{0,32},{32,64},{64,96},{96,0},{1,33},{33,65},{65,97},{97,1},{2,34}... | collective-permute-start | bytes 393224 | tf_op jit(solution)/shard_map/ppermute | solution.py:489

commit v5 on v4

--- a/solution.py
+++ b/solution.py
@@ -204,40 +204,44 @@
 
 
 def of_head(refs, h):
-    span = VH // len(refs)
-    return refs[h // span].at[h % span]
+    for ref in refs:
+        if h < ref.shape[0]:
+            return ref.at[h]
+        h -= ref.shape[0]
 
 
 def readers_kernel(
-    normed_ref, wq_ref, kt_ref, rt_ref, rb_ref, *refs
+    keys, normed_ref, wq_ref, kt_ref, rt_ref, rb_ref, *refs
 ):
     yt_refs, (local_ref, reader_ref) = refs[:SPLIT], refs[SPLIT:]
+    columns_of = slice(keys[0] * DK, (keys[-1] + 1) * DK)
     rows, columns = square_iotas()
     inclusive = rows >= columns
-    query_all = silu(jnp.dot(normed_ref[...], wq_ref[...], preferred_element_type=f32))
-    for i in range(KH):
+    query_all = silu(jnp.dot(normed_ref[...], wq_ref[:, columns_of], preferred_element_type=f32))
+    for i, key in enumerate(keys):
         query = unit(query_all[:, i * DK : (i + 1) * DK]) * DK ** (-0.5)
-        product = mm(query, kt_ref[i])
-        for h in (2 * i, 2 * i + 1):
+        product = mm(query, kt_ref[key])
+        for n in (2 * i, 2 * i + 1):
+            h = 2 * key + n % 2
             spread = jnp.minimum(rb_ref[h] - rt_ref[h : h + 1], 0.0)
             both = mm_t(jnp.where(inclusive, jnp.exp(spread) * product, 0.0), of_head(yt_refs, h)[...])
-            local_ref[h] = both[:, :DV]
-            reader_ref[h] = jnp.exp(rb_ref[h]) * query - both[:, DV:]
-
-
-def make_readers(normed, wq, *arguments):
+            local_ref[n] = both[:, :DV]
+            reader_ref[n] = jnp.exp(rb_ref[h]) * query - both[:, DV:]
+
+
+def make_readers(keys, *arguments):
     vmem = pl.BlockSpec(memory_space=pltpu.VMEM)
     return pl.pallas_call(
-        readers_kernel,
-        in_specs=[vmem] * (2 + len(arguments)),
+        functools.partial(readers_kernel, keys),
+        in_specs=[vmem] * len(arguments),
         out_specs=[vmem, vmem],
-        out_shape=[jax.ShapeDtypeStruct((VH, T, T), f32)] * 2,
+        out_shape=[jax.ShapeDtypeStruct((VH // KH * len(keys), T, T), f32)] * 2,
         compiler_params=pltpu.CompilerParams(vmem_limit_bytes=8 * MIB),
         cost_estimate=pl.CostEstimate(
             flops=2 * 10**9, bytes_accessed=8 * 2**20, transcendentals=10**6
         ),
         name="readers",
-    )(normed, wq, *arguments)
+    )(*arguments)
 
 
 def on_each_core(core_ref, body):
@@ -329,13 +333,14 @@
 
 
 def output_kernel(
-    part, core_ref, keep_ref, got_ref, local_ref, reader_ref, gain_ref, x_ref, wo_ref, out_ref
+    part, core_ref, keep_ref, got_ref, gain_ref, x_ref, wo_ref, *refs
 ):
+    local_refs, reader_refs, out_ref = refs[:2], refs[2:4], refs[-1]
     rows = slice(part * T // PARTS, (part + 1) * T // PARTS)
     heads = []
     for h in range(VH):
         entering = entering_of(core_ref, keep_ref, got_ref, h)
-        core = local_ref[h, rows] + mm_t(reader_ref[h, rows], entering)
+        core = of_head(local_refs, h)[rows] + mm_t(of_head(reader_refs, h)[rows], entering)
         mean_square = jnp.mean(core * core, axis=-1, keepdims=True)
         heads.append((core * lax.rsqrt(mean_square + 1e-06) * gain_ref[...]).astype(bf16))
     out_ref[...] = x_ref[rows] + jnp.dot(
@@ -441,8 +446,8 @@
         drives.append(own)
         solved.append(yt)
         maps_other.append(lax.ppermute(sent, "seq", pairs))
-    local, reader = make_readers(normed, w_query[0], kt, rt, rb, *solved)
-    maps_other, local, reader = lax.optimization_barrier((maps_other, local, reader))
+    readers = [make_readers(range(6), normed, w_query[0], kt, rt, rb, *solved)]
+    maps_other, readers = lax.optimization_barrier((maps_other, readers))
 
     chip_maps = plain_call(
         compose_kernel,
@@ -454,6 +459,9 @@
     )
     gathered = lax.all_to_all(chip_maps, "seq", 0, 0, axis_index_groups=groups)
     gathered_other = lax.ppermute(gathered[:, :HALF], "seq", pairs)
+    rt, gathered = lax.optimization_barrier((rt, gathered))
+    readers.append(make_readers(range(6, KH), normed, w_query[0], kt, rt, rb, *solved))
+    gathered_other, readers = lax.optimization_barrier((gathered_other, readers))
     states = plain_call(
         scan_kernel,
         "scan_chips",
@@ -472,6 +480,7 @@
         (core, returned, *maps, *drives, *maps_other),
     )
     got = lax.ppermute(send, "seq", pairs)
+    locals_, readers_ = zip(*readers)
     sections = lax.axis_size("section")
     onward = [(i, (i + 1) % sections) for i in range(sections)]
     chunk = T // CHUNKS
@@ -483,7 +492,7 @@
             shape(T // PARTS, x.shape[1]),
             10**9,
             8 * 2**20,
-            (core, keep, got, local, reader, head_gain, x, w_output[0]),
+            (core, keep, got, head_gain, x, w_output[0], *locals_, *readers_),
         )
         for i in range(0, T // PARTS, chunk):
             arrived.append(lax.ppermute(rows_out[i : i + chunk], "section", onward))

time: 77.7 us -> 77.6 us (level)
  starting transfers between devices: 9.25 us -> 8.43 us
    ppermute x1, waiting for transfers between devices: 0.88 us -> 0.01 us  [on_device(): gathered_other = lax.ppermute(gathered[:, :HALF], 'seq', pairs)]
    pallas_call x1 -> x2, Pallas kernels: 2.33 us -> 2.78 us  [make_readers(): pl.pallas_call(functools.partial(readers_kernel, keys), in_specs=[vmem] *...]
  transfers between devices with their start and end apart: 8 -> 8, of which waited for: 6 -> 6; matrix products, arithmetic and copies ran while one was open for 0% -> 0% of each run, Pallas kernels for 7% -> 8%
where the time goes in v5:
time: 77.6 us; the launch traced here: 77.4 us
  blocking collectives  37.8 us (49%)
  Pallas kernels  17.2 us (22%)
  waiting for transfers between devices  11.2 us (14%)
  starting transfers between devices  8.43 us (11%)
  local copies, waits for them, and re-layouts  0.99 us (1%)
  between operations  0.92 us (1%)
  other arithmetic  0.91 us (1%)
    all_to_all x1, blocking collectives, on_device(): gathered = lax.all_to_all(chip_maps, 'seq', 0, 0, axis_index_groups=groups)  24.2 us
    pallas_call x11, Pallas kernels, plain_call(): pl.pallas_call(kernel, in_specs=specs, out_specs=[vmem] * len(outputs) if...  14.4 us
    all_to_all x1, blocking collectives, on_device(): returned = lax.all_to_all(states, 'seq', 0, 0, axis_index_groups=groups)  13.6 us
    ppermute x4, waiting for transfers between devices, on_device(): arrived.append(lax.ppermute(rows_out[i:i + chunk], 'section', onward))  9.24 us
    ppermute x4, starting transfers between devices, on_device(): arrived.append(lax.ppermute(rows_out[i:i + chunk], 'section', onward))  3.61 us
    pallas_call x2, Pallas kernels, make_readers(): pl.pallas_call(functools.partial(readers_kernel, keys), in_specs=[vmem] *...  2.78 us
    ppermute x1, starting transfers between devices, on_device(): gathered_other = lax.ppermute(gathered[:, :HALF], 'seq', pairs)  1.66 us
    ppermute x2, starting transfers between devices, on_device(): maps_other.append(lax.ppermute(sent, 'seq', pairs))  1.61 us
  transfers between devices with their start and end apart: 8, of which 6 were waited for; matrix products, arithmetic and copies ran while one was open for 0% of the time, Pallas kernels for 8%

profile of v5, /device:TPU:1, one launch (start us, length us, event | category | flops | bytes accessed | tf_op | source)
XLA Modules:
  0.0 77.4 jit_solution(9006838371040116482)
XLA Ops:
  0.8 0.1 pad_add_fusion.place_ref
  0.8 0.8 %copy-done.2 = f32[1,128,1024]{2,1,0:T(8,128)S(1)} copy-done((f32[1,128,1024]{2,1,0:T(8,128)S(1)}, f32[1,128,1024]{2,1,0:T(8,128)}, u32[]{:S(2)}) %copy-start.2) | copy-done | bytes 524312
  1.7 0.9 %norm_and_gates.1 = (bf16[128,1024]{1,0:T(8,128)(2,1)S(1)}, f32[16,128]{1,0:T(8,128)S(1)}, f32[16,128]{1,0:T(8,128)S(1)}, f32[16,128,128]{2,1,0:T(8,128)S(1)}) custom-call(s32[1]{0:T(128)} %bitcast.core_ref, f32[2,128,128]{2,1,0:T(8,128)S(1)} %masks.1.mask_ref, f32[128,1024]{1,0:T(8,128)S(1)} %bitcast.19, f32[1,1024]{1,0:T(1,128)S(1)} %copy-done.9, ...), custom_call_target="tpu_custom_call" | custom-call | flops 1000000000 | bytes 104857600 | tf_op jit(solution)/shard_map/norm_and_gates/pallas_call | solution.py:363
  2.6 0.0 copy-start.4
  2.7 5.0 %inverses.1 = (f32[8,128,128]{2,1,0:T(8,128)S(1)}, f32[8,128,128]{2,1,0:T(8,128)S(1)}, f32[16,128,128]{2,1,0:T(8,128)S(1)}) custom-call(s32[1]{0:T(128)} %bitcast.core_ref, bf16[128,1024]{1,0:T(8,128)(2,1)S(1)} %get-tuple-element.36.normed_ref, f32[16,128]{1,0:T(8,128)S(1)} %get-tuple-element.37.bt_ref, f32[16,128]{1,0:T(8,128)S(1)} %get-tuple-element.55.rt_ref, ...), custom_call_target="tpu_custom_call" | custom-call | flops 2000000000 | bytes 20971520 | tf_op jit(solution)/shard_map/inverses/pallas_call | solution.py:363
  7.7 1.2 %block_maps.3 = (f32[8,192,128]{2,1,0:T(8,128)S(1)}, f32[8,128,128]{2,1,0:T(8,128)S(1)}, f32[8,256,128]{2,1,0:T(8,128)S(1)}) custom-call(s32[1]{0:T(128)} %bitcast.core_ref, f32[2,128,128]{2,1,0:T(8,128)S(1)} %masks.1.mask_ref, bf16[128,1024]{1,0:T(8,128)(2,1)S(1)} %get-tuple-element.36.normed_ref, f32[16,128]{1,0:T(8,128)S(1)} %get-tuple-element.37.bt_ref, ...), custom_call_target="tpu_custom_call" | custom-call | flops 2000000000 | bytes 10485760 | tf_op jit(solution)/shard_map/block_maps/pallas_call | solution.py:363
  8.9 1.5 %collective-permute-start.1 = (f32[8,192,128]{2,1,0:T(8,128)S(1)}, f32[8,192,128]{2,1,0:T(8,128)S(1)}, u32[]{:S(2)}, u32[]{:S(2)}) collective-permute-start(f32[8,192,128]{2,1,0:T(8,128)S(1)} %get-tuple-element.43.refs_1_), channel_id=1, source_target_pairs={{0,1},{1,0},{2,3},{3,2},{4,5},{5,4},{6,7},{7,6},{8,9},{9,8},{10,11... | collective-permute-start | bytes 2359304 | tf_op jit(solution)/shard_map/ppermute | solution.py:448
  10.4 1.2 %block_maps.2 = (f32[8,192,128]{2,1,0:T(8,128)S(1)}, f32[8,128,128]{2,1,0:T(8,128)S(1)}, f32[8,256,128]{2,1,0:T(8,128)S(1)}) custom-call(s32[1]{0:T(128)} %bitcast.core_ref, f32[2,128,128]{2,1,0:T(8,128)S(1)} %masks.1.mask_ref, bf16[128,1024]{1,0:T(8,128)(2,1)S(1)} %get-tuple-element.36.normed_ref, f32[16,128]{1,0:T(8,128)S(1)} %get-tuple-element.37.bt_ref, ...), custom_call_target="tpu_custom_call" | custom-call | flops 2000000000 | bytes 10485760 | tf_op jit(solution)/shard_map/block_maps/pallas_call | solution.py:363
  11.6 0.1 collective-permute-start
  11.8 1.9 %readers.2 = (f32[12,128,128]{2,1,0:T(8,128)S(1)}, f32[12,128,128]{2,1,0:T(8,128)S(1)}) custom-call(bf16[128,1024]{1,0:T(8,128)(2,1)S(1)} %get-tuple-element.36.normed_ref, bf16[1024,1024]{1,0:T(8,128)(2,1)S(1)} %bitcast.24, f32[8,128,128]{2,1,0:T(8,128)S(1)} %get-tuple-element.40.kt_ref, f32[16,128]{1,0:T(8,128)S(1)} %get-tuple-element.55.rt_ref, ...), custom_call_target="tpu_custom_call" | custom-call | flops 2000000000 | bytes 8388608 | tf_op jit(solution)/shard_map/readers/pallas_call | solution.py:234
  13.6 0.4 collective-permute-done.refs_4_
  14.0 0.5 compose.1
  14.5 24.2 %all_to_all.10.map_ref = f32[16,128,128]{2,1,0:T(8,128)S(1)} all-to-all(f32[16,128,128]{2,1,0:T(8,128)S(1)} %compose.1), channel_id=1, replica_groups={{0,2,4,6,8,10,12,14,16,18,20,22,24,26,28,30},{1,3,5,7,9,11,13,15,17,19,..., dimensions={0} | all-to-all | bytes 2097152 | tf_op jit(solution)/shard_map/all_to_all | solution.py:460
  38.7 1.7 %collective-permute-start.2 = (f32[16,64,128]{2,1,0:T(8,128)S(1)}, f32[16,64,128]{2,1,0:T(8,128)S(1)}, u32[]{:S(2)}, u32[]{:S(2)}) collective-permute-start(f32[16,64,128]{2,1,0:T(8,128)S(1)} %slice.20), channel_id=1, source_target_pairs={{0,1},{1,0},{2,3},{3,2},{4,5},{5,4},{6,7},{7,6},{8,9},{9,8},{10,11... | collective-permute-start | bytes 1572872 | tf_op jit(solution)/shard_map/ppermute | solution.py:461
  40.4 0.8 %initial_state.1.initial_ref = f32[64,128]{1,0:T(8,128)S(1)} custom-call(s32[2]{0:T(128)S(1)} %pad_add_fusion.place_ref, f32[16,128,128]{2,1,0:T(8,128)S(1)} %bitcast.18), custom_call_target="tpu_custom_call" | custom-call | flops 1000000 | bytes 1048576 | tf_op jit(solution)/shard_map/initial_state/pallas_call | solution.py:363
  41.2 0.9 %readers.3 = (f32[4,128,128]{2,1,0:T(8,128)S(1)}, f32[4,128,128]{2,1,0:T(8,128)S(1)}) custom-call(bf16[128,1024]{1,0:T(8,128)(2,1)S(1)} %get-tuple-element.36.normed_ref, bf16[1024,1024]{1,0:T(8,128)(2,1)S(1)} %bitcast.25, f32[8,128,128]{2,1,0:T(8,128)S(1)} %get-tuple-element.40.kt_ref, f32[16,128]{1,0:T(8,128)S(1)} %get-tuple-element.55.rt_ref, ...), custom_call_target="tpu_custom_call" | custom-call | flops 2000000000 | bytes 8388608 | tf_op jit(solution)/shard_map/readers/pallas_call | solution.py:234
  42.1 1.3 %scan_chips.1 = f32[16,64,128]{2,1,0:T(8,128)S(1)} custom-call(s32[1]{0:T(128)} %bitcast.core_ref, f32[16,128,128]{2,1,0:T(8,128)S(1)} %all_to_all.10.map_ref, f32[16,64,128]{2,1,0:T(8,128)S(1)} %collective-permute-done.2.other_ref, f32[64,128]{1,0:T(8,128)S(1)} %initial_state.1.initial_ref), custom_call_target="tpu_custom_call" | custom-call | flops 100000000 | bytes 31457280 | tf_op jit(solution)/shard_map/scan_chips/pallas_call | solution.py:363
  43.4 13.6 %all_to_all.11.state_ref = f32[16,64,128]{2,1,0:T(8,128)S(1)} all-to-all(f32[16,64,128]{2,1,0:T(8,128)S(1)} %scan_chips.1), channel_id=1, replica_groups={{0,2,4,6,8,10,12,14,16,18,20,22,24,26,28,30},{1,3,5,7,9,11,13,15,17,19,..., dimensions={0} | all-to-all | bytes 1048576 | tf_op jit(solution)/shard_map/all_to_all | solution.py:473
  57.1 0.5 enter.1
  57.6 1.6 %collective-permute-start.3 = (f32[16,64,128]{2,1,0:T(8,128)S(1)}, f32[16,64,128]{2,1,0:T(8,128)S(1)}, u32[]{:S(2)}, u32[]{:S(2)}) collective-permute-start(f32[16,64,128]{2,1,0:T(8,128)S(1)} %get-tuple-element.61), channel_id=1, source_target_pairs={{0,1},{1,0},{2,3},{3,2},{4,5},{5,4},{6,7},{7,6},{8,9},{9,8},{10,11... | collective-permute-start | bytes 1572872 | tf_op jit(solution)/shard_map/ppermute | solution.py:482
  59.1 1.5 %collective-permute-done.3.got_ref = f32[16,64,128]{2,1,0:T(8,128)S(1)} collective-permute-done((f32[16,64,128]{2,1,0:T(8,128)S(1)}, f32[16,64,128]{2,1,0:T(8,128)S(1)}, u32[]{:S(2)}, u32[]{:S(2)}) %collective-permute-start.3) | collective-permute-done | bytes 524320 | tf_op jit(solution)/shard_map/ppermute | solution.py:482
  60.7 1.4 %output_rows.1 = f32[128,1024]{1,0:T(8,128)S(1)} custom-call(s32[1]{0:T(128)} %bitcast.core_ref, f32[16,64,128]{2,1,0:T(8,128)S(1)} %get-tuple-element.60.keep_ref, f32[16,64,128]{2,1,0:T(8,128)S(1)} %collective-permute-done.3.got_ref, f32[1,128]{1,0:T(1,128)S(1)} %copy-done.3, f32[128,1024]{1,0:T(8,128)S(1)} %bitcast.20, bf16[2048,1024]{1,0:T(8,128)(2,1)S(1)} %bitcast.17, ...), custom_call_target="tpu_custom_call" | custom-call | flops 1000000000 | bytes 8388608 | tf_op jit(solution)/shard_map/output_rows/pallas_call | solution.py:363
  62.2 1.3 %collective-permute-start.4 = (f32[32,1024]{1,0:T(8,128)S(1)}, f32[32,1024]{1,0:T(8,128)S(1)}, u32[]{:S(2)}, u32[]{:S(2)}) collective-permute-start(f32[32,1024]{1,0:T(8,128)S(1)} %get-tuple-element.66), channel_id=1, source_target_pairs={{0,32},{32,64},{64,96},{96,0},{1,33},{33,65},{65,97},{97,1},{2,34}... | collective-permute-start | bytes 393224 | tf_op jit(solution)/shard_map/ppermute | solution.py:498
  63.4 1.2 %collective-permute-start.5 = (f32[32,1024]{1,0:T(8,128)S(1)}, f32[32,1024]{1,0:T(8,128)S(1)}, u32[]{:S(2)}, u32[]{:S(2)}) collective-permute-start(f32[32,1024]{1,0:T(8,128)S(1)} %get-tuple-element.69), channel_id=1, source_target_pairs={{0,32},{32,64},{64,96},{96,0},{1,33},{33,65},{65,97},{97,1},{2,34}... | collective-permute-start | bytes 393224 | tf_op jit(solution)/shard_map/ppermute | solution.py:498
  64.6 0.9 %collective-permute-start.6 = (f32[32,1024]{1,0:T(8,128)S(1)}, f32[32,1024]{1,0:T(8,128)S(1)}, u32[]{:S(2)}, u32[]{:S(2)}) collective-permute-start(f32[32,1024]{1,0:T(8,128)S(1)} %get-tuple-element.68), channel_id=1, source_target_pairs={{0,32},{32,64},{64,96},{96,0},{1,33},{33,65},{65,97},{97,1},{2,34}... | collective-permute-start | bytes 393224 | tf_op jit(solution)/shard_map/ppermute | solution.py:498
  65.6 0.2 collective-permute-start.7
  65.8 1.6 %boundary.1 = f32[16,128,128]{2,1,0:T(8,128)} custom-call(s32[1]{0:T(128)} %bitcast.core_ref, f32[16,64,128]{2,1,0:T(8,128)S(1)} %get-tuple-element.60.keep_ref, f32[16,64,128]{2,1,0:T(8,128)S(1)} %collective-permute-done.3.got_ref, f32[8,192,128]{2,1,0:T(8,128)S(1)} %get-tuple-element.42.refs_0_, f32[8,192,128]{2,1,0:T(8,128)S(1)} %get-tuple-element.43.refs_1_, ...), custom_call_target="tpu_custom_call" | custom-call | flops 1000000000 | bytes 4194304 | tf_op jit(solution)/shard_map/boundary/pallas_call | solution.py:363
  67.3 0.8 %collective-permute-done.4 = f32[32,1024]{1,0:T(8,128)S(1)} collective-permute-done((f32[32,1024]{1,0:T(8,128)S(1)}, f32[32,1024]{1,0:T(8,128)S(1)}, u32[]{:S(2)}, u32[]{:S(2)}) %collective-permute-start.4) | collective-permute-done | bytes 131104 | tf_op jit(solution)/shard_map/ppermute | solution.py:498
  68.1 2.8 %collective-permute-done.5 = f32[32,1024]{1,0:T(8,128)S(1)} collective-permute-done((f32[32,1024]{1,0:T(8,128)S(1)}, f32[32,1024]{1,0:T(8,128)S(1)}, u32[]{:S(2)}, u32[]{:S(2)}) %collective-permute-start.5) | collective-permute-done | bytes 131104 | tf_op jit(solution)/shard_map/ppermute | solution.py:498
  70.9 2.8 %collective-permute-done.6 = f32[32,1024]{1,0:T(8,128)S(1)} collective-permute-done((f32[32,1024]{1,0:T(8,128)S(1)}, f32[32,1024]{1,0:T(8,128)S(1)}, u32[]{:S(2)}, u32[]{:S(2)}) %collective-permute-start.6) | collective-permute-done | bytes 131104 | tf_op jit(solution)/shard_map/ppermute | solution.py:498
  73.8 2.8 %collective-permute-done.7 = f32[32,1024]{1,0:T(8,128)S(1)} collective-permute-done((f32[32,1024]{1,0:T(8,128)S(1)}, f32[32,1024]{1,0:T(8,128)S(1)}, u32[]{:S(2)}, u32[]{:S(2)}) %collective-permute-start.7) | collective-permute-done | bytes 131104 | tf_op jit(solution)/shard_map/ppermute | solution.py:498
  76.6 0.8 %maximum_bitcast_fusion = f32[1,128,1024]{2,1,0:T(8,128)} fusion(f32[32,1024]{1,0:T(8,128)S(1)} %collective-permute-done.7, f32[32,1024]{1,0:T(8,128)S(1)} %collective-permute-done.6, f32[32,1024]{1,0:T(8,128)S(1)} %collective-permute-done.5, f32[32,1024]{1,0:T(8,128)S(1)} %collective-permute-done.4), kind=kLoop, calls=%fused_computation | loop fusion | flops 393216 | bytes 1048576 | tf_op jit(solution)/shard_map/broadcast_in_dim | solution.py:503
  (29 shorter events, 0.2 us)
Async XLA Ops:
  0.6 1.0 %copy-start.2 = (f32[1,128,1024]{2,1,0:T(8,128)S(1)}, f32[1,128,1024]{2,1,0:T(8,128)}, u32[]{:S(2)}) copy-start(f32[1,128,1024]{2,1,0:T(8,128)} %param.13) | copy-start | bytes 1572868
  0.7 1.0 %copy-start.7 = (bf16[1,1024,16]{1,2,0:T(8,128)(2,1)S(1)}, bf16[1,1024,16]{1,2,0:T(8,128)(2,1)}, u32[]{:S(2)}) copy-start(bf16[1,1024,16]{1,2,0:T(8,128)(2,1)} %param.18) | copy-start | bytes 98308
  0.7 1.0 %copy-start.8 = (bf16[1,1024,16]{1,2,0:T(8,128)(2,1)S(1)}, bf16[1,1024,16]{1,2,0:T(8,128)(2,1)}, u32[]{:S(2)}) copy-start(bf16[1,1024,16]{1,2,0:T(8,128)(2,1)} %param.19) | copy-start | bytes 98308
  0.7 1.0 %copy-start.9 = (f32[1,1024]{1,0:T(1,128)S(1)}, f32[1,1024]{1,0:T(1,128)}, u32[]{:S(2)}) copy-start(f32[1,1024]{1,0:T(1,128)} %gain_ref.2) | copy-start | bytes 12292
  0.7 1.0 %copy-start.10 = (f32[1,16]{1,0:T(1,128)S(1)}, f32[1,16]{1,0:T(1,128)}, u32[]{:S(2)}) copy-start(f32[1,16]{1,0:T(1,128)} %rate_ref.1) | copy-start | bytes 196
  0.7 1.0 %copy-start.11 = (f32[1,16]{1,0:T(1,128)S(1)}, f32[1,16]{1,0:T(1,128)}, u32[]{:S(2)}) copy-start(f32[1,16]{1,0:T(1,128)} %dtb_ref.1) | copy-start | bytes 196
  0.7 1.0 %copy-start.12 = (f32[1,16]{1,0:T(1,128)S(1)}, f32[1,16]{1,0:T(1,128)}, u32[]{:S(2)}) copy-start(f32[1,16]{1,0:T(1,128)} %bb_ref.1) | copy-start | bytes 196
  0.7 1.9 %copy-start.5 = (bf16[1,1024,1024]{2,1,0:T(8,128)(2,1)S(1)}, bf16[1,1024,1024]{2,1,0:T(8,128)(2,1)}, u32[]{:S(2)}) copy-start(bf16[1,1024,1024]{2,1,0:T(8,128)(2,1)} %param.16) | copy-start | bytes 6291460
  2.6 5.0 %copy-start.4 = (bf16[1,1024,2048]{2,1,0:T(8,128)(2,1)S(1)}, bf16[1,1024,2048]{2,1,0:T(8,128)(2,1)}, u32[]{:S(2)}) copy-start(bf16[1,1024,2048]{2,1,0:T(8,128)(2,1)} %param.17) | copy-start | bytes 12582916
  8.9 2.8 %copy-start.6 = (bf16[1,1024,1024]{2,1,0:T(8,128)(2,1)S(1)}, bf16[1,1024,1024]{2,1,0:T(8,128)(2,1)}, u32[]{:S(2)}) copy-start(bf16[1,1024,1024]{2,1,0:T(8,128)(2,1)} %param.15) | copy-start | bytes 6291460
  8.9 4.7 %collective-permute-start.1 = (f32[8,192,128]{2,1,0:T(8,128)S(1)}, f32[8,192,128]{2,1,0:T(8,128)S(1)}, u32[]{:S(2)}, u32[]{:S(2)}) collective-permute-start(f32[8,192,128]{2,1,0:T(8,128)S(1)} %get-tuple-element.43.refs_1_), channel_id=1, source_target_pairs={{0,1},{1,0},{2,3},{3,2},{4,5},{5,4},{6,7},{7,6},{8,9},{9,8},{10,11... | collective-permute-start | bytes 2359304 | tf_op jit(solution)/shard_map/ppermute | solution.py:448
  11.6 2.4 %collective-permute-start = (f32[8,192,128]{2,1,0:T(8,128)S(1)}, f32[8,192,128]{2,1,0:T(8,128)S(1)}, u32[]{:S(2)}, u32[]{:S(2)}) collective-permute-start(f32[8,192,128]{2,1,0:T(8,128)S(1)} %get-tuple-element.42.refs_0_), channel_id=1, source_target_pairs={{0,1},{1,0},{2,3},{3,2},{4,5},{5,4},{6,7},{7,6},{8,9},{9,8},{10,11... | collective-permute-start | bytes 2359304 | tf_op jit(solution)/shard_map/ppermute | solution.py:448
  14.0 26.4 %copy-start.1 = (f32[1,16,128,128]{3,2,1,0:T(8,128)S(1)}, f32[1,16,128,128]{3,2,1,0:T(8,128)}, u32[]{:S(2)}) copy-start(f32[1,16,128,128]{3,2,1,0:T(8,128)} %param.25) | copy-start | bytes 3145732
  38.7 3.4 %collective-permute-start.2 = (f32[16,64,128]{2,1,0:T(8,128)S(1)}, f32[16,64,128]{2,1,0:T(8,128)S(1)}, u32[]{:S(2)}, u32[]{:S(2)}) collective-permute-start(f32[16,64,128]{2,1,0:T(8,128)S(1)} %slice.20), channel_id=1, source_target_pairs={{0,1},{1,0},{2,3},{3,2},{4,5},{5,4},{6,7},{7,6},{8,9},{9,8},{10,11... | collective-permute-start | bytes 1572872 | tf_op jit(solution)/shard_map/ppermute | solution.py:461
  42.1 18.6 %copy-start = (bf16[1,2048,1024]{2,1,0:T(8,128)(2,1)S(1)}, bf16[1,2048,1024]{2,1,0:T(8,128)(2,1)}, u32[]{:S(2)}) copy-start(bf16[1,2048,1024]{2,1,0:T(8,128)(2,1)} %param.24) | copy-start | bytes 12582916
  42.1 18.6 %copy-start.3 = (f32[1,128]{1,0:T(1,128)S(1)}, f32[1,128]{1,0:T(1,128)}, u32[]{:S(2)}) copy-start(f32[1,128]{1,0:T(1,128)} %gain_ref.3) | copy-start | bytes 1540
  57.6 3.1 %collective-permute-start.3 = (f32[16,64,128]{2,1,0:T(8,128)S(1)}, f32[16,64,128]{2,1,0:T(8,128)S(1)}, u32[]{:S(2)}, u32[]{:S(2)}) collective-permute-start(f32[16,64,128]{2,1,0:T(8,128)S(1)} %get-tuple-element.61), channel_id=1, source_target_pairs={{0,1},{1,0},{2,3},{3,2},{4,5},{5,4},{6,7},{7,6},{8,9},{9,8},{10,11... | collective-permute-start | bytes 1572872 | tf_op jit(solution)/shard_map/ppermute | solution.py:482
  62.2 6.0 %collective-permute-start.4 = (f32[32,1024]{1,0:T(8,128)S(1)}, f32[32,1024]{1,0:T(8,128)S(1)}, u32[]{:S(2)}, u32[]{:S(2)}) collective-permute-start(f32[32,1024]{1,0:T(8,128)S(1)} %get-tuple-element.66), channel_id=1, source_target_pairs={{0,32},{32,64},{64,96},{96,0},{1,33},{33,65},{65,97},{97,1},{2,34}... | collective-permute-start | bytes 393224 | tf_op jit(solution)/shard_map/ppermute | solution.py:498
  63.4 7.5 %collective-permute-start.5 = (f32[32,1024]{1,0:T(8,128)S(1)}, f32[32,1024]{1,0:T(8,128)S(1)}, u32[]{:S(2)}, u32[]{:S(2)}) collective-permute-start(f32[32,1024]{1,0:T(8,128)S(1)} %get-tuple-element.69), channel_id=1, source_target_pairs={{0,32},{32,64},{64,96},{96,0},{1,33},{33,65},{65,97},{97,1},{2,34}... | collective-permute-start | bytes 393224 | tf_op jit(solution)/shard_map/ppermute | solution.py:498
  64.6 9.1 %collective-permute-start.6 = (f32[32,1024]{1,0:T(8,128)S(1)}, f32[32,1024]{1,0:T(8,128)S(1)}, u32[]{:S(2)}, u32[]{:S(2)}) collective-permute-start(f32[32,1024]{1,0:T(8,128)S(1)} %get-tuple-element.68), channel_id=1, source_target_pairs={{0,32},{32,64},{64,96},{96,0},{1,33},{33,65},{65,97},{97,1},{2,34}... | collective-permute-start | bytes 393224 | tf_op jit(solution)/shard_map/ppermute | solution.py:498
  65.6 11.0 %collective-permute-start.7 = (f32[32,1024]{1,0:T(8,128)S(1)}, f32[32,1024]{1,0:T(8,128)S(1)}, u32[]{:S(2)}, u32[]{:S(2)}) collective-permute-start(f32[32,1024]{1,0:T(8,128)S(1)} %get-tuple-element.67), channel_id=1, source_target_pairs={{0,32},{32,64},{64,96},{96,0},{1,33},{33,65},{65,97},{97,1},{2,34}... | collective-permute-start | bytes 393224 | tf_op jit(solution)/shard_map/ppermute | solution.py:498

commit v6 on v4

--- a/solution.py
+++ b/solution.py
@@ -290,16 +290,23 @@
             return jnp.concatenate(halves if core == 0 else halves[::-1], axis=0)
 
         drive = lambda p: map_ref[p, HALF : 2 * HALF]
-        pairs = []
-        for p in range(0, count - 2, 2):
-            both = mm(jnp.concatenate([full(p), drive(p)], axis=0), full(p + 1))
-            pairs.append((both[:DK], both[DK:] + drive(p + 1)))
+        def after(first, second):
+            both = mm(jnp.concatenate(first, axis=0), second[0])
+            return both[:DK], both[DK:] + second[1]
+
+        apply = lambda state, move: mm(state, move[0]) + move[1]
+        single = [(full(p), drive(p)) for p in range(count)]
+        pairs = [after(single[p], single[p + 1]) for p in range(0, count - 2, 2)]
+        fours = [after(pairs[n], pairs[n + 1]) for n in range(0, len(pairs) - 1, 2)]
         current = initial_ref[...]
-        for p in range(0, count, 2):
+        for p in range(0, count, 4):
+            middle = apply(current, pairs[p // 2])
             out_ref[p] = current
-            out_ref[p + 1] = mm(current, full(p)) + drive(p)
-            if p < count - 2:
-                current = mm(current, pairs[p // 2][0]) + pairs[p // 2][1]
+            out_ref[p + 1] = apply(current, single[p])
+            out_ref[p + 2] = middle
+            out_ref[p + 3] = apply(middle, single[p + 2])
+            if p < count - 4:
+                current = apply(current, fours[p // 4])
 
     on_each_core(core_ref, body)
 

time: 77.7 us -> 77.6 us (level)
  no operation moved by 1% of the time
where the time goes in v6:
time: 77.6 us; the launch traced here: 77.4 us
  blocking collectives  37.2 us (48%)
  Pallas kernels  16.4 us (21%)
  waiting for transfers between devices  11.7 us (15%)
  starting transfers between devices  9.25 us (12%)
  local copies, waits for them, and re-layouts  0.99 us (1%)
  between operations  0.92 us (1%)
  other arithmetic  0.91 us (1%)
    all_to_all x1, blocking collectives, on_device(): gathered = lax.all_to_all(chip_maps, 'seq', 0, 0, axis_index_groups=groups)  23.8 us
    pallas_call x11, Pallas kernels, plain_call(): pl.pallas_call(kernel, in_specs=specs, out_specs=[vmem] * len(outputs) if...  14.1 us
    all_to_all x1, blocking collectives, on_device(): returned = lax.all_to_all(states, 'seq', 0, 0, axis_index_groups=groups)  13.4 us
    ppermute x4, waiting for transfers between devices, on_device(): arrived.append(lax.ppermute(rows_out[i:i + chunk], 'section', onward))  9.26 us
    ppermute x4, starting transfers between devices, on_device(): arrived.append(lax.ppermute(rows_out[i:i + chunk], 'section', onward))  3.61 us
    pallas_call x1, Pallas kernels, make_readers(): pl.pallas_call(readers_kernel, in_specs=[vmem] * (2 + len(arguments)), ou...  2.33 us
    ppermute x1, starting transfers between devices, on_device(): gathered_other = lax.ppermute(gathered[:, :HALF], 'seq', pairs)  2.17 us
    ppermute x1, starting transfers between devices, on_device(): got = lax.ppermute(send, 'seq', pairs)  1.87 us
  transfers between devices with their start and end apart: 8, of which 6 were waited for; matrix products, arithmetic and copies ran while one was open for 0% of the time, Pallas kernels for 7%

profile of v6, /device:TPU:1, one launch (start us, length us, event | category | flops | bytes accessed | tf_op | source)
XLA Modules:
  0.0 77.4 jit_solution(6728829718567307984)
XLA Ops:
  0.8 0.1 pad_add_fusion.place_ref
  0.8 0.8 %copy-done.2 = f32[1,128,1024]{2,1,0:T(8,128)S(1)} copy-done((f32[1,128,1024]{2,1,0:T(8,128)S(1)}, f32[1,128,1024]{2,1,0:T(8,128)}, u32[]{:S(2)}) %copy-start.2) | copy-done | bytes 524312
  1.7 0.9 %norm_and_gates.1 = (bf16[128,1024]{1,0:T(8,128)(2,1)S(1)}, f32[16,128]{1,0:T(8,128)S(1)}, f32[16,128]{1,0:T(8,128)S(1)}, f32[16,128,128]{2,1,0:T(8,128)S(1)}) custom-call(s32[1]{0:T(128)} %bitcast.core_ref, f32[2,128,128]{2,1,0:T(8,128)S(1)} %masks.1.mask_ref, f32[128,1024]{1,0:T(8,128)S(1)} %bitcast.19, f32[1,1024]{1,0:T(1,128)S(1)} %copy-done.9, ...), custom_call_target="tpu_custom_call" | custom-call | flops 1000000000 | bytes 104857600 | tf_op jit(solution)/shard_map/norm_and_gates/pallas_call | solution.py:365
  2.7 5.0 %inverses.1 = (f32[8,128,128]{2,1,0:T(8,128)S(1)}, f32[8,128,128]{2,1,0:T(8,128)S(1)}, f32[16,128,128]{2,1,0:T(8,128)S(1)}) custom-call(s32[1]{0:T(128)} %bitcast.core_ref, bf16[128,1024]{1,0:T(8,128)(2,1)S(1)} %get-tuple-element.26.normed_ref, f32[16,128]{1,0:T(8,128)S(1)} %get-tuple-element.27.bt_ref, f32[16,128]{1,0:T(8,128)S(1)} %get-tuple-element.28.rt_ref, ...), custom_call_target="tpu_custom_call" | custom-call | flops 2000000000 | bytes 20971520 | tf_op jit(solution)/shard_map/inverses/pallas_call | solution.py:365
  7.7 1.2 %block_maps.3 = (f32[8,192,128]{2,1,0:T(8,128)S(1)}, f32[8,128,128]{2,1,0:T(8,128)S(1)}, f32[8,256,128]{2,1,0:T(8,128)S(1)}) custom-call(s32[1]{0:T(128)} %bitcast.core_ref, f32[2,128,128]{2,1,0:T(8,128)S(1)} %masks.1.mask_ref, bf16[128,1024]{1,0:T(8,128)(2,1)S(1)} %get-tuple-element.26.normed_ref, f32[16,128]{1,0:T(8,128)S(1)} %get-tuple-element.27.bt_ref, ...), custom_call_target="tpu_custom_call" | custom-call | flops 2000000000 | bytes 10485760 | tf_op jit(solution)/shard_map/block_maps/pallas_call | solution.py:365
  8.9 0.0 copy-start.6
  8.9 1.5 %collective-permute-start.1 = (f32[8,192,128]{2,1,0:T(8,128)S(1)}, f32[8,192,128]{2,1,0:T(8,128)S(1)}, u32[]{:S(2)}, u32[]{:S(2)}) collective-permute-start(f32[8,192,128]{2,1,0:T(8,128)S(1)} %get-tuple-element.34.refs_1_), channel_id=1, source_target_pairs={{0,1},{1,0},{2,3},{3,2},{4,5},{5,4},{6,7},{7,6},{8,9},{9,8},{10,11... | collective-permute-start | bytes 2359304 | tf_op jit(solution)/shard_map/ppermute | solution.py:450
  10.4 1.2 %block_maps.2 = (f32[8,192,128]{2,1,0:T(8,128)S(1)}, f32[8,128,128]{2,1,0:T(8,128)S(1)}, f32[8,256,128]{2,1,0:T(8,128)S(1)}) custom-call(s32[1]{0:T(128)} %bitcast.core_ref, f32[2,128,128]{2,1,0:T(8,128)S(1)} %masks.1.mask_ref, bf16[128,1024]{1,0:T(8,128)(2,1)S(1)} %get-tuple-element.26.normed_ref, f32[16,128]{1,0:T(8,128)S(1)} %get-tuple-element.27.bt_ref, ...), custom_call_target="tpu_custom_call" | custom-call | flops 2000000000 | bytes 10485760 | tf_op jit(solution)/shard_map/block_maps/pallas_call | solution.py:365
  11.7 0.1 collective-permute-start
  11.8 2.3 %readers.1 = (f32[16,128,128]{2,1,0:T(8,128)S(1)}, f32[16,128,128]{2,1,0:T(8,128)S(1)}) custom-call(bf16[128,1024]{1,0:T(8,128)(2,1)S(1)} %get-tuple-element.26.normed_ref, bf16[1024,1024]{1,0:T(8,128)(2,1)S(1)} %bitcast.24, f32[8,128,128]{2,1,0:T(8,128)S(1)} %get-tuple-element.31.kt_ref, f32[16,128]{1,0:T(8,128)S(1)} %get-tuple-element.28.rt_ref, ...), custom_call_target="tpu_custom_call" | custom-call | flops 2000000000 | bytes 8388608 | tf_op jit(solution)/shard_map/readers/pallas_call | solution.py:230
  14.1 0.5 compose.1
  14.6 23.8 %all_to_all.10.map_ref = f32[16,128,128]{2,1,0:T(8,128)S(1)} all-to-all(f32[16,128,128]{2,1,0:T(8,128)S(1)} %compose.1), channel_id=1, replica_groups={{0,2,4,6,8,10,12,14,16,18,20,22,24,26,28,30},{1,3,5,7,9,11,13,15,17,19,..., dimensions={0} | all-to-all | bytes 2097152 | tf_op jit(solution)/shard_map/all_to_all | solution.py:462
  38.5 2.2 %collective-permute-start.2 = (f32[16,64,128]{2,1,0:T(8,128)S(1)}, f32[16,64,128]{2,1,0:T(8,128)S(1)}, u32[]{:S(2)}, u32[]{:S(2)}) collective-permute-start(f32[16,64,128]{2,1,0:T(8,128)S(1)} %slice.20), channel_id=1, source_target_pairs={{0,1},{1,0},{2,3},{3,2},{4,5},{5,4},{6,7},{7,6},{8,9},{9,8},{10,11... | collective-permute-start | bytes 1572872 | tf_op jit(solution)/shard_map/ppermute | solution.py:463
  40.7 0.6 initial_state.1.initial_ref
  41.3 0.0 copy-start.3
  41.4 0.9 %collective-permute-done.2.other_ref = f32[16,64,128]{2,1,0:T(8,128)S(1)} collective-permute-done((f32[16,64,128]{2,1,0:T(8,128)S(1)}, f32[16,64,128]{2,1,0:T(8,128)S(1)}, u32[]{:S(2)}, u32[]{:S(2)}) %collective-permute-start.2) | collective-permute-done | bytes 524320 | tf_op jit(solution)/shard_map/ppermute | solution.py:463
  42.2 1.1 %scan_chips.1 = f32[16,64,128]{2,1,0:T(8,128)S(1)} custom-call(s32[1]{0:T(128)} %bitcast.core_ref, f32[16,128,128]{2,1,0:T(8,128)S(1)} %all_to_all.10.map_ref, f32[16,64,128]{2,1,0:T(8,128)S(1)} %collective-permute-done.2.other_ref, f32[64,128]{1,0:T(8,128)S(1)} %initial_state.1.initial_ref), custom_call_target="tpu_custom_call" | custom-call | flops 100000000 | bytes 31457280 | tf_op jit(solution)/shard_map/scan_chips/pallas_call | solution.py:365
  43.4 13.4 %all_to_all.11.state_ref = f32[16,64,128]{2,1,0:T(8,128)S(1)} all-to-all(f32[16,64,128]{2,1,0:T(8,128)S(1)} %scan_chips.1), channel_id=1, replica_groups={{0,2,4,6,8,10,12,14,16,18,20,22,24,26,28,30},{1,3,5,7,9,11,13,15,17,19,..., dimensions={0} | all-to-all | bytes 1048576 | tf_op jit(solution)/shard_map/all_to_all | solution.py:472
  56.8 0.5 enter.1
  57.3 1.9 %collective-permute-start.3 = (f32[16,64,128]{2,1,0:T(8,128)S(1)}, f32[16,64,128]{2,1,0:T(8,128)S(1)}, u32[]{:S(2)}, u32[]{:S(2)}) collective-permute-start(f32[16,64,128]{2,1,0:T(8,128)S(1)} %get-tuple-element.45), channel_id=1, source_target_pairs={{0,1},{1,0},{2,3},{3,2},{4,5},{5,4},{6,7},{7,6},{8,9},{9,8},{10,11... | collective-permute-start | bytes 1572872 | tf_op jit(solution)/shard_map/ppermute | solution.py:481
  59.1 1.5 %collective-permute-done.3.got_ref = f32[16,64,128]{2,1,0:T(8,128)S(1)} collective-permute-done((f32[16,64,128]{2,1,0:T(8,128)S(1)}, f32[16,64,128]{2,1,0:T(8,128)S(1)}, u32[]{:S(2)}, u32[]{:S(2)}) %collective-permute-start.3) | collective-permute-done | bytes 524320 | tf_op jit(solution)/shard_map/ppermute | solution.py:481
  60.7 1.4 %output_rows.1 = f32[128,1024]{1,0:T(8,128)S(1)} custom-call(s32[1]{0:T(128)} %bitcast.core_ref, f32[16,64,128]{2,1,0:T(8,128)S(1)} %get-tuple-element.44.keep_ref, f32[16,64,128]{2,1,0:T(8,128)S(1)} %collective-permute-done.3.got_ref, f32[16,128,128]{2,1,0:T(8,128)S(1)} %get-tuple-element.46.local_ref, f32[16,128,128]{2,1,0:T(8,128)S(1)} %get-tuple-element.47.reader_ref, ...), custom_call_target="tpu_custom_call" | custom-call | flops 1000000000 | bytes 8388608 | tf_op jit(solution)/shard_map/output_rows/pallas_call | solution.py:365
  62.2 1.3 %collective-permute-start.4 = (f32[32,1024]{1,0:T(8,128)S(1)}, f32[32,1024]{1,0:T(8,128)S(1)}, u32[]{:S(2)}, u32[]{:S(2)}) collective-permute-start(f32[32,1024]{1,0:T(8,128)S(1)} %get-tuple-element.48), channel_id=1, source_target_pairs={{0,32},{32,64},{64,96},{96,0},{1,33},{33,65},{65,97},{97,1},{2,34}... | collective-permute-start | bytes 393224 | tf_op jit(solution)/shard_map/ppermute | solution.py:496
  63.4 1.2 %collective-permute-start.5 = (f32[32,1024]{1,0:T(8,128)S(1)}, f32[32,1024]{1,0:T(8,128)S(1)}, u32[]{:S(2)}, u32[]{:S(2)}) collective-permute-start(f32[32,1024]{1,0:T(8,128)S(1)} %get-tuple-element.51), channel_id=1, source_target_pairs={{0,32},{32,64},{64,96},{96,0},{1,33},{33,65},{65,97},{97,1},{2,34}... | collective-permute-start | bytes 393224 | tf_op jit(solution)/shard_map/ppermute | solution.py:496
  64.7 0.9 %collective-permute-start.6 = (f32[32,1024]{1,0:T(8,128)S(1)}, f32[32,1024]{1,0:T(8,128)S(1)}, u32[]{:S(2)}, u32[]{:S(2)}) collective-permute-start(f32[32,1024]{1,0:T(8,128)S(1)} %get-tuple-element.50), channel_id=1, source_target_pairs={{0,32},{32,64},{64,96},{96,0},{1,33},{33,65},{65,97},{97,1},{2,34}... | collective-permute-start | bytes 393224 | tf_op jit(solution)/shard_map/ppermute | solution.py:496
  65.6 0.2 collective-permute-start.7
  65.8 1.5 %boundary.1 = f32[16,128,128]{2,1,0:T(8,128)} custom-call(s32[1]{0:T(128)} %bitcast.core_ref, f32[16,64,128]{2,1,0:T(8,128)S(1)} %get-tuple-element.44.keep_ref, f32[16,64,128]{2,1,0:T(8,128)S(1)} %collective-permute-done.3.got_ref, f32[8,192,128]{2,1,0:T(8,128)S(1)} %get-tuple-element.33.refs_0_, f32[8,192,128]{2,1,0:T(8,128)S(1)} %get-tuple-element.34.refs_1_, ...), custom_call_target="tpu_custom_call" | custom-call | flops 1000000000 | bytes 4194304 | tf_op jit(solution)/shard_map/boundary/pallas_call | solution.py:365
  67.3 0.8 %collective-permute-done.4 = f32[32,1024]{1,0:T(8,128)S(1)} collective-permute-done((f32[32,1024]{1,0:T(8,128)S(1)}, f32[32,1024]{1,0:T(8,128)S(1)}, u32[]{:S(2)}, u32[]{:S(2)}) %collective-permute-start.4) | collective-permute-done | bytes 131104 | tf_op jit(solution)/shard_map/ppermute | solution.py:496
  68.2 2.8 %collective-permute-done.5 = f32[32,1024]{1,0:T(8,128)S(1)} collective-permute-done((f32[32,1024]{1,0:T(8,128)S(1)}, f32[32,1024]{1,0:T(8,128)S(1)}, u32[]{:S(2)}, u32[]{:S(2)}) %collective-permute-start.5) | collective-permute-done | bytes 131104 | tf_op jit(solution)/shard_map/ppermute | solution.py:496
  71.0 2.8 %collective-permute-done.6 = f32[32,1024]{1,0:T(8,128)S(1)} collective-permute-done((f32[32,1024]{1,0:T(8,128)S(1)}, f32[32,1024]{1,0:T(8,128)S(1)}, u32[]{:S(2)}, u32[]{:S(2)}) %collective-permute-start.6) | collective-permute-done | bytes 131104 | tf_op jit(solution)/shard_map/ppermute | solution.py:496
  73.8 2.8 %collective-permute-done.7 = f32[32,1024]{1,0:T(8,128)S(1)} collective-permute-done((f32[32,1024]{1,0:T(8,128)S(1)}, f32[32,1024]{1,0:T(8,128)S(1)}, u32[]{:S(2)}, u32[]{:S(2)}) %collective-permute-start.7) | collective-permute-done | bytes 131104 | tf_op jit(solution)/shard_map/ppermute | solution.py:496
  76.6 0.8 %maximum_bitcast_fusion = f32[1,128,1024]{2,1,0:T(8,128)} fusion(f32[32,1024]{1,0:T(8,128)S(1)} %collective-permute-done.7, f32[32,1024]{1,0:T(8,128)S(1)} %collective-permute-done.6, f32[32,1024]{1,0:T(8,128)S(1)} %collective-permute-done.5, f32[32,1024]{1,0:T(8,128)S(1)} %collective-permute-done.4), kind=kLoop, calls=%fused_computation | loop fusion | flops 393216 | bytes 1048576 | tf_op jit(solution)/shard_map/broadcast_in_dim | solution.py:501
  (28 shorter events, 0.2 us)
Async XLA Ops:
  0.6 1.0 %copy-start.2 = (f32[1,128,1024]{2,1,0:T(8,128)S(1)}, f32[1,128,1024]{2,1,0:T(8,128)}, u32[]{:S(2)}) copy-start(f32[1,128,1024]{2,1,0:T(8,128)} %param.13) | copy-start | bytes 1572868
  0.7 1.0 %copy-start.7 = (bf16[1,1024,16]{1,2,0:T(8,128)(2,1)S(1)}, bf16[1,1024,16]{1,2,0:T(8,128)(2,1)}, u32[]{:S(2)}) copy-start(bf16[1,1024,16]{1,2,0:T(8,128)(2,1)} %param.18) | copy-start | bytes 98308
  0.7 1.0 %copy-start.8 = (bf16[1,1024,16]{1,2,0:T(8,128)(2,1)S(1)}, bf16[1,1024,16]{1,2,0:T(8,128)(2,1)}, u32[]{:S(2)}) copy-start(bf16[1,1024,16]{1,2,0:T(8,128)(2,1)} %param.19) | copy-start | bytes 98308
  0.7 1.0 %copy-start.9 = (f32[1,1024]{1,0:T(1,128)S(1)}, f32[1,1024]{1,0:T(1,128)}, u32[]{:S(2)}) copy-start(f32[1,1024]{1,0:T(1,128)} %gain_ref.2) | copy-start | bytes 12292
  0.7 1.0 %copy-start.10 = (f32[1,16]{1,0:T(1,128)S(1)}, f32[1,16]{1,0:T(1,128)}, u32[]{:S(2)}) copy-start(f32[1,16]{1,0:T(1,128)} %rate_ref.1) | copy-start | bytes 196
  0.7 1.0 %copy-start.11 = (f32[1,16]{1,0:T(1,128)S(1)}, f32[1,16]{1,0:T(1,128)}, u32[]{:S(2)}) copy-start(f32[1,16]{1,0:T(1,128)} %dtb_ref.1) | copy-start | bytes 196
  0.7 1.0 %copy-start.12 = (f32[1,16]{1,0:T(1,128)S(1)}, f32[1,16]{1,0:T(1,128)}, u32[]{:S(2)}) copy-start(f32[1,16]{1,0:T(1,128)} %bb_ref.1) | copy-start | bytes 196
  0.7 1.9 %copy-start.5 = (bf16[1,1024,1024]{2,1,0:T(8,128)(2,1)S(1)}, bf16[1,1024,1024]{2,1,0:T(8,128)(2,1)}, u32[]{:S(2)}) copy-start(bf16[1,1024,1024]{2,1,0:T(8,128)(2,1)} %param.16) | copy-start | bytes 6291460
  2.6 5.0 %copy-start.4 = (bf16[1,1024,2048]{2,1,0:T(8,128)(2,1)S(1)}, bf16[1,1024,2048]{2,1,0:T(8,128)(2,1)}, u32[]{:S(2)}) copy-start(bf16[1,1024,2048]{2,1,0:T(8,128)(2,1)} %param.17) | copy-start | bytes 12582916
  8.9 2.9 %copy-start.6 = (bf16[1,1024,1024]{2,1,0:T(8,128)(2,1)S(1)}, bf16[1,1024,1024]{2,1,0:T(8,128)(2,1)}, u32[]{:S(2)}) copy-start(bf16[1,1024,1024]{2,1,0:T(8,128)(2,1)} %param.15) | copy-start | bytes 6291460
  8.9 5.2 %collective-permute-start.1 = (f32[8,192,128]{2,1,0:T(8,128)S(1)}, f32[8,192,128]{2,1,0:T(8,128)S(1)}, u32[]{:S(2)}, u32[]{:S(2)}) collective-permute-start(f32[8,192,128]{2,1,0:T(8,128)S(1)} %get-tuple-element.34.refs_1_), channel_id=1, source_target_pairs={{0,1},{1,0},{2,3},{3,2},{4,5},{5,4},{6,7},{7,6},{8,9},{9,8},{10,11... | collective-permute-start | bytes 2359304 | tf_op jit(solution)/shard_map/ppermute | solution.py:450
  11.7 2.5 %collective-permute-start = (f32[8,192,128]{2,1,0:T(8,128)S(1)}, f32[8,192,128]{2,1,0:T(8,128)S(1)}, u32[]{:S(2)}, u32[]{:S(2)}) collective-permute-start(f32[8,192,128]{2,1,0:T(8,128)S(1)} %get-tuple-element.33.refs_0_), channel_id=1, source_target_pairs={{0,1},{1,0},{2,3},{3,2},{4,5},{5,4},{6,7},{7,6},{8,9},{9,8},{10,11... | collective-permute-start | bytes 2359304 | tf_op jit(solution)/shard_map/ppermute | solution.py:450
  14.1 26.6 %copy-start.1 = (f32[1,16,128,128]{3,2,1,0:T(8,128)S(1)}, f32[1,16,128,128]{3,2,1,0:T(8,128)}, u32[]{:S(2)}) copy-start(f32[1,16,128,128]{3,2,1,0:T(8,128)} %param.25) | copy-start | bytes 3145732
  38.5 3.7 %collective-permute-start.2 = (f32[16,64,128]{2,1,0:T(8,128)S(1)}, f32[16,64,128]{2,1,0:T(8,128)S(1)}, u32[]{:S(2)}, u32[]{:S(2)}) collective-permute-start(f32[16,64,128]{2,1,0:T(8,128)S(1)} %slice.20), channel_id=1, source_target_pairs={{0,1},{1,0},{2,3},{3,2},{4,5},{5,4},{6,7},{7,6},{8,9},{9,8},{10,11... | collective-permute-start | bytes 1572872 | tf_op jit(solution)/shard_map/ppermute | solution.py:463
  41.3 19.3 %copy-start = (bf16[1,2048,1024]{2,1,0:T(8,128)(2,1)S(1)}, bf16[1,2048,1024]{2,1,0:T(8,128)(2,1)}, u32[]{:S(2)}) copy-start(bf16[1,2048,1024]{2,1,0:T(8,128)(2,1)} %param.24) | copy-start | bytes 12582916
  41.3 19.3 %copy-start.3 = (f32[1,128]{1,0:T(1,128)S(1)}, f32[1,128]{1,0:T(1,128)}, u32[]{:S(2)}) copy-start(f32[1,128]{1,0:T(1,128)} %gain_ref.3) | copy-start | bytes 1540
  57.3 3.4 %collective-permute-start.3 = (f32[16,64,128]{2,1,0:T(8,128)S(1)}, f32[16,64,128]{2,1,0:T(8,128)S(1)}, u32[]{:S(2)}, u32[]{:S(2)}) collective-permute-start(f32[16,64,128]{2,1,0:T(8,128)S(1)} %get-tuple-element.45), channel_id=1, source_target_pairs={{0,1},{1,0},{2,3},{3,2},{4,5},{5,4},{6,7},{7,6},{8,9},{9,8},{10,11... | collective-permute-start | bytes 1572872 | tf_op jit(solution)/shard_map/ppermute | solution.py:481
  62.2 6.0 %collective-permute-start.4 = (f32[32,1024]{1,0:T(8,128)S(1)}, f32[32,1024]{1,0:T(8,128)S(1)}, u32[]{:S(2)}, u32[]{:S(2)}) collective-permute-start(f32[32,1024]{1,0:T(8,128)S(1)} %get-tuple-element.48), channel_id=1, source_target_pairs={{0,32},{32,64},{64,96},{96,0},{1,33},{33,65},{65,97},{97,1},{2,34}... | collective-permute-start | bytes 393224 | tf_op jit(solution)/shard_map/ppermute | solution.py:496
  63.4 7.5 %collective-permute-start.5 = (f32[32,1024]{1,0:T(8,128)S(1)}, f32[32,1024]{1,0:T(8,128)S(1)}, u32[]{:S(2)}, u32[]{:S(2)}) collective-permute-start(f32[32,1024]{1,0:T(8,128)S(1)} %get-tuple-element.51), channel_id=1, source_target_pairs={{0,32},{32,64},{64,96},{96,0},{1,33},{33,65},{65,97},{97,1},{2,34}... | collective-permute-start | bytes 393224 | tf_op jit(solution)/shard_map/ppermute | solution.py:496
  64.7 9.1 %collective-permute-start.6 = (f32[32,1024]{1,0:T(8,128)S(1)}, f32[32,1024]{1,0:T(8,128)S(1)}, u32[]{:S(2)}, u32[]{:S(2)}) collective-permute-start(f32[32,1024]{1,0:T(8,128)S(1)} %get-tuple-element.50), channel_id=1, source_target_pairs={{0,32},{32,64},{64,96},{96,0},{1,33},{33,65},{65,97},{97,1},{2,34}... | collective-permute-start | bytes 393224 | tf_op jit(solution)/shard_map/ppermute | solution.py:496
  65.6 11.0 %collective-permute-start.7 = (f32[32,1024]{1,0:T(8,128)S(1)}, f32[32,1024]{1,0:T(8,128)S(1)}, u32[]{:S(2)}, u32[]{:S(2)}) collective-permute-start(f32[32,1024]{1,0:T(8,128)S(1)} %get-tuple-element.49), channel_id=1, source_target_pairs={{0,32},{32,64},{64,96},{96,0},{1,33},{33,65},{65,97},{97,1},{2,34}... | collective-permute-start | bytes 393224 | tf_op jit(solution)/shard_map/ppermute | solution.py:496
